TPU v7x, 512 devices: a whole 4x8x8 slice. The times are simulated.
512 devices in a mesh: psg: 64 (over x, z, core), qry: 8 (over y).
Axes of the slice: x: 4, y: 8, z: 8, core: 2. Of those that a mesh axis runs over, the one named last changes fastest.
Arguments:
- queries: bfloat16 [2048, 4096], P('psg', 'qry'), may hold values from -6 to 6
- grad_out: bfloat16 [2048, 4096], P('psg', 'qry'), may hold values from -6 to 6
- attn_out: bfloat16 [2048, 4096], P('psg', 'qry'), may hold values from -6 to 6
- log_sum: float32 [32, 2048], P('qry', 'psg'), may hold values from 3 to 5
- keys: bfloat16 [32768, 1024], P('psg', 'qry'), may hold values from -6 to 6
- values: bfloat16 [32768, 1024], P('psg', 'qry'), may hold values from -6 to 6
- proj_weight: bfloat16 [4096, 4096], P('psg', 'qry'), may hold values from -0.09375 to 0.09375
- attend: int32 [8, 16], replicated, may hold values from 0 to 63, all different within a row; in each aligned block of 8 rows (0 to 7, 8 to 15, ...) at most 4 rows name the same one
- qlen: int32 [8], replicated, may hold values from 128 to 256, as said below
Outputs:
- grad_query: float32 [2048, 4096], P('psg', 'qry')
- grad_keys: float32 [32768, 1024], P('psg', 'qry')
- grad_values: float32 [32768, 1024], P('psg', 'qry')
- grad_hidden: float32 [2048, 4096], P('psg')
Inputs may be any that keep to these rules, and one draw needn't show every extreme that they name: `attend`: each question names 16 different blocks; each block is named by at least one question and at most 4, and some block by exactly 4. `qlen`: each a multiple of 128; some question has 256 rows.
All inputs are finite; a program needn't handle non-finite values.
Results may differ from a plain program's by a relative error of at most 0.0049.
Values may be sent and summed in bfloat16 or wider, within the bound.
No kernel may reach another device: no remote copies, remote signals or barrier semaphores. Data moves between devices by JAX's collectives and lax.ppermute only.
A program may use at most 64 MiB of HBM per device.

v0:
```python
import jax
import jax.numpy as jnp
from jax import lax
from jax.sharding import PartitionSpec as P

ATTN_WIDTH = 128
GROUP = 4
PADDED_ASK_LEN = 256
TOPB = 16


def row_delta(grad_out, attn_out, head_count):
    products = grad_out.astype(jnp.float32) * attn_out.astype(jnp.float32)
    return jnp.sum(products.reshape(products.shape[0], head_count, ATTN_WIDTH), axis=2).T


def on_device(queries, grad_out, attn_out, log_sum, keys, values, proj_weight, attend, qlen):
    inverse_root_dimension = ATTN_WIDTH ** (-0.5)
    row_count, number_of_columns = queries.shape
    head_count = log_sum.shape[0]
    kv_local = head_count // GROUP
    block_len = keys.shape[0]
    psg_count = lax.axis_size("psg")
    owner_block = lax.axis_index("psg")
    all_queries, all_grads, all_outputs = (
        lax.all_gather(queries, "psg", axis=0, tiled=True),
        lax.all_gather(grad_out, "psg", axis=0, tiled=True),
        lax.all_gather(attn_out, "psg", axis=0, tiled=True),
    )
    all_lse = lax.all_gather(log_sum, "psg", axis=1, tiled=True)
    all_delta = row_delta(all_grads, all_outputs, head_count)
    total_rows = all_queries.shape[0]
    question_total = attend.shape[0]
    attending = jnp.any(attend == owner_block, axis=1).astype(jnp.int32)
    slot_total = jnp.sum(attending)
    slot_rank = jnp.cumsum(attending) - 1
    question_ids = jnp.arange(question_total, dtype=jnp.int32)
    capacity = min(question_total, 2 * question_total * TOPB // psg_count)
    slot_matrix = (attending[None, :] == 1) & (
        slot_rank[None, :] == jnp.arange(capacity, dtype=jnp.int32)[:, None]
    )
    slot_question = jnp.sum(jnp.where(slot_matrix, question_ids[None, :], 0), axis=1)
    passage_lookup_matrix = keys.reshape(block_len, kv_local, ATTN_WIDTH)
    value_block_rows = values.reshape(block_len, kv_local, ATTN_WIDTH)
    sub_len = min(512, block_len)
    sub_count = block_len // sub_len

    def visit(slot_index, totals):
        grad_q, grad_k, grad_v = totals
        question = slot_question[slot_index]
        row_start = question * PADDED_ASK_LEN
        asking_matrix_tile = lax.dynamic_slice_in_dim(
            all_queries, row_start, PADDED_ASK_LEN, 0
        ).reshape(PADDED_ASK_LEN, kv_local, GROUP, ATTN_WIDTH)
        output_gradient_rows = lax.dynamic_slice_in_dim(
            all_grads, row_start, PADDED_ASK_LEN, 0
        ).reshape(PADDED_ASK_LEN, kv_local, GROUP, ATTN_WIDTH)
        lse_rows = lax.dynamic_slice_in_dim(all_lse, row_start, PADDED_ASK_LEN, 1).reshape(
            kv_local, GROUP, PADDED_ASK_LEN
        )
        delta_rows = lax.dynamic_slice_in_dim(all_delta, row_start, PADDED_ASK_LEN, 1).reshape(
            kv_local, GROUP, PADDED_ASK_LEN
        )
        row_valid = (jnp.arange(PADDED_ASK_LEN) < qlen[question]).astype(jnp.float32)

        def sub_visit(sub_index, inner):
            inner_k, inner_v, query_acc = inner
            raw_attention_energies = (
                jnp.einsum(
                    "dlyb,ilb->lydi",
                    asking_matrix_tile,
                    passage_lookup_matrix,
                    preferred_element_type=jnp.float32,
                )
                * inverse_root_dimension
            )
            probs = (
                jnp.exp(raw_attention_energies - lse_rows[..., None])
                * row_valid[None, None, :, None]
            )
            probability_narrow = probs.astype(jnp.bfloat16)
            probability_gradient = jnp.einsum(
                "dlyb,ilb->lydi",
                output_gradient_rows,
                value_block_rows,
                preferred_element_type=jnp.float32,
            )
            energy_derivative_lowprec = (
                probs * (probability_gradient - delta_rows[..., None])
            ).astype(jnp.bfloat16)
            asking_partial_term = jnp.einsum(
                "ilgy,yiu->gilu",
                energy_derivative_lowprec,
                passage_lookup_matrix,
                preferred_element_type=jnp.float32,
            )
            lookup_partial_term = (
                jnp.einsum(
                    "nwde,dnwj->enj",
                    energy_derivative_lowprec,
                    asking_matrix_tile,
                    preferred_element_type=jnp.float32,
                )
                * inverse_root_dimension
            )
            value_contribution = jnp.einsum(
                "nwde,dnwj->enj",
                probability_narrow,
                output_gradient_rows,
                preferred_element_type=jnp.float32,
            )
            old_k = inner_k
            old_v = inner_v
            inner_k = old_k + lookup_partial_term.reshape(sub_len, kv_local * ATTN_WIDTH)
            inner_v = old_v + value_contribution.reshape(sub_len, kv_local * ATTN_WIDTH)
            return (inner_k, inner_v, query_acc + asking_partial_term)

        query_start = jnp.zeros((PADDED_ASK_LEN, kv_local, GROUP, ATTN_WIDTH), jnp.float32)
        grad_k, grad_v, asking_accumulator = lax.fori_loop(
            0, sub_count, sub_visit, (grad_k, grad_v, query_start)
        )
        grad_q = lax.dynamic_update_slice_in_dim(
            grad_q,
            (asking_accumulator * inverse_root_dimension).reshape(
                PADDED_ASK_LEN, number_of_columns
            ),
            row_start,
            0,
        )
        return (grad_q, grad_k, grad_v)

    start_totals = (
        jnp.zeros((total_rows, number_of_columns), jnp.float32),
        jnp.zeros((block_len, kv_local * ATTN_WIDTH), jnp.float32),
        jnp.zeros((block_len, kv_local * ATTN_WIDTH), jnp.float32),
    )
    query_terms, grad_keys, grad_values = lax.fori_loop(0, slot_total, visit, start_totals)
    grad_query = lax.psum_scatter(query_terms, "psg", scatter_dimension=0, tiled=True)
    query_low = grad_query.astype(jnp.bfloat16)
    hidden_terms = lax.dot_general(
        query_low,
        lax.all_gather(proj_weight, "psg", axis=0, tiled=True),
        (((1,), (1,)), ((), ())),
        preferred_element_type=jnp.float32,
    )
    grad_hidden = lax.psum(hidden_terms, "qry")
    return (grad_query, grad_keys, grad_values, grad_hidden)


def solution(mesh):
    in_specs = (
        P("psg", "qry"),
        P("psg", "qry"),
        P("psg", "qry"),
        P("qry", "psg"),
        P("psg", "qry"),
        P("psg", "qry"),
        P("psg", "qry"),
        P(),
        P(),
    )
    out_specs = (P("psg", "qry"), P("psg", "qry"), P("psg", "qry"), P("psg", None))
    return jax.shard_map(
        on_device, mesh=mesh, in_specs=in_specs, out_specs=out_specs, check_vma=False
    )
```

profile of v0, /device:TPU:6, one launch (start us, length us, event | category | flops | bytes accessed | tf_op | source)
XLA Modules:
  0.0 597.4 jit_solution(7665506807522888726)
XLA Ops:
  7.2 0.0 all-gather.8.cloned.1.call-start
  7.2 0.7 all-gather.8.cloned.1.call-update
  7.9 0.0 all-gather.10.cloned.1.call-start
  7.9 0.7 all-gather.10.cloned.1.call-update
  8.6 0.0 all-gather.6.cloned.1.call-start
  8.7 0.7 all-gather.6.cloned.1.call-update
  9.4 0.0 all-gather.12.cloned.1.call-start
  9.4 0.5 all-gather.12.cloned.1.call-update
  10.0 0.0 reduce-scatter.2.cloned.1.call-start
  10.0 0.8 compare_reduce_fusion
  10.8 0.6 convert_reduce_fusion
  11.4 0.2 reduce-window.8
  11.6 55.4 %all-gather = f32[64,32,4]{1,2,0:T(4,128)S(1)} all-gather(f32[1,32,4]{1,2,0:T(4,128)} %bitcast.141), channel_id=1, replica_groups=mesh['psg'=64,'qry'=8] {'psg'}, dimensions={0}, use_global_device_ids=true | all-gather | bytes 33280 | tf_op jit(solution)/shard_map/all_gather | solution.py:30
  67.0 0.1 reshape.133
  67.1 1.0 copy.63
  68.1 0.1 select_reduce_fusion
  68.3 30.3 %all-gather.8.cloned.1.call-done = bf16[2048,512]{1,0:T(8,128)(2,1)} async-done(((bf16[32,512]{1,0:T(8,128)(2,1)}), bf16[2048,512]{1,0:T(8,128)(2,1)}) %all-gather.8.cloned.1.call-update) | async-done | bytes 2097168 | tf_op jit(solution)/shard_map/all_gather | solution.py:27
  98.5 84.0 %all-gather.10.cloned.1.call-done = bf16[2048,512]{1,0:T(8,128)(2,1)} async-done(((bf16[32,512]{1,0:T(8,128)(2,1)}), bf16[2048,512]{1,0:T(8,128)(2,1)}) %all-gather.10.cloned.1.call-update) | async-done | bytes 2097168 | tf_op jit(solution)/shard_map/all_gather | solution.py:28
  182.5 4.8 convert_multiply_fusion
  187.4 5.3 reshape.130
  192.7 5.0 reduce_sum.29
  197.7 0.3 copy.68
  198.0 68.5 %all-gather.6.cloned.1.call-done = bf16[2048,512]{1,0:T(8,128)(2,1)} async-done(((bf16[32,512]{1,0:T(8,128)(2,1)}), bf16[2048,512]{1,0:T(8,128)(2,1)}) %all-gather.6.cloned.1.call-update) | async-done | bytes 2097168 | tf_op jit(solution)/shard_map/all_gather | solution.py:26
  266.6 2.5 broadcast_in_dim.21.clone
  269.1 0.7 broadcast.57
  269.8 0.7 broadcast.57.clone
  270.5 37.6 %while.16 = (s32[]{:T(128)}, f32[2048,512]{1,0:T(8,128)}, f32[512,128]{0,1:T(8,128)}, f32[512,128]{1,0:T(8,128)}, s32[]{:T(128)}, /*index=5*/s32[4]{0:T(128)S(1)...) while((s32[]{:T(128)}, f32[2048,512]{1,0:T(8,128)}, ...), condition=%wide.region_6.7_spmd, body=%wide.region_5.6_spmd.sunk | while | flops 675086848 | bytes 18246100 | solution.py:137
  271.1 0.0 copy-start.2
  271.1 0.6 dynamic_slice.28
  272.4 1.1 constant_dynamic-slice_fusion.6
  273.4 0.1 copy.85
  275.5 0.6 dynamic_slice.29
  276.1 0.6 compare_convert_fusion.2
  276.8 0.6 fusion.48
  277.3 0.9 copy.86
  278.2 1.5 fusion.49
  279.7 1.3 convolution_multiply_fusion.2
  281.0 2.1 copy.87
  283.0 1.9 constant_dynamic-update-slice_fusion.2
  284.9 2.0 fusion.50
  286.9 2.1 fusion.51
  289.6 0.0 copy-start.2
  289.6 0.6 dynamic_slice.28
  290.9 1.1 constant_dynamic-slice_fusion.6
  292.0 0.1 copy.85
  294.1 0.6 dynamic_slice.29
  294.6 0.6 compare_convert_fusion.2
  295.3 0.6 fusion.48
  295.9 0.9 copy.86
  296.7 1.5 fusion.49
  298.2 1.3 convolution_multiply_fusion.2
  299.5 2.1 copy.87
  301.6 1.9 constant_dynamic-update-slice_fusion.2
  303.5 2.0 fusion.50
  305.5 2.1 fusion.51
  308.2 0.0 reduce-scatter.2.cloned.1.call-update
  308.2 0.0 all-reduce.2.cloned.1.call-start
  308.2 43.7 %all-gather.12.cloned.1.call-done = bf16[4096,512]{1,0:T(8,128)(2,1)} async-done(((bf16[64,512]{1,0:T(8,128)(2,1)}), bf16[4096,512]{1,0:T(8,128)(2,1)}) %all-gather.12.cloned.1.call-update) | async-done | bytes 4194320 | tf_op jit(solution)/shard_map/all_gather | solution.py:142
  352.0 154.9 %reduce-scatter.2.cloned.1.call-done = f32[32,512]{1,0:T(8,128)} async-done(((f32[2048,512]{1,0:T(8,128)}), f32[32,512]{1,0:T(8,128)}) %reduce-scatter.2.cloned.1.call-update) | async-done | bytes 65552 | tf_op jit(solution)/shard_map/reduce_scatter | solution.py:138
  506.9 4.3 fusion.14
  511.2 0.0 all-reduce.2.cloned.1.call-update
  511.3 0.8 copy.70
  512.1 76.6 %all-reduce.2.cloned.1.call-done = f32[32,4096]{1,0:T(8,128)} async-done(((f32[32,4096]{1,0:T(8,128)}), f32[32,4096]{1,0:T(8,128)}) %all-reduce.2.cloned.1.call-update) | async-done | bytes 524304 | tf_op jit(solution)/shard_map/psum | solution.py:146
  588.7 1.9 copy.102
  (27 shorter events, 0.1 us)
Async XLA Ops:
  7.2 91.4 %all-gather.8.cloned.1.call-start = ((), (), s32[]{:S(2)}) async-start(), calls=%async_computation.2 | async-start | bytes 2129920 | tf_op jit(solution)/shard_map/all_gather | solution.py:27
  7.9 174.6 %all-gather.10.cloned.1.call-start = ((), (), s32[]{:S(2)}) async-start(), calls=%async_computation.3 | async-start | bytes 2129920 | tf_op jit(solution)/shard_map/all_gather | solution.py:28
  8.6 257.9 %all-gather.6.cloned.1.call-start = ((), (), s32[]{:S(2)}) async-start(), calls=%async_computation.1 | async-start | bytes 2129920 | tf_op jit(solution)/shard_map/all_gather | solution.py:26
  9.4 342.6 %all-gather.12.cloned.1.call-start = ((), (), s32[]{:S(2)}) async-start(), calls=%async_computation.5 | async-start | bytes 4259840 | tf_op jit(solution)/shard_map/all_gather | solution.py:142
  10.0 496.9 %reduce-scatter.2.cloned.1.call-start = ((), (), s32[]{:S(2)}) async-start(), calls=%async_computation.4 | async-start | bytes 4259840 | tf_op jit(solution)/shard_map/reduce_scatter | solution.py:138
  266.6 4.0 copy-start.6
  271.1 7.1 %copy-start.2 = (f32[4,2048]{1,0:T(4,128)}, f32[4,2048]{1,0:T(4,128)S(1)}, u32[]{:S(2)}) copy-start(f32[4,2048]{1,0:T(4,128)S(1)} %get-tuple-element.388) | copy-start | bytes 98308 | tf_op jit(solution)/shard_map/while
  271.1 7.1 %copy-start.4 = (f32[4,2048]{1,0:T(4,128)}, f32[4,2048]{1,0:T(4,128)S(1)}, u32[]{:S(2)}) copy-start(f32[4,2048]{1,0:T(4,128)S(1)} %get-tuple-element.392) | copy-start | bytes 98308 | tf_op jit(solution)/shard_map/while
  283.0 3.9 copy-start
  286.9 2.1 copy-start.3
  286.9 2.1 copy-start.5
  289.6 7.1 %copy-start.2 = (f32[4,2048]{1,0:T(4,128)}, f32[4,2048]{1,0:T(4,128)S(1)}, u32[]{:S(2)}) copy-start(f32[4,2048]{1,0:T(4,128)S(1)} %get-tuple-element.388) | copy-start | bytes 98308 | tf_op jit(solution)/shard_map/while
  289.6 7.1 %copy-start.4 = (f32[4,2048]{1,0:T(4,128)}, f32[4,2048]{1,0:T(4,128)S(1)}, u32[]{:S(2)}) copy-start(f32[4,2048]{1,0:T(4,128)S(1)} %get-tuple-element.392) | copy-start | bytes 98308 | tf_op jit(solution)/shard_map/while
  301.6 3.9 copy-start
  305.4 2.1 copy-start.3
  305.4 2.1 copy-start.5
  308.2 203.1 %copy-start.1 = (f32[512,128]{0,1:T(8,128)S(1)}, f32[512,128]{0,1:T(8,128)}, u32[]{:S(2)}) copy-start(f32[512,128]{0,1:T(8,128)} %get-tuple-element.219) | copy-start | bytes 786436
  308.2 280.5 %all-reduce.2.cloned.1.call-start = ((), (), s32[]{:S(2)}) async-start(), calls=%async_computation.6 | async-start | bytes 1048576 | tf_op jit(solution)/shard_map/psum | solution.py:146
Sparse Core Ops, SparseCore 0:
  11.4 87.1 all-gather.7
  101.9 80.6 all-gather.9
  185.9 80.6 all-gather.5
  269.8 82.1 all-gather.11
  357.1 149.7 reduce-scatter.1
  511.4 77.2 all-reduce.1
where the time goes:
time: 599 us; the launch traced here: 597 us
  waiting for transfers between devices  461 us (77%)
  blocking collectives  55.4 us (9%)
  local copies, waits for them, and re-layouts  28 us (5%)
  matrix products  19.1 us (3%)
  between operations  14.2 us (2%)
  other arithmetic  12.9 us (2%)
  loops' own time  7 us (1%)
    reduce_scatter x1, waiting for transfers between devices, on_device(): lax.psum_scatter(query_terms, 'psg', scatter_dimension=0, tiled=True)  155 us
    all_gather x1, waiting for transfers between devices, on_device(): lax.all_gather(attn_out, 'psg', axis=0, tiled=True)  84 us
    psum x1, waiting for transfers between devices, on_device(): grad_hidden = lax.psum(hidden_terms, 'qry')  76.6 us
    all_gather x1, waiting for transfers between devices, on_device(): lax.all_gather(queries, 'psg', axis=0, tiled=True)  68.5 us
    all_gather x1, blocking collectives, on_device(): all_lse = lax.all_gather(log_sum, 'psg', axis=1, tiled=True)  55.4 us
    all_gather x1, waiting for transfers between devices, on_device(): lax.all_gather(proj_weight, 'psg', axis=0, tiled=True)  43.7 us
    all_gather x1, waiting for transfers between devices, on_device(): lax.all_gather(grad_out, 'psg', axis=0, tiled=True)  30.3 us
  transfers between devices with their start and end apart: 6, of which 6 were waited for; matrix products, arithmetic and copies ran while one was open for 9% of the time, Pallas kernels for 0%

commit v1 on v0

v1 whole, which is shorter than its diff:
```python
import functools

import jax
import jax.numpy as jnp
from jax import lax
from jax.experimental import pallas as pl
from jax.experimental.pallas import tpu as pltpu
from jax.sharding import PartitionSpec as P

WIDTH = 128
GROUP = 4
ASK_LEN = 256
XS, ZS, CS = 4, 8, 2
LOG2E = 1.4426950408889634
FAR = 1.0e6


def index_of(x, z, c):
    return (x * ZS + z) * CS + c


Z_GROUPS = [[index_of(x, z, c) for z in range(ZS)] for x in range(XS) for c in range(CS)]
X_GROUPS = [[index_of(x, z, c) for x in range(XS)] for z in range(ZS) for c in range(CS)]
CORE_SWAP = [(i, i ^ 1) for i in range(XS * ZS * CS)]


def pieces(value):
    high = lax.reduce_precision(value, 8, 7)
    rest = value - high
    middle = lax.reduce_precision(rest, 8, 7)
    low = rest - middle
    return [part.astype(jnp.bfloat16) for part in (high, middle, low)]


def pack_rows(queries, grad_out, attn_out, log_sum, qlen, owner):
    rows = queries.shape[0]
    heads = log_sum.shape[0]
    products = grad_out.astype(jnp.float32) * attn_out.astype(jnp.float32)
    delta = jnp.sum(products.reshape(rows, heads, WIDTH), axis=2)
    first = owner * rows
    question = first // ASK_LEN
    place = first - question * ASK_LEN + jnp.arange(rows)
    live = place < qlen[question]
    shift = jnp.where(live[:, None], log_sum.T * (WIDTH**0.5), FAR)
    columns = pieces(shift) + pieces(delta)
    side = jnp.concatenate(columns, axis=1)
    side = jnp.pad(side, ((0, 0), (0, WIDTH - side.shape[1])))
    return jnp.concatenate([queries, grad_out, side], axis=1)


def visit_kernel(heads, span, attending, own_ref, other_ref, key_ref, value_ref, own_q, other_q, out_k, out_v):
    question = pl.program_id(0)
    scale = WIDTH**-0.5
    half = ASK_LEN // 2

    @pl.when(question == 0)
    def _():
        out_k[...] = jnp.zeros_like(out_k)
        out_v[...] = jnp.zeros_like(out_v)

    @pl.when(attending[question] == 0)
    def _():
        own_q[...] = jnp.zeros_like(own_q)
        other_q[...] = jnp.zeros_like(other_q)

    @pl.when(attending[question] != 0)
    def _():
        key = key_ref[...]
        value = value_ref[...]
        key_t = key.astype(jnp.float32).T.astype(jnp.bfloat16)
        columns = lax.broadcasted_iota(jnp.int32, (span, WIDTH), 1)
        grad_k = jnp.zeros((span, WIDTH), jnp.float32)
        grad_v = jnp.zeros((span, WIDTH), jnp.float32)

        def take(start):
            both = [
                ref[0, :, :, start : start + WIDTH].reshape(half, WIDTH) for ref in (own_ref, other_ref)
            ]
            return jnp.concatenate(both, axis=0)

        side = take(2 * heads * WIDTH)
        for head in range(heads):
            query = take(head * WIDTH)
            cotangent = take((heads + head) * WIDTH)
            for_shift = (columns < 3 * heads) & (columns % heads == head)
            for_delta = (columns >= 3 * heads) & (columns < 6 * heads) & (columns % heads == head)
            minus_s = jnp.where(for_shift, -1.0, 0.0).astype(jnp.bfloat16)
            minus_d = jnp.where(for_delta, -1.0, 0.0).astype(jnp.bfloat16)
            energy = lax.dot_general(
                jnp.concatenate([key, minus_s], axis=1),
                jnp.concatenate([query, side], axis=1),
                (((1,), (1,)), ((), ())),
                preferred_element_type=jnp.float32,
            )
            prob = jnp.exp2(energy * (scale * LOG2E))
            change = lax.dot_general(
                jnp.concatenate([value, minus_d], axis=1),
                jnp.concatenate([cotangent, side], axis=1),
                (((1,), (1,)), ((), ())),
                preferred_element_type=jnp.float32,
            )
            low_score = (prob * change).astype(jnp.bfloat16)
            low_prob = prob.astype(jnp.bfloat16)
            grad_k = grad_k + jnp.dot(low_score, query, preferred_element_type=jnp.float32)
            grad_v = grad_v + jnp.dot(low_prob, cotangent, preferred_element_type=jnp.float32)
            term = jnp.dot(key_t, low_score, preferred_element_type=jnp.float32).T * scale
            term = term.astype(jnp.bfloat16)
            place = slice(head * WIDTH, (head + 1) * WIDTH)
            own_q[0, :, :, place] = term[:half].reshape(own_q.shape[1], own_q.shape[2], WIDTH)
            other_q[0, :, :, place] = term[half:].reshape(own_q.shape[1], own_q.shape[2], WIDTH)
        out_k[...] += grad_k * scale
        out_v[...] += grad_v


def visits(attending, own, other, keys, values, heads):
    questions, chunks, rows, packed = own.shape
    span = keys.shape[0]
    columns = heads * WIDTH
    block = pl.BlockSpec((1, chunks, rows, packed), lambda n, a: (n, 0, 0, 0))
    whole = pl.BlockSpec((span, WIDTH), lambda n, a: (0, 0))
    term = pl.BlockSpec((1, chunks, rows, columns), lambda n, a: (n, 0, 0, 0))
    return pl.pallas_call(
        functools.partial(visit_kernel, heads, span),
        grid_spec=pltpu.PrefetchScalarGridSpec(
            num_scalar_prefetch=1,
            grid=(questions,),
            in_specs=[block, block, whole, whole],
            out_specs=[term, term, whole, whole],
        ),
        out_shape=[
            jax.ShapeDtypeStruct((questions, chunks, rows, columns), jnp.bfloat16),
            jax.ShapeDtypeStruct((questions, chunks, rows, columns), jnp.bfloat16),
            jax.ShapeDtypeStruct((span, WIDTH), jnp.float32),
            jax.ShapeDtypeStruct((span, WIDTH), jnp.float32),
        ],
        compiler_params=pltpu.CompilerParams(vmem_limit_bytes=40 * 2**20),
        cost_estimate=pl.CostEstimate(flops=6 * 10**9, bytes_accessed=10**7, transcendentals=2 * 10**6),
    )(attending, own, other, keys, values)


def hidden_kernel(query_ref, weight_ref, out_ref):
    out_ref[0] = lax.dot_general(
        query_ref[...], weight_ref[...], (((1,), (1,)), ((), ())), preferred_element_type=jnp.float32
    ).astype(out_ref.dtype)


def hidden_parts(query_low, weight, parts):
    rows, columns = query_low.shape
    wide = weight.shape[0] // parts
    return pl.pallas_call(
        hidden_kernel,
        grid=(parts,),
        in_specs=[
            pl.BlockSpec((rows, columns), lambda n: (0, 0)),
            pl.BlockSpec((wide, columns), lambda n: (n, 0)),
        ],
        out_specs=pl.BlockSpec((1, rows, wide), lambda n: (n, 0, 0)),
        out_shape=jax.ShapeDtypeStruct((parts, rows, wide), jnp.bfloat16),
        cost_estimate=pl.CostEstimate(flops=2 * rows * columns * weight.shape[0], bytes_accessed=5 * 10**6, transcendentals=0),
    )(query_low, weight)


def on_device(queries, grad_out, attn_out, log_sum, keys, values, proj_weight, attend, qlen):
    heads = log_sum.shape[0]
    rows, columns = queries.shape
    owner = lax.axis_index("psg")
    weight = lax.all_gather(proj_weight, "psg", axis=0, tiled=True)

    packed = pack_rows(queries, grad_out, attn_out, log_sum, qlen, owner)
    gathered = lax.all_gather(packed, "psg", axis=0, axis_index_groups=Z_GROUPS)
    gathered = lax.all_gather(gathered, "psg", axis=0, axis_index_groups=X_GROUPS)
    question_total = attend.shape[0]
    own = gathered.reshape(question_total, -1, rows, packed.shape[1])
    other = lax.ppermute(own, "psg", CORE_SWAP)

    attending = jnp.any(attend == owner, axis=1).astype(jnp.int32)
    own_q, other_q, grad_keys, grad_values = visits(attending, own, other, keys, values, heads)

    swapped = lax.ppermute(other_q, "psg", CORE_SWAP)
    pair = (own_q.astype(jnp.float32) + swapped.astype(jnp.float32)).astype(jnp.bfloat16)
    pair = pair.reshape(XS, ZS, rows, columns)
    pair = lax.all_to_all(pair, "psg", 0, 0, tiled=True, axis_index_groups=X_GROUPS)
    line = jnp.sum(pair.astype(jnp.float32), axis=0).astype(jnp.bfloat16)
    line = lax.all_to_all(line, "psg", 0, 0, tiled=True, axis_index_groups=Z_GROUPS)
    grad_query = jnp.sum(line.astype(jnp.float32), axis=0)
    query_low = grad_query.astype(jnp.bfloat16)

    parts = lax.axis_size("qry")
    terms = hidden_parts(query_low, weight, parts)
    terms = lax.all_to_all(terms, "qry", 0, 0, tiled=True)
    hidden = jnp.sum(terms.astype(jnp.float32), axis=0)
    grad_hidden = lax.all_gather(hidden, "qry", axis=1, tiled=True)
    return (grad_query, grad_keys, grad_values, grad_hidden)


def solution(mesh):
    in_specs = (
        P("psg", "qry"),
        P("psg", "qry"),
        P("psg", "qry"),
        P("qry", "psg"),
        P("psg", "qry"),
        P("psg", "qry"),
        P("psg", "qry"),
        P(),
        P(),
    )
    out_specs = (P("psg", "qry"), P("psg", "qry"), P("psg", "qry"), P("psg", None))
    return jax.shard_map(
        on_device, mesh=mesh, in_specs=in_specs, out_specs=out_specs, check_vma=False
    )
```

time: 599 us -> 229 us (0.38)
  waiting for transfers between devices: 461 us -> 69.6 us
  blocking collectives: 55.4 us -> 116 us
  local copies, waits for them, and re-layouts: 28 us -> 5.79 us
  matrix products: 19.1 us -> 0 us
  Pallas kernels: 0 us -> 13.6 us
  other arithmetic: 12.9 us -> 5.1 us
  loops' own time: 7 us -> 0 us
    all_gather x4 -> x2, waiting for transfers between devices: 227 us -> 62.5 us  [the longest x1 33.9 us: on_device(): lax.all_gather(gathered, 'psg', axis=0, axis_index_groups=X_GROUPS)]
    reduce_scatter x1 -> x0, waiting for transfers between devices: 155 us -> none  [on_device(): lax.psum_scatter(query_terms, 'psg', scatter_dimension=0, tiled=True)]
    psum x1 -> x0, waiting for transfers between devices: 76.6 us -> none  [on_device(): grad_hidden = lax.psum(hidden_terms, 'qry')]
    all_to_all x0 -> x3, blocking collectives: none -> 57.1 us  [the longest x1 19.5 us: on_device(): lax.all_to_all(pair, 'psg', 0, 0, tiled=True, axis_index_groups=X_GROUPS)]
    dot_general x11 -> x0, matrix products: 19.1 us -> none  [the longest x1 4.35 us: on_device(): lax.dot_general(query_low, lax.all_gather(proj_weight, 'psg', axis=0, til...]
    pallas_call x0 -> x2, Pallas kernels: none -> 13.6 us  [the longest x1 6.96 us: visits(): pl.pallas_call(functools.partial(visit_kernel, heads, span), grid_spec=pl...]
    dynamic_update_slice x4 -> x0, local copies, waits for them, and re-layouts: 7.98 us -> none  [visit(): lax.dynamic_update_slice_in_dim(grad_q, (asking_accumulator * inverse_roo...]
    another operation x1 -> x0, loops' own time: 7 us -> none  [on_device(): lax.fori_loop(0, slot_total, visit, start_totals)]
  transfers between devices with their start and end apart: 6 -> 4, of which waited for: 6 -> 4; matrix products, arithmetic and copies ran while one was open for 9% -> 1% of each run, Pallas kernels for 0% -> 3%
where the time goes in v1:
time: 229 us
  blocking collectives  116 us (51%)
  waiting for transfers between devices  69.6 us (30%)
  between operations  14.1 us (6%)
  Pallas kernels  13.6 us (6%)
  local copies, waits for them, and re-layouts  5.79 us (3%)
  other arithmetic  5.1 us (2%)
  starting transfers between devices  4.03 us (2%)
    all_gather x1, blocking collectives, on_device(): gathered = lax.all_gather(packed, 'psg', axis=0, axis_index_groups=Z_GROUPS)  34.1 us
    all_gather x1, waiting for transfers between devices, on_device(): lax.all_gather(gathered, 'psg', axis=0, axis_index_groups=X_GROUPS)  33.9 us
    all_gather x1, waiting for transfers between devices, on_device(): weight = lax.all_gather(proj_weight, 'psg', axis=0, tiled=True)  28.6 us
    all_gather x1, blocking collectives, on_device(): grad_hidden = lax.all_gather(hidden, 'qry', axis=1, tiled=True)  25.4 us
    all_to_all x1, blocking collectives, on_device(): lax.all_to_all(pair, 'psg', 0, 0, tiled=True, axis_index_groups=X_GROUPS)  19.5 us
    all_to_all x1, blocking collectives, on_device(): terms = lax.all_to_all(terms, 'qry', 0, 0, tiled=True)  19 us
    all_to_all x1, blocking collectives, on_device(): lax.all_to_all(line, 'psg', 0, 0, tiled=True, axis_index_groups=Z_GROUPS)  18.6 us
    pallas_call x1, Pallas kernels, visits(): pl.pallas_call(functools.partial(visit_kernel, heads, span), grid_spec=pl...  6.96 us
  transfers between devices with their start and end apart: 4, of which 4 were waited for; matrix products, arithmetic and copies ran while one was open for 1% of the time, Pallas kernels for 3%

profile of v1, /device:TPU:6, one launch (start us, length us, event | category | flops | bytes accessed | tf_op | source)
XLA Modules:
  0.0 228.7 jit_solution(11031156656566334004)
XLA Ops:
  7.2 0.0 all-gather.7.cloned.1.call-start
  7.2 0.8 convert_multiply_fusion
  8.1 0.1 reduce_sum.39
  8.2 0.1 copy.22
  8.2 1.2 dynamic_slice.3
  9.5 0.7 add_compare_fusion
  10.1 0.7 fusion.2
  10.8 0.1 concatenate.6
  10.9 0.1 copy.25
  11.0 0.8 fusion.1
  11.8 34.1 %all-gather = bf16[256,1152]{1,0:T(8,128)(2,1)} all-gather(bf16[32,1152]{1,0:T(8,128)(2,1)S(1)} %fusion.1), channel_id=2, replica_groups={{0,16,32,48,64,80,96,112},{8,24,40,56,72,88,104,120},{128,144,160,176,1..., dimensions={0}, use_global_device_ids=true | all-gather | bytes 663552 | tf_op jit(solution)/shard_map/all_gather | solution.py:170
  45.9 0.0 all-gather.7.cloned.1.call-update
  45.9 0.0 all-gather.5.cloned.1.call-start
  45.9 0.7 all-gather.5.cloned.1.call-update
  46.6 33.9 %all-gather.7.cloned.1.call-done = bf16[32,32,1152]{2,1,0:T(8,128)(2,1)} async-done(((bf16[8,32,1152]{2,1,0:T(8,128)(2,1)}), bf16[32,32,1152]{2,1,0:T(8,128)(2,1)}) %all-gather.7.cloned.1.call-update) | async-done | bytes 2359312 | tf_op jit(solution)/shard_map/all_gather | solution.py:171
  80.5 1.9 collective-permute-start
  82.4 0.8 compare_reduce_fusion
  83.2 3.9 %collective-permute-done.other_ref = bf16[8,4,32,1152]{3,2,1,0:T(8,128)(2,1)S(1)} collective-permute-done((bf16[8,4,32,1152]{3,2,1,0:T(8,128)(2,1)}, bf16[8,4,32,1152]{3,2,1,0:T(8,128)(2,1)S(1)}, u32[]{:S(2)}, u32[]{:S(2)}) %collective-permute-start) | collective-permute-done | bytes 2359328 | tf_op jit(solution)/shard_map/ppermute | solution.py:174
  87.1 0.0 copy-start
  87.1 1.7 copy-done
  88.8 0.0 copy-start.1
  88.8 0.9 copy-done.1
  89.7 0.0 copy-start.2
  89.7 0.9 copy-done.2
  90.6 7.0 %shard_map.120 = (bf16[8,4,32,512]{3,2,1,0:T(8,128)(2,1)S(1)}, bf16[8,4,32,512]{3,2,1,0:T(8,128)(2,1)S(1)}, f32[512,128]{1,0:T(8,128)}, f32[512,128]{1,0:T(8,128)}) custom-call(s32[8]{0:T(128)S(1)} %convert_element_type.49.attending, bf16[8,4,32,1152]{3,2,1,0:T(8,128)(2,1)S(1)} %bitcast.12, bf16[8,4,32,1152]{3,2,1,0:T(8,128)(2,1)S(1)} %collective-permute-done.other_ref, ...), custom_call_target="tpu_custom_call" | custom-call | flops 6000000000 | bytes 10000000 | tf_op jit(solution)/shard_map/pallas_call | solution.py:122
  97.6 2.0 collective-permute-start.1
  99.6 2.5 %collective-permute-done.1 = bf16[8,4,32,512]{3,2,1,0:T(8,128)(2,1)S(1)} collective-permute-done((bf16[8,4,32,512]{3,2,1,0:T(8,128)(2,1)S(1)}, bf16[8,4,32,512]{3,2,1,0:T(8,128)(2,1)S(1)}, u32[]{:S(2)}, u32[]{:S(2)}) %collective-permute-start.1) | collective-permute-done | bytes 1048608 | tf_op jit(solution)/shard_map/ppermute | solution.py:179
  102.1 0.4 add_convert_fusion
  102.5 19.5 %all_to_all.15 = bf16[4,8,32,512]{3,2,1,0:T(8,128)(2,1)S(1)} all-to-all(bf16[4,8,32,512]{3,2,1,0:T(8,128)(2,1)S(1)} %bitcast.13), channel_id=1, replica_groups={{0,128,256,384},{8,136,264,392},{16,144,272,400},{24,152,280,408},{32,1..., dimensions={0} | all-to-all | bytes 2097152 | tf_op jit(solution)/shard_map/all_to_all | solution.py:182
  122.0 0.2 reduce_sum.40
  122.2 18.6 %all_to_all.16 = bf16[8,32,512]{2,1,0:T(8,128)(2,1)S(1)} all-to-all(bf16[8,32,512]{2,1,0:T(8,128)(2,1)S(1)} %reduce_sum.40), channel_id=1, replica_groups={{0,16,32,48,64,80,96,112},{8,24,40,56,72,88,104,120},{128,144,160,176,1..., dimensions={0} | all-to-all | bytes 524288 | tf_op jit(solution)/shard_map/all_to_all | solution.py:184
  140.8 0.0 copy-start.3
  140.8 0.6 convert_element_type.62.query_ref
  141.4 28.6 %all-gather.5.cloned.1.call-done.weight_ref = bf16[4096,512]{1,0:T(8,128)(2,1)} async-done(((bf16[64,512]{1,0:T(8,128)(2,1)}), bf16[4096,512]{1,0:T(8,128)(2,1)}) %all-gather.5.cloned.1.call-update) | async-done | bytes 4194320 | tf_op jit(solution)/shard_map/all_gather | solution.py:167
  170.0 6.6 %shard_map.121 = bf16[8,32,512]{2,1,0:T(8,128)(2,1)} custom-call(bf16[32,512]{1,0:T(8,128)(2,1)} %convert_element_type.62.query_ref, bf16[4096,512]{1,0:T(8,128)(2,1)} %all-gather.5.cloned.1.call-done.weight_ref), custom_call_target="tpu_custom_call" | custom-call | flops 134217728 | bytes 5000000 | tf_op jit(solution)/shard_map/pallas_call | solution.py:150
  176.6 19.0 %all_to_all.17 = bf16[8,32,512]{2,1,0:T(8,128)(2,1)S(1)} all-to-all(bf16[8,32,512]{2,1,0:T(8,128)(2,1)} %shard_map.121), channel_id=1, replica_groups=mesh['psg'=64,'qry'=8] {'qry'}, dimensions={0} | all-to-all | bytes 524288 | tf_op jit(solution)/shard_map/all_to_all | solution.py:190
  195.7 0.0 copy-done.3
  195.7 25.4 %all_gather.23 = f32[32,4096]{1,0:T(8,128)S(1)} all-gather(f32[32,512]{1,0:T(8,128)S(1)} %convert_reduce_fusion), channel_id=1, replica_groups=mesh['psg'=64,'qry'=8] {'qry'}, dimensions={1}, use_global_device_ids=true | all-gather | bytes 589824 | tf_op jit(solution)/shard_map/all_gather | solution.py:192
  221.1 0.8 copy.27
  (4 shorter events, 0.1 us)
Async XLA Ops:
  7.2 73.4 %all-gather.7.cloned.1.call-start = ((), (), s32[]{:S(2)}) async-start(), calls=%async_computation.4 | async-start | bytes 2949120 | tf_op jit(solution)/shard_map/all_gather | solution.py:171
  45.9 124.2 %all-gather.5.cloned.1.call-start = ((), (), s32[]{:S(2)}) async-start(), calls=%async_computation.3 | async-start | bytes 4259840 | tf_op jit(solution)/shard_map/all_gather | solution.py:167
  80.5 6.6 %collective-permute-start = (bf16[8,4,32,1152]{3,2,1,0:T(8,128)(2,1)}, bf16[8,4,32,1152]{3,2,1,0:T(8,128)(2,1)S(1)}, u32[]{:S(2)}, u32[]{:S(2)}) collective-permute-start(bf16[8,4,32,1152]{3,2,1,0:T(8,128)(2,1)} %bitcast.11), channel_id=1, source_target_pairs={{0,8},{8,0},{16,24},{24,16},{32,40},{40,32},{48,56},{56,48},{64,72... | collective-permute-start | bytes 7077896 | tf_op jit(solution)/shard_map/ppermute | solution.py:174
  87.1 1.7 copy-start
  88.8 0.9 copy-start.1
  89.7 0.9 copy-start.2
  97.6 4.5 %collective-permute-start.1 = (bf16[8,4,32,512]{3,2,1,0:T(8,128)(2,1)S(1)}, bf16[8,4,32,512]{3,2,1,0:T(8,128)(2,1)S(1)}, u32[]{:S(2)}, u32[]{:S(2)}) collective-permute-start(bf16[8,4,32,512]{3,2,1,0:T(8,128)(2,1)S(1)} %get-tuple-element.9), channel_id=1, source_target_pairs={{0,8},{8,0},{16,24},{24,16},{32,40},{40,32},{48,56},{56,48},{64,72... | collective-permute-start | bytes 3145736 | tf_op jit(solution)/shard_map/ppermute | solution.py:179
  140.8 54.9 %copy-start.3 = (f32[32,512]{1,0:T(8,128)}, f32[32,512]{1,0:T(8,128)S(1)}, u32[]{:S(2)}) copy-start(f32[32,512]{1,0:T(8,128)S(1)} %convert_reduce_fusion.1) | copy-start | bytes 196612
Sparse Core Ops, SparseCore 0:
  46.0 34.4 all-gather.6
  83.9 86.1 all-gather.4

commit v2 on v1

v2 whole, which is shorter than its diff:
```python
import functools

import jax
import jax.numpy as jnp
from jax import lax
from jax.experimental import pallas as pl
from jax.experimental.pallas import tpu as pltpu
from jax.sharding import PartitionSpec as P

WIDTH = 128
GROUP = 4
ASK_LEN = 256
XS, ZS, CS = 4, 8, 2
LOG2E = 1.4426950408889634
FAR = 1.0e6
WIDE = 60 * 2**20


def index_of(x, z, c):
    return (x * ZS + z) * CS + c


Z_GROUPS = [[index_of(x, z, c) for z in range(ZS)] for x in range(XS) for c in range(CS)]
X_GROUPS = [[index_of(x, z, c) for x in range(XS)] for z in range(ZS) for c in range(CS)]
C_GROUPS = [[index_of(x, z, c) for c in range(CS)] for x in range(XS) for z in range(ZS)]


def spread(blocks, axis, groups):
    return lax.all_to_all(blocks, axis, 0, 0, tiled=True, axis_index_groups=groups)


def pack_kernel(heads, qlen_ref, query_in, grad_in, output_in, lse_in, out_ref, query_ref, grad_ref, output_ref, lse_ref, sems):
    copies = [
        pltpu.make_async_copy(source, target, sems.at[k])
        for k, (source, target) in enumerate(
            ((grad_in, grad_ref), (output_in, output_ref), (lse_in, lse_ref), (query_in, query_ref))
        )
    ]
    for copy in copies:
        copy.start()
    rows, columns = query_ref.shape
    shape = (rows, WIDTH)
    owner = lax.axis_index("psg")
    per_question = ASK_LEN // rows
    question = lax.div(owner, per_question)
    first = (owner - question * per_question) * rows
    column = lax.broadcasted_iota(jnp.int32, shape, 1)
    row = lax.broadcasted_iota(jnp.int32, shape, 0)
    live = first + row < qlen_ref[question]
    square = lax.broadcasted_iota(jnp.int32, (rows, rows), 0) == lax.broadcasted_iota(jnp.int32, (rows, rows), 1)
    value = jnp.zeros(shape, jnp.float32)
    for copy in copies:
        copy.wait()
    for head in range(heads):
        part = slice(head * WIDTH, (head + 1) * WIDTH)
        products = grad_ref[:, part].astype(jnp.float32) * output_ref[:, part].astype(jnp.float32)
        delta = jnp.sum(products, axis=1, keepdims=True)
        spread_lse = jnp.broadcast_to(lse_ref[head : head + 1, :], (rows, rows))
        shift = jnp.sum(jnp.where(square, spread_lse, 0.0), axis=1, keepdims=True) * (WIDTH**0.5)
        shift = jnp.where(live, shift, FAR)
        value = jnp.where(column % heads == head, jnp.where(column < 3 * heads, shift, delta), value)
    high = value.astype(jnp.bfloat16).astype(jnp.float32)
    middle = (value - high).astype(jnp.bfloat16).astype(jnp.float32)
    low = value - high - middle
    piece = (column // heads) % 3
    side = jnp.where(piece == 0, high, jnp.where(piece == 1, middle, low))
    side = jnp.where(column < 6 * heads, side, 0.0).astype(jnp.bfloat16)
    for copy in range(out_ref.shape[0]):
        out_ref[copy, :, :columns] = query_ref[...]
        out_ref[copy, :, columns : 2 * columns] = grad_ref[...]
        out_ref[copy, :, 2 * columns :] = side


def pack_rows(queries, grad_out, attn_out, log_sum, qlen, copies):
    rows, columns = queries.shape
    heads = log_sum.shape[0]
    anywhere = pl.BlockSpec(memory_space=pl.ANY)
    return pl.pallas_call(
        functools.partial(pack_kernel, heads),
        in_specs=[pl.BlockSpec(memory_space=pltpu.SMEM)] + [anywhere] * 4,
        out_specs=pl.BlockSpec(memory_space=pltpu.VMEM),
        out_shape=jax.ShapeDtypeStruct((copies, rows, 2 * columns + WIDTH), jnp.bfloat16),
        scratch_shapes=[
            pltpu.VMEM((rows, columns), jnp.bfloat16),
            pltpu.VMEM((rows, columns), jnp.bfloat16),
            pltpu.VMEM((rows, columns), jnp.bfloat16),
            pltpu.VMEM((heads, rows), jnp.float32),
            pltpu.SemaphoreType.DMA((4,)),
        ],
        compiler_params=pltpu.CompilerParams(vmem_limit_bytes=WIDE),
    )(qlen, queries, grad_out, attn_out, log_sum)


def select_kernel(attend_ref, rows_ref, out_ref, plan_ref, sems):
    questions, top = attend_ref.shape
    slots = out_ref.shape[1]
    owner = lax.axis_index("psg")
    core = lax.rem(owner, CS)
    copies = []
    for target in range(CS):
        block = owner - core + target
        count = jnp.int32(0)
        chosen = [jnp.int32(0)] * slots
        for question in range(questions):
            hit = jnp.int32(0)
            for place in range(top):
                hit = hit | (attend_ref[question, place] == block).astype(jnp.int32)
            chosen = [jnp.where((hit == 1) & (count == k), question, chosen[k]) for k in range(slots)]
            count = count + hit

            @pl.when(core == target)
            def _():
                plan_ref[0, question] = hit
                plan_ref[1, question] = jnp.clip(count - 1, 0, slots - 1)

        for slot in range(slots):
            copy = pltpu.make_async_copy(
                rows_ref.at[chosen[slot]], out_ref.at[target, slot], sems.at[target * slots + slot]
            )
            copy.start()
            copies.append(copy)
    for copy in copies:
        copy.wait()


def select(attend, rows, slots):
    return pl.pallas_call(
        select_kernel,
        in_specs=[pl.BlockSpec(memory_space=pltpu.SMEM), pl.BlockSpec(memory_space=pl.ANY)],
        out_specs=[pl.BlockSpec(memory_space=pl.ANY), pl.BlockSpec(memory_space=pltpu.SMEM)],
        out_shape=[
            jax.ShapeDtypeStruct((CS, slots, *rows.shape[1:]), rows.dtype),
            jax.ShapeDtypeStruct((2, attend.shape[0]), jnp.int32),
        ],
        scratch_shapes=[pltpu.SemaphoreType.DMA((CS * slots,))],
    )(attend, rows)


def visit_kernel(heads, span, plan, rows_ref, key_ref, value_ref, out_q, out_k, out_v):
    question = pl.program_id(0)
    scale = WIDTH**-0.5

    @pl.when(question == 0)
    def _():
        out_k[...] = jnp.zeros_like(out_k)
        out_v[...] = jnp.zeros_like(out_v)

    @pl.when(plan[0, question] == 0)
    def _():
        out_q[...] = jnp.zeros_like(out_q)

    @pl.when(plan[0, question] != 0)
    def _():
        key = key_ref[...]
        value = value_ref[...]
        key_t = key.astype(jnp.float32).T.astype(jnp.bfloat16)
        columns = lax.broadcasted_iota(jnp.int32, (span, WIDTH), 1)
        grad_k = jnp.zeros((span, WIDTH), jnp.float32)
        grad_v = jnp.zeros((span, WIDTH), jnp.float32)

        def take(start):
            return rows_ref[:, 0, :, :, start : start + WIDTH].reshape(ASK_LEN, WIDTH)

        side = take(2 * heads * WIDTH)
        for head in range(heads):
            query = take(head * WIDTH)
            cotangent = take((heads + head) * WIDTH)
            for_shift = (columns < 3 * heads) & (columns % heads == head)
            for_delta = (columns >= 3 * heads) & (columns < 6 * heads) & (columns % heads == head)
            minus_s = jnp.where(for_shift, -1.0, 0.0).astype(jnp.bfloat16)
            minus_d = jnp.where(for_delta, -1.0, 0.0).astype(jnp.bfloat16)
            energy = lax.dot_general(
                jnp.concatenate([key, minus_s], axis=1),
                jnp.concatenate([query, side], axis=1),
                (((1,), (1,)), ((), ())),
                preferred_element_type=jnp.float32,
            )
            prob = jnp.exp2(energy * (scale * LOG2E))
            change = lax.dot_general(
                jnp.concatenate([value, minus_d], axis=1),
                jnp.concatenate([cotangent, side], axis=1),
                (((1,), (1,)), ((), ())),
                preferred_element_type=jnp.float32,
            )
            low_score = (prob * change).astype(jnp.bfloat16)
            low_prob = prob.astype(jnp.bfloat16)
            grad_k = grad_k + jnp.dot(low_score, query, preferred_element_type=jnp.float32)
            grad_v = grad_v + jnp.dot(low_prob, cotangent, preferred_element_type=jnp.float32)
            term = jnp.dot(key_t, low_score, preferred_element_type=jnp.float32).T * scale
            term = term.astype(jnp.bfloat16)
            place = slice(head * WIDTH, (head + 1) * WIDTH)
            out_q[:, 0, :, :, place] = term.reshape(out_q.shape[0], out_q.shape[2], out_q.shape[3], WIDTH)
        out_k[...] += grad_k * scale
        out_v[...] += grad_v


def visits(plan, rows, keys, values, heads):
    cores, _, chunks, chunk, packed = rows.shape
    questions = plan.shape[1]
    span = keys.shape[0]
    columns = heads * WIDTH
    whole = pl.BlockSpec((span, WIDTH), lambda n, p: (0, 0))
    return pl.pallas_call(
        functools.partial(visit_kernel, heads, span),
        grid_spec=pltpu.PrefetchScalarGridSpec(
            num_scalar_prefetch=1,
            grid=(questions,),
            in_specs=[
                pl.BlockSpec((cores, 1, chunks, chunk, packed), lambda n, p: (0, p[1, n], 0, 0, 0)),
                whole,
                whole,
            ],
            out_specs=[
                pl.BlockSpec((cores, 1, chunks, chunk, columns), lambda n, p: (0, n, 0, 0, 0)),
                whole,
                whole,
            ],
        ),
        out_shape=[
            jax.ShapeDtypeStruct((cores, questions, chunks, chunk, columns), jnp.bfloat16),
            jax.ShapeDtypeStruct((span, WIDTH), jnp.float32),
            jax.ShapeDtypeStruct((span, WIDTH), jnp.float32),
        ],
        compiler_params=pltpu.CompilerParams(vmem_limit_bytes=40 * 2**20),
    )(plan, rows, keys, values)


def hidden_kernel(query_ref, weight_ref, out_ref):
    out_ref[0] = lax.dot_general(
        query_ref[...], weight_ref[...], (((1,), (1,)), ((), ())), preferred_element_type=jnp.float32
    ).astype(out_ref.dtype)


def hidden_parts(query_low, weight, parts):
    rows, columns = query_low.shape
    wide = weight.shape[0] // parts
    return pl.pallas_call(
        hidden_kernel,
        grid=(parts,),
        in_specs=[
            pl.BlockSpec((rows, columns), lambda n: (0, 0)),
            pl.BlockSpec((wide, columns), lambda n: (n, 0)),
        ],
        out_specs=pl.BlockSpec((1, rows, wide), lambda n: (n, 0, 0)),
        out_shape=jax.ShapeDtypeStruct((parts, rows, wide), jnp.bfloat16),
        compiler_params=pltpu.CompilerParams(vmem_limit_bytes=WIDE),
    )(query_low, weight)


def on_device(queries, grad_out, attn_out, log_sum, keys, values, proj_weight, attend, qlen):
    heads = log_sum.shape[0]
    rows, columns = queries.shape
    weight = lax.all_gather(proj_weight, "psg", axis=0, tiled=True)

    packed = pack_rows(queries, grad_out, attn_out, log_sum, qlen, ZS)
    line = spread(packed, "psg", Z_GROUPS)
    gathered = spread(jnp.broadcast_to(line[None], (XS, *line.shape)), "psg", X_GROUPS)
    question_total, top = attend.shape
    gathered = gathered.reshape(question_total, -1, rows, packed.shape[2])
    slots = min(question_total, 2 * question_total * top // (XS * ZS * CS))
    chosen, plan = select(attend, gathered, slots)
    chosen = spread(chosen, "psg", C_GROUPS)

    terms, grad_keys, grad_values = visits(plan, chosen, keys, values, heads)

    terms = spread(terms, "psg", C_GROUPS)
    pair = jnp.sum(terms.astype(jnp.float32), axis=0).astype(jnp.bfloat16)
    pair = spread(pair.reshape(XS, ZS, rows, columns), "psg", X_GROUPS)
    line = jnp.sum(pair.astype(jnp.float32), axis=0).astype(jnp.bfloat16)
    line, weight = lax.optimization_barrier((line, weight))
    line = spread(line, "psg", Z_GROUPS)
    grad_query = jnp.sum(line.astype(jnp.float32), axis=0)
    query_low = grad_query.astype(jnp.bfloat16)

    parts = lax.axis_size("qry")
    terms = hidden_parts(query_low, weight, parts)
    terms = spread(terms, "qry", None)
    hidden = jnp.sum(terms.astype(jnp.float32), axis=0)
    hidden = spread(jnp.broadcast_to(hidden[None], (parts, *hidden.shape)), "qry", None)
    grad_hidden = jnp.swapaxes(hidden, 0, 1).reshape(rows, -1)
    return (grad_query, grad_keys, grad_values, grad_hidden)


def solution(mesh):
    in_specs = (
        P("psg", "qry"),
        P("psg", "qry"),
        P("psg", "qry"),
        P("qry", "psg"),
        P("psg", "qry"),
        P("psg", "qry"),
        P("psg", "qry"),
        P(),
        P(),
    )
    out_specs = (P("psg", "qry"), P("psg", "qry"), P("psg", "qry"), P("psg", None))
    return jax.shard_map(
        on_device, mesh=mesh, in_specs=in_specs, out_specs=out_specs, check_vma=False
    )
```

time: 229 us -> 248 us (1.083)
  Pallas kernels: 13.6 us -> 92.3 us
  waiting for transfers between devices: 69.6 us -> 0.7 us
  blocking collectives: 116 us -> 137 us
  local copies, waits for them, and re-layouts: 5.79 us -> 1.11 us
  starting transfers between devices: 4.03 us -> 0.04 us
  other arithmetic: 5.1 us -> 1.51 us
    all_to_all x3 -> x8, blocking collectives: 57.1 us -> 137 us  [spread(): lax.all_to_all(blocks, axis, 0, 0, tiled=True, axis_index_groups=groups)]
    pallas_call x0 -> x2, Pallas kernels: none -> 76.5 us  [the longest x1 74.1 us: select(): pl.pallas_call(select_kernel, in_specs=[pl.BlockSpec(memory_space=pltpu.S...]
    all_gather x2 -> x0, blocking collectives: 59.4 us -> none  [the longest x1 34.1 us: on_device(): gathered = lax.all_gather(packed, 'psg', axis=0, axis_index_groups=Z_GROUPS)]
    all_gather x1 -> x0, waiting for transfers between devices: 33.9 us -> none  [on_device(): lax.all_gather(gathered, 'psg', axis=0, axis_index_groups=X_GROUPS)]
    all_gather x1, waiting for transfers between devices: 28.6 us -> 0.02 us  [on_device(): weight = lax.all_gather(proj_weight, 'psg', axis=0, tiled=True)]
    ppermute x2 -> x0, waiting for transfers between devices: 6.39 us -> none  [the longest x1 3.9 us: on_device(): other = lax.ppermute(own, 'psg', CORE_SWAP)]
    unnamed x10 -> x8, local copies, waits for them, and re-layouts: 4.36 us -> 0.03 us
    ppermute x2 -> x0, starting transfers between devices: 3.95 us -> none  [the longest x1 2.04 us: on_device(): swapped = lax.ppermute(other_q, 'psg', CORE_SWAP)]
  transfers between devices with their start and end apart: 4 -> 1, of which waited for: 4 -> 0; matrix products, arithmetic and copies ran while one was open for 1% -> 0% of each run, Pallas kernels for 3% -> 35%
where the time goes in v2:
time: 248 us; the launch traced here: 247 us
  blocking collectives  137 us (55%)
  Pallas kernels  92.3 us (37%)
  between operations  14.1 us (6%)
    all_to_all x8, blocking collectives, spread(): lax.all_to_all(blocks, axis, 0, 0, tiled=True, axis_index_groups=groups)  137 us
    pallas_call x1, Pallas kernels, select(): pl.pallas_call(select_kernel, in_specs=[pl.BlockSpec(memory_space=pltpu.S...  74.1 us
    pallas_call x1, Pallas kernels, visits(): pl.pallas_call(functools.partial(visit_kernel, heads, span), grid_spec=pl...  9.16 us
    pallas_call x1, Pallas kernels, hidden_parts(): pl.pallas_call(hidden_kernel, grid=(parts,), in_specs=[pl.BlockSpec((rows...  6.6 us
  transfers between devices with their start and end apart: 1, of which 0 were waited for; matrix products, arithmetic and copies ran while one was open for 0% of the time, Pallas kernels for 35%

profile of v2, /device:TPU:6, one launch (start us, length us, event | category | flops | bytes accessed | tf_op | source)
XLA Modules:
  0.0 246.8 jit_solution(7468598215555988404)
XLA Ops:
  7.2 0.0 all-gather.2.cloned.1.call-start
  7.2 0.7 all-gather.2.cloned.1.call-update
  7.9 2.5 shard_map.120
  10.4 29.6 %all_to_all.40 = bf16[8,32,1152]{2,1,0:T(8,128)(2,1)S(1)} all-to-all(bf16[8,32,1152]{2,1,0:T(8,128)(2,1)} %shard_map.120), channel_id=1, replica_groups={{0,16,32,48,64,80,96,112},{8,24,40,56,72,88,104,120},{128,144,160,176,1..., dimensions={0} | all-to-all | bytes 1179648 | tf_op jit(solution)/shard_map/all_to_all | solution.py:29
  40.0 0.2 broadcast_in_dim.4
  40.2 29.8 %all_to_all.41 = bf16[4,8,32,1152]{3,2,1,0:T(8,128)(2,1)} all-to-all(bf16[4,8,32,1152]{3,2,1,0:T(8,128)(2,1)S(1)} %broadcast_in_dim.4), channel_id=1, replica_groups={{0,128,256,384},{8,136,264,392},{16,144,272,400},{24,152,280,408},{32,1..., dimensions={0} | all-to-all | bytes 4718592 | tf_op jit(solution)/shard_map/all_to_all | solution.py:29
  70.0 74.1 %shard_map.121 = (bf16[2,4,4,32,1152]{4,3,2,1,0:T(8,128)(2,1)}, s32[2,8]{1,0:T(2,128)}) custom-call(s32[8,16]{1,0:T(8,128)} %attend_ref.1, bf16[8,4,32,1152]{3,2,1,0:T(8,128)(2,1)} %bitcast.5), custom_call_target="tpu_custom_call" | custom-call | tf_op jit(solution)/shard_map/pallas_call | solution.py:127
  144.1 0.0 copy-start
  144.1 0.0 copy-start.1
  144.1 0.0 copy-start.2
  144.1 7.0 %all_to_all.42.rows_ref = bf16[2,4,4,32,1152]{4,3,2,1,0:T(8,128)(2,1)S(1)} all-to-all(bf16[2,4,4,32,1152]{4,3,2,1,0:T(8,128)(2,1)} %get-tuple-element.12), channel_id=1, replica_groups={{0,8},{16,24},{32,40},{48,56},{64,72},{80,88},{96,104},{112,120},{128,1..., dimensions={0} | all-to-all | bytes 4718592 | tf_op jit(solution)/shard_map/all_to_all | solution.py:29
  151.1 0.0 copy-done
  151.1 0.0 copy-done.1
  151.1 0.0 copy-done.2
  151.1 9.2 %shard_map.122 = (bf16[2,8,4,32,512]{4,3,2,1,0:T(8,128)(2,1)S(1)}, f32[512,128]{1,0:T(8,128)}, f32[512,128]{1,0:T(8,128)}) custom-call(s32[2,8]{1,0:T(2,128)S(1)} %copy-done.2, bf16[2,4,4,32,1152]{4,3,2,1,0:T(8,128)(2,1)S(1)} %all_to_all.42.rows_ref, bf16[512,128]{1,0:T(8,128)(2,1)S(1)} %copy-done, bf16[512,128]{1,0:T(8,128)(2,1)S(1)} %copy-done.1), custom_call_target="tpu_custom_call" | custom-call | tf_op jit(solution)/shard_map/pallas_call | solution.py:203
  160.3 5.4 %all_to_all.43 = bf16[2,8,4,32,512]{4,3,2,1,0:T(8,128)(2,1)S(1)} all-to-all(bf16[2,8,4,32,512]{4,3,2,1,0:T(8,128)(2,1)S(1)} %get-tuple-element.13), channel_id=1, replica_groups={{0,8},{16,24},{32,40},{48,56},{64,72},{80,88},{96,104},{112,120},{128,1..., dimensions={0} | all-to-all | bytes 4194304 | tf_op jit(solution)/shard_map/all_to_all | solution.py:29
  165.7 0.6 reduce_sum.42
  166.3 17.6 %all_to_all.44 = bf16[4,8,32,512]{3,2,1,0:T(8,128)(2,1)S(1)} all-to-all(bf16[4,8,32,512]{3,2,1,0:T(8,128)(2,1)S(1)} %bitcast.6), channel_id=1, replica_groups={{0,128,256,384},{8,136,264,392},{16,144,272,400},{24,152,280,408},{32,1..., dimensions={0} | all-to-all | bytes 2097152 | tf_op jit(solution)/shard_map/all_to_all | solution.py:29
  184.0 0.2 reduce_sum.43
  184.2 0.0 all-gather.2.cloned.1.call-done.weight_ref
  184.2 13.4 %all_to_all.45 = bf16[8,32,512]{2,1,0:T(8,128)(2,1)S(1)} all-to-all(bf16[8,32,512]{2,1,0:T(8,128)(2,1)S(1)} %reduce_sum.43), channel_id=1, replica_groups={{0,16,32,48,64,80,96,112},{8,24,40,56,72,88,104,120},{128,144,160,176,1..., dimensions={0} | all-to-all | bytes 524288 | tf_op jit(solution)/shard_map/all_to_all | solution.py:29
  197.7 0.0 copy-start.3
  197.7 0.6 convert_element_type.14.query_ref
  198.3 6.6 %shard_map.123 = bf16[8,32,512]{2,1,0:T(8,128)(2,1)} custom-call(bf16[32,512]{1,0:T(8,128)(2,1)} %convert_element_type.14.query_ref, bf16[4096,512]{1,0:T(8,128)(2,1)} %all-gather.2.cloned.1.call-done.weight_ref), custom_call_target="tpu_custom_call" | custom-call | tf_op jit(solution)/shard_map/pallas_call | solution.py:237
  204.9 17.7 %all_to_all.46 = bf16[8,32,512]{2,1,0:T(8,128)(2,1)S(1)} all-to-all(bf16[8,32,512]{2,1,0:T(8,128)(2,1)} %shard_map.123), channel_id=1, replica_groups=mesh['psg'=64,'qry'=8] {'qry'}, dimensions={0} | all-to-all | bytes 524288 | tf_op jit(solution)/shard_map/all_to_all | solution.py:29
  222.6 0.0 copy-done.3
  222.6 0.1 broadcast_in_dim.5
  222.7 16.5 %all_to_all.47 = f32[8,32,512]{2,1,0:T(8,128)S(1)} all-to-all(f32[8,32,512]{2,1,0:T(8,128)S(1)} %broadcast_in_dim.5), channel_id=1, replica_groups=mesh['psg'=64,'qry'=8] {'qry'}, dimensions={0} | all-to-all | bytes 1048576 | tf_op jit(solution)/shard_map/all_to_all | solution.py:29
  239.1 0.8 copy.15
  (2 shorter events, 0.1 us)
Async XLA Ops:
  7.2 177.0 %all-gather.2.cloned.1.call-start = ((), (), s32[]{:S(2)}) async-start(), calls=%async_computation.8 | async-start | bytes 4259840 | tf_op jit(solution)/shard_map/all_gather | solution.py:253
  144.1 7.0 %copy-start = (bf16[512,128]{1,0:T(8,128)(2,1)S(1)}, bf16[512,128]{1,0:T(8,128)(2,1)}, u32[]{:S(2)}) copy-start(bf16[512,128]{1,0:T(8,128)(2,1)} %key_ref.1) | copy-start | bytes 393220
  144.1 7.0 %copy-start.1 = (bf16[512,128]{1,0:T(8,128)(2,1)S(1)}, bf16[512,128]{1,0:T(8,128)(2,1)}, u32[]{:S(2)}) copy-start(bf16[512,128]{1,0:T(8,128)(2,1)} %value_ref.1) | copy-start | bytes 393220
  144.1 7.0 %copy-start.2 = (s32[2,8]{1,0:T(2,128)S(1)}, s32[2,8]{1,0:T(2,128)}, u32[]{:S(2)}) copy-start(s32[2,8]{1,0:T(2,128)} %get-tuple-element.11.plan) | copy-start | bytes 196
  197.7 24.9 %copy-start.3 = (f32[32,512]{1,0:T(8,128)}, f32[32,512]{1,0:T(8,128)S(1)}, u32[]{:S(2)}) copy-start(f32[32,512]{1,0:T(8,128)S(1)} %convert_reduce_fusion.1) | copy-start | bytes 196612
Sparse Core Ops, SparseCore 0:
  11.4 88.7 all-gather.1

commit v3 on v2

--- a/solution.py
+++ b/solution.py
@@ -13,7 +13,7 @@
 XS, ZS, CS = 4, 8, 2
 LOG2E = 1.4426950408889634
 FAR = 1.0e6
-WIDE = 60 * 2**20
+WIDE = 63 * 2**20
 
 
 def index_of(x, z, c):
@@ -23,6 +23,9 @@
 Z_GROUPS = [[index_of(x, z, c) for z in range(ZS)] for x in range(XS) for c in range(CS)]
 X_GROUPS = [[index_of(x, z, c) for x in range(XS)] for z in range(ZS) for c in range(CS)]
 C_GROUPS = [[index_of(x, z, c) for c in range(CS)] for x in range(XS) for z in range(ZS)]
+
+CORE_GROUPS = [[index_of(x, z, c) for x in range(XS) for z in range(ZS)] for c in range(CS)]
+CORE_SWAP = [(i, i ^ 1) for i in range(XS * ZS * CS)]
 
 
 def spread(blocks, axis, groups):
@@ -91,12 +94,11 @@
     )(qlen, queries, grad_out, attn_out, log_sum)
 
 
-def select_kernel(attend_ref, rows_ref, out_ref, plan_ref, sems):
+def select_kernel(attend_ref, rows_ref, out_ref, plan_ref):
     questions, top = attend_ref.shape
     slots = out_ref.shape[1]
     owner = lax.axis_index("psg")
     core = lax.rem(owner, CS)
-    copies = []
     for target in range(CS):
         block = owner - core + target
         count = jnp.int32(0)
@@ -114,25 +116,18 @@
                 plan_ref[1, question] = jnp.clip(count - 1, 0, slots - 1)
 
         for slot in range(slots):
-            copy = pltpu.make_async_copy(
-                rows_ref.at[chosen[slot]], out_ref.at[target, slot], sems.at[target * slots + slot]
-            )
-            copy.start()
-            copies.append(copy)
-    for copy in copies:
-        copy.wait()
+            out_ref[target, slot] = rows_ref[chosen[slot]]
 
 
 def select(attend, rows, slots):
     return pl.pallas_call(
         select_kernel,
-        in_specs=[pl.BlockSpec(memory_space=pltpu.SMEM), pl.BlockSpec(memory_space=pl.ANY)],
-        out_specs=[pl.BlockSpec(memory_space=pl.ANY), pl.BlockSpec(memory_space=pltpu.SMEM)],
+        in_specs=[pl.BlockSpec(memory_space=pltpu.SMEM), pl.BlockSpec(memory_space=pltpu.VMEM)],
+        out_specs=[pl.BlockSpec(memory_space=pltpu.VMEM), pl.BlockSpec(memory_space=pltpu.SMEM)],
         out_shape=[
             jax.ShapeDtypeStruct((CS, slots, *rows.shape[1:]), rows.dtype),
             jax.ShapeDtypeStruct((2, attend.shape[0]), jnp.int32),
         ],
-        scratch_shapes=[pltpu.SemaphoreType.DMA((CS * slots,))],
     )(attend, rows)
 
 
@@ -225,37 +220,56 @@
     )(plan, rows, keys, values)
 
 
-def hidden_kernel(query_ref, weight_ref, out_ref):
-    out_ref[0] = lax.dot_general(
-        query_ref[...], weight_ref[...], (((1,), (1,)), ((), ())), preferred_element_type=jnp.float32
-    ).astype(out_ref.dtype)
-
-
-def hidden_parts(query_low, weight, parts):
+def hidden_kernel(query_ref, own_ref, other_ref, out_ref):
+    core = lax.rem(lax.axis_index("psg"), CS)
+    parts, _, wide = out_ref.shape
+    blocks = own_ref.shape[0] // parts
+
+    def product(first_ref, second_ref):
+        for part in range(parts):
+            here = pl.ds(part * blocks, blocks)
+            weight = jnp.concatenate([first_ref[here], second_ref[here]], axis=1)
+            out_ref[part] = lax.dot_general(
+                query_ref[...],
+                weight.reshape(wide, weight.shape[2]),
+                (((1,), (1,)), ((), ())),
+                preferred_element_type=jnp.float32,
+            ).astype(out_ref.dtype)
+
+    @pl.when(core == 0)
+    def _():
+        product(own_ref, other_ref)
+
+    @pl.when(core != 0)
+    def _():
+        product(other_ref, own_ref)
+
+
+def hidden_parts(query_low, own, other, parts):
     rows, columns = query_low.shape
-    wide = weight.shape[0] // parts
+    chips, height, _ = own.shape
+    wide = CS * chips * height // parts
+    steps = 4
+    weights = pl.BlockSpec((chips // steps, height, columns), lambda n: (n, 0, 0))
     return pl.pallas_call(
         hidden_kernel,
-        grid=(parts,),
-        in_specs=[
-            pl.BlockSpec((rows, columns), lambda n: (0, 0)),
-            pl.BlockSpec((wide, columns), lambda n: (n, 0)),
-        ],
-        out_specs=pl.BlockSpec((1, rows, wide), lambda n: (n, 0, 0)),
+        grid=(steps,),
+        in_specs=[pl.BlockSpec((rows, columns), lambda n: (0, 0)), weights, weights],
+        out_specs=pl.BlockSpec((parts // steps, rows, wide), lambda n: (n, 0, 0)),
         out_shape=jax.ShapeDtypeStruct((parts, rows, wide), jnp.bfloat16),
         compiler_params=pltpu.CompilerParams(vmem_limit_bytes=WIDE),
-    )(query_low, weight)
+    )(query_low, own, other)
 
 
 def on_device(queries, grad_out, attn_out, log_sum, keys, values, proj_weight, attend, qlen):
     heads = log_sum.shape[0]
     rows, columns = queries.shape
-    weight = lax.all_gather(proj_weight, "psg", axis=0, tiled=True)
-
     packed = pack_rows(queries, grad_out, attn_out, log_sum, qlen, ZS)
     line = spread(packed, "psg", Z_GROUPS)
     gathered = spread(jnp.broadcast_to(line[None], (XS, *line.shape)), "psg", X_GROUPS)
     question_total, top = attend.shape
+    gathered, proj_weight = lax.optimization_barrier((gathered, proj_weight))
+    own_weight = lax.all_gather(proj_weight, "psg", axis=0, axis_index_groups=CORE_GROUPS)
     gathered = gathered.reshape(question_total, -1, rows, packed.shape[2])
     slots = min(question_total, 2 * question_total * top // (XS * ZS * CS))
     chosen, plan = select(attend, gathered, slots)
@@ -267,13 +281,14 @@
     pair = jnp.sum(terms.astype(jnp.float32), axis=0).astype(jnp.bfloat16)
     pair = spread(pair.reshape(XS, ZS, rows, columns), "psg", X_GROUPS)
     line = jnp.sum(pair.astype(jnp.float32), axis=0).astype(jnp.bfloat16)
-    line, weight = lax.optimization_barrier((line, weight))
+    line, own_weight = lax.optimization_barrier((line, own_weight))
+    other_weight = lax.ppermute(own_weight, "psg", CORE_SWAP)
     line = spread(line, "psg", Z_GROUPS)
     grad_query = jnp.sum(line.astype(jnp.float32), axis=0)
     query_low = grad_query.astype(jnp.bfloat16)
 
     parts = lax.axis_size("qry")
-    terms = hidden_parts(query_low, weight, parts)
+    terms = hidden_parts(query_low, own_weight, other_weight, parts)
     terms = spread(terms, "qry", None)
     hidden = jnp.sum(terms.astype(jnp.float32), axis=0)
     hidden = spread(jnp.broadcast_to(hidden[None], (parts, *hidden.shape)), "qry", None)

time: 248 us -> 219 us (0.88)
  Pallas kernels: 92.3 us -> 14.3 us
  waiting for transfers between devices: 0.7 us -> 39.9 us
  blocking collectives: 137 us -> 146 us
    pallas_call x1, Pallas kernels: 74.1 us -> 3.46 us  [select(): pl.pallas_call(select_kernel, in_specs=[pl.BlockSpec(memory_space=pltpu.S...]
    all_gather x1, waiting for transfers between devices: 0.02 us -> 39.9 us  [on_device(): lax.all_gather(proj_weight, 'psg', axis=0, axis_index_groups=CORE_GROUPS)]
    all_to_all x8, blocking collectives: 137 us -> 146 us  [spread(): lax.all_to_all(blocks, axis, 0, 0, tiled=True, axis_index_groups=groups)]
    pallas_call x1, Pallas kernels: 9.16 us -> 3.8 us  [visits(): pl.pallas_call(functools.partial(visit_kernel, heads, span), grid_spec=pl...]
  transfers between devices with their start and end apart: 1 -> 2, of which waited for: 0 -> 1; matrix products, arithmetic and copies ran while one was open for 0% -> 1% of each run, Pallas kernels for 35% -> 3%
where the time goes in v3:
time: 219 us; the launch traced here: 218 us
  blocking collectives  146 us (67%)
  waiting for transfers between devices  39.9 us (18%)
  Pallas kernels  14.3 us (7%)
  between operations  14.1 us (6%)
    all_to_all x8, blocking collectives, spread(): lax.all_to_all(blocks, axis, 0, 0, tiled=True, axis_index_groups=groups)  146 us
    all_gather x1, waiting for transfers between devices, on_device(): lax.all_gather(proj_weight, 'psg', axis=0, axis_index_groups=CORE_GROUPS)  39.9 us
    pallas_call x1, Pallas kernels, hidden_parts(): pl.pallas_call(hidden_kernel, grid=(steps,), in_specs=[pl.BlockSpec((rows...  4.57 us
  transfers between devices with their start and end apart: 2, of which 1 were waited for; matrix products, arithmetic and copies ran while one was open for 1% of the time, Pallas kernels for 3%

profile of v3, /device:TPU:6, one launch (start us, length us, event | category | flops | bytes accessed | tf_op | source)
XLA Modules:
  0.0 218.5 jit_solution(7734214480826344727)
XLA Ops:
  7.2 0.0 all-gather.3.cloned.1.call-start
  7.2 2.4 %shard_map.120 = bf16[8,32,1152]{2,1,0:T(8,128)(2,1)} custom-call(s32[8]{0:T(128)} %qlen_ref.1, bf16[32,512]{1,0:T(8,128)(2,1)} %query_in.1, bf16[32,512]{1,0:T(8,128)(2,1)} %grad_in.1, bf16[32,512]{1,0:T(8,128)(2,1)} %output_in.1, f32[4,32]{1,0:T(4,128)} %lse_in.1), custom_call_target="tpu_custom_call" | custom-call | tf_op jit(solution)/shard_map/pallas_call | solution.py:81
  9.7 29.2 %all_to_all.40 = bf16[8,32,1152]{2,1,0:T(8,128)(2,1)S(1)} all-to-all(bf16[8,32,1152]{2,1,0:T(8,128)(2,1)} %shard_map.120), channel_id=1, replica_groups={{0,16,32,48,64,80,96,112},{8,24,40,56,72,88,104,120},{128,144,160,176,1..., dimensions={0} | all-to-all | bytes 1179648 | tf_op jit(solution)/shard_map/all_to_all | solution.py:32
  38.9 0.2 broadcast_in_dim.4
  39.1 30.0 %all_to_all.41 = bf16[4,8,32,1152]{3,2,1,0:T(8,128)(2,1)} all-to-all(bf16[4,8,32,1152]{3,2,1,0:T(8,128)(2,1)S(1)} %broadcast_in_dim.4), channel_id=1, replica_groups={{0,128,256,384},{8,136,264,392},{16,144,272,400},{24,152,280,408},{32,1..., dimensions={0} | all-to-all | bytes 4718592 | tf_op jit(solution)/shard_map/all_to_all | solution.py:32
  69.1 0.0 all-gather.3.cloned.1.call-update
  69.1 3.5 %shard_map.121 = (bf16[2,4,4,32,1152]{4,3,2,1,0:T(8,128)(2,1)}, s32[2,8]{1,0:T(2,128)}) custom-call(s32[8,16]{1,0:T(8,128)} %attend_ref.1, bf16[8,4,32,1152]{3,2,1,0:T(8,128)(2,1)} %bitcast.6), custom_call_target="tpu_custom_call" | custom-call | tf_op jit(solution)/shard_map/pallas_call | solution.py:123
  72.6 0.0 copy-start
  72.6 0.0 copy-start.1
  72.6 0.0 copy-start.2
  72.6 7.0 %all_to_all.42.rows_ref = bf16[2,4,4,32,1152]{4,3,2,1,0:T(8,128)(2,1)S(1)} all-to-all(bf16[2,4,4,32,1152]{4,3,2,1,0:T(8,128)(2,1)} %get-tuple-element.15), channel_id=1, replica_groups={{0,8},{16,24},{32,40},{48,56},{64,72},{80,88},{96,104},{112,120},{128,1..., dimensions={0} | all-to-all | bytes 4718592 | tf_op jit(solution)/shard_map/all_to_all | solution.py:32
  79.6 0.0 copy-done
  79.6 0.0 copy-done.1
  79.6 0.0 copy-done.2
  79.6 3.8 %shard_map.122 = (bf16[2,8,4,32,512]{4,3,2,1,0:T(8,128)(2,1)S(1)}, f32[512,128]{1,0:T(8,128)}, f32[512,128]{1,0:T(8,128)}) custom-call(s32[2,8]{1,0:T(2,128)S(1)} %copy-done.2, bf16[2,4,4,32,1152]{4,3,2,1,0:T(8,128)(2,1)S(1)} %all_to_all.42.rows_ref, bf16[512,128]{1,0:T(8,128)(2,1)S(1)} %copy-done, bf16[512,128]{1,0:T(8,128)(2,1)S(1)} %copy-done.1), custom_call_target="tpu_custom_call" | custom-call | tf_op jit(solution)/shard_map/pallas_call | solution.py:198
  83.4 5.4 %all_to_all.43 = bf16[2,8,4,32,512]{4,3,2,1,0:T(8,128)(2,1)S(1)} all-to-all(bf16[2,8,4,32,512]{4,3,2,1,0:T(8,128)(2,1)S(1)} %get-tuple-element.16), channel_id=1, replica_groups={{0,8},{16,24},{32,40},{48,56},{64,72},{80,88},{96,104},{112,120},{128,1..., dimensions={0} | all-to-all | bytes 4194304 | tf_op jit(solution)/shard_map/all_to_all | solution.py:32
  88.8 0.6 reduce_sum.42
  89.5 19.9 %all_to_all.44 = bf16[4,8,32,512]{3,2,1,0:T(8,128)(2,1)S(1)} all-to-all(bf16[4,8,32,512]{3,2,1,0:T(8,128)(2,1)S(1)} %bitcast.7), channel_id=1, replica_groups={{0,128,256,384},{8,136,264,392},{16,144,272,400},{24,152,280,408},{32,1..., dimensions={0} | all-to-all | bytes 2097152 | tf_op jit(solution)/shard_map/all_to_all | solution.py:32
  109.3 0.2 reduce_sum.43
  109.5 39.9 %all-gather.3.cloned.1.call-done = bf16[2048,512]{1,0:T(8,128)(2,1)} async-done(((bf16[64,512]{1,0:T(8,128)(2,1)}), bf16[2048,512]{1,0:T(8,128)(2,1)}) %all-gather.3.cloned.1.call-update) | async-done | bytes 2097168 | tf_op jit(solution)/shard_map/all_gather | solution.py:272
  149.4 1.9 collective-permute-start
  151.3 16.5 %all_to_all.45 = bf16[8,32,512]{2,1,0:T(8,128)(2,1)S(1)} all-to-all(bf16[8,32,512]{2,1,0:T(8,128)(2,1)S(1)} %reduce_sum.43), channel_id=1, replica_groups={{0,16,32,48,64,80,96,112},{8,24,40,56,72,88,104,120},{128,144,160,176,1..., dimensions={0} | all-to-all | bytes 524288 | tf_op jit(solution)/shard_map/all_to_all | solution.py:32
  167.9 0.0 copy-start.3
  167.9 0.6 convert_element_type.14.query_ref
  168.5 0.0 collective-permute-done.other_ref
  168.5 4.6 %shard_map.123 = bf16[8,32,512]{2,1,0:T(8,128)(2,1)} custom-call(bf16[32,512]{1,0:T(8,128)(2,1)} %convert_element_type.14.query_ref, bf16[32,64,512]{2,1,0:T(8,128)(2,1)} %bitcast.9, bf16[32,64,512]{2,1,0:T(8,128)(2,1)} %collective-permute-done.other_ref), custom_call_target="tpu_custom_call" | custom-call | tf_op jit(solution)/shard_map/pallas_call | solution.py:254
  173.1 18.8 %all_to_all.46 = bf16[8,32,512]{2,1,0:T(8,128)(2,1)S(1)} all-to-all(bf16[8,32,512]{2,1,0:T(8,128)(2,1)} %shard_map.123), channel_id=1, replica_groups=mesh['psg'=64,'qry'=8] {'qry'}, dimensions={0} | all-to-all | bytes 524288 | tf_op jit(solution)/shard_map/all_to_all | solution.py:32
  191.9 0.0 copy-done.3
  192.0 0.1 broadcast_in_dim.5
  192.0 18.8 %all_to_all.47 = f32[8,32,512]{2,1,0:T(8,128)S(1)} all-to-all(f32[8,32,512]{2,1,0:T(8,128)S(1)} %broadcast_in_dim.5), channel_id=1, replica_groups=mesh['psg'=64,'qry'=8] {'qry'}, dimensions={0} | all-to-all | bytes 1048576 | tf_op jit(solution)/shard_map/all_to_all | solution.py:32
  210.8 0.8 copy.15
  (2 shorter events, 0.1 us)
Async XLA Ops:
  7.2 142.2 %all-gather.3.cloned.1.call-start = ((), (), s32[]{:S(2)}) async-start(), calls=%async_computation.8 | async-start | bytes 2162688 | tf_op jit(solution)/shard_map/all_gather | solution.py:272
  72.6 7.0 %copy-start = (bf16[512,128]{1,0:T(8,128)(2,1)S(1)}, bf16[512,128]{1,0:T(8,128)(2,1)}, u32[]{:S(2)}) copy-start(bf16[512,128]{1,0:T(8,128)(2,1)} %key_ref.1) | copy-start | bytes 393220
  72.6 7.0 %copy-start.1 = (bf16[512,128]{1,0:T(8,128)(2,1)S(1)}, bf16[512,128]{1,0:T(8,128)(2,1)}, u32[]{:S(2)}) copy-start(bf16[512,128]{1,0:T(8,128)(2,1)} %value_ref.1) | copy-start | bytes 393220
  72.6 7.0 %copy-start.2 = (s32[2,8]{1,0:T(2,128)S(1)}, s32[2,8]{1,0:T(2,128)}, u32[]{:S(2)}) copy-start(s32[2,8]{1,0:T(2,128)} %get-tuple-element.14.plan) | copy-start | bytes 196
  149.4 19.1 %collective-permute-start = (bf16[32,64,512]{2,1,0:T(8,128)(2,1)}, bf16[32,64,512]{2,1,0:T(8,128)(2,1)}, u32[]{:S(2)}, u32[]{:S(2)}) collective-permute-start(bf16[32,64,512]{2,1,0:T(8,128)(2,1)} %bitcast.8), channel_id=1, source_target_pairs={{0,8},{8,0},{16,24},{24,16},{32,40},{40,32},{48,56},{56,48},{64,72... | collective-permute-start | bytes 6291464 | tf_op jit(solution)/shard_map/ppermute | solution.py:285
  167.9 24.0 %copy-start.3 = (f32[32,512]{1,0:T(8,128)}, f32[32,512]{1,0:T(8,128)S(1)}, u32[]{:S(2)}) copy-start(f32[32,512]{1,0:T(8,128)S(1)} %convert_reduce_fusion.1) | copy-start | bytes 196612
Sparse Core Ops, SparseCore 0:
  69.2 80.1 all-gather.2

commit v4 on v2

--- a/solution.py
+++ b/solution.py
@@ -13,7 +13,7 @@
 XS, ZS, CS = 4, 8, 2
 LOG2E = 1.4426950408889634
 FAR = 1.0e6
-WIDE = 60 * 2**20
+WIDE = 63 * 2**20
 
 
 def index_of(x, z, c):
@@ -23,6 +23,8 @@
 Z_GROUPS = [[index_of(x, z, c) for z in range(ZS)] for x in range(XS) for c in range(CS)]
 X_GROUPS = [[index_of(x, z, c) for x in range(XS)] for z in range(ZS) for c in range(CS)]
 C_GROUPS = [[index_of(x, z, c) for c in range(CS)] for x in range(XS) for z in range(ZS)]
+
+PLANE_GROUPS = [[index_of(x, z, c) for x in range(XS) for z in range(ZS)] for c in range(CS)]
 
 
 def spread(blocks, axis, groups):
@@ -91,12 +93,11 @@
     )(qlen, queries, grad_out, attn_out, log_sum)
 
 
-def select_kernel(attend_ref, rows_ref, out_ref, plan_ref, sems):
+def select_kernel(attend_ref, rows_ref, out_ref, plan_ref):
     questions, top = attend_ref.shape
     slots = out_ref.shape[1]
     owner = lax.axis_index("psg")
     core = lax.rem(owner, CS)
-    copies = []
     for target in range(CS):
         block = owner - core + target
         count = jnp.int32(0)
@@ -114,25 +115,19 @@
                 plan_ref[1, question] = jnp.clip(count - 1, 0, slots - 1)
 
         for slot in range(slots):
-            copy = pltpu.make_async_copy(
-                rows_ref.at[chosen[slot]], out_ref.at[target, slot], sems.at[target * slots + slot]
-            )
-            copy.start()
-            copies.append(copy)
-    for copy in copies:
-        copy.wait()
+            out_ref[target, slot] = rows_ref[chosen[slot]]
 
 
 def select(attend, rows, slots):
     return pl.pallas_call(
         select_kernel,
-        in_specs=[pl.BlockSpec(memory_space=pltpu.SMEM), pl.BlockSpec(memory_space=pl.ANY)],
-        out_specs=[pl.BlockSpec(memory_space=pl.ANY), pl.BlockSpec(memory_space=pltpu.SMEM)],
+        in_specs=[pl.BlockSpec(memory_space=pltpu.SMEM), pl.BlockSpec(memory_space=pltpu.VMEM)],
+        out_specs=[pl.BlockSpec(memory_space=pltpu.VMEM), pl.BlockSpec(memory_space=pltpu.SMEM)],
         out_shape=[
             jax.ShapeDtypeStruct((CS, slots, *rows.shape[1:]), rows.dtype),
             jax.ShapeDtypeStruct((2, attend.shape[0]), jnp.int32),
         ],
-        scratch_shapes=[pltpu.SemaphoreType.DMA((CS * slots,))],
+        compiler_params=pltpu.CompilerParams(vmem_limit_bytes=16 * 2**20),
     )(attend, rows)
 
 
@@ -221,29 +216,36 @@
             jax.ShapeDtypeStruct((span, WIDTH), jnp.float32),
             jax.ShapeDtypeStruct((span, WIDTH), jnp.float32),
         ],
-        compiler_params=pltpu.CompilerParams(vmem_limit_bytes=40 * 2**20),
+        compiler_params=pltpu.CompilerParams(vmem_limit_bytes=32 * 2**20),
     )(plan, rows, keys, values)
 
 
 def hidden_kernel(query_ref, weight_ref, out_ref):
-    out_ref[0] = lax.dot_general(
-        query_ref[...], weight_ref[...], (((1,), (1,)), ((), ())), preferred_element_type=jnp.float32
-    ).astype(out_ref.dtype)
+    parts, _, wide = out_ref.shape
+    for part in range(parts):
+        out_ref[part] = lax.dot_general(
+            query_ref[...],
+            weight_ref[pl.ds(part * wide, wide)],
+            (((1,), (1,)), ((), ())),
+            preferred_element_type=jnp.float32,
+        ).astype(out_ref.dtype)
 
 
 def hidden_parts(query_low, weight, parts):
     rows, columns = query_low.shape
-    wide = weight.shape[0] // parts
+    total = weight.shape[0]
+    wide = total // parts
+    steps = 4
     return pl.pallas_call(
         hidden_kernel,
-        grid=(parts,),
+        grid=(steps,),
         in_specs=[
             pl.BlockSpec((rows, columns), lambda n: (0, 0)),
-            pl.BlockSpec((wide, columns), lambda n: (n, 0)),
-        ],
-        out_specs=pl.BlockSpec((1, rows, wide), lambda n: (n, 0, 0)),
+            pl.BlockSpec((total // steps, columns), lambda n: (n, 0)),
+        ],
+        out_specs=pl.BlockSpec((parts // steps, rows, wide), lambda n: (n, 0, 0)),
         out_shape=jax.ShapeDtypeStruct((parts, rows, wide), jnp.bfloat16),
-        compiler_params=pltpu.CompilerParams(vmem_limit_bytes=WIDE),
+        compiler_params=pltpu.CompilerParams(vmem_limit_bytes=60 * 2**20),
     )(query_low, weight)
 
 
@@ -265,19 +267,16 @@
 
     terms = spread(terms, "psg", C_GROUPS)
     pair = jnp.sum(terms.astype(jnp.float32), axis=0).astype(jnp.bfloat16)
-    pair = spread(pair.reshape(XS, ZS, rows, columns), "psg", X_GROUPS)
-    line = jnp.sum(pair.astype(jnp.float32), axis=0).astype(jnp.bfloat16)
-    line, weight = lax.optimization_barrier((line, weight))
-    line = spread(line, "psg", Z_GROUPS)
-    grad_query = jnp.sum(line.astype(jnp.float32), axis=0)
+    plane = spread(pair.reshape(XS * ZS, rows, columns), "psg", PLANE_GROUPS)
+    grad_query = jnp.sum(plane.astype(jnp.float32), axis=0)
     query_low = grad_query.astype(jnp.bfloat16)
 
     parts = lax.axis_size("qry")
     terms = hidden_parts(query_low, weight, parts)
     terms = spread(terms, "qry", None)
-    hidden = jnp.sum(terms.astype(jnp.float32), axis=0)
+    hidden = jnp.sum(terms.astype(jnp.float32), axis=0).astype(jnp.bfloat16)
     hidden = spread(jnp.broadcast_to(hidden[None], (parts, *hidden.shape)), "qry", None)
-    grad_hidden = jnp.swapaxes(hidden, 0, 1).reshape(rows, -1)
+    grad_hidden = jnp.swapaxes(hidden.astype(jnp.float32), 0, 1).reshape(rows, -1)
     return (grad_query, grad_keys, grad_values, grad_hidden)
 
 

time: 248 us -> 171 us (0.69)
  Pallas kernels: 92.3 us -> 12.5 us
    pallas_call x1, Pallas kernels: 74.1 us -> 1.57 us  [select(): pl.pallas_call(select_kernel, in_specs=[pl.BlockSpec(memory_space=pltpu.S...]
    pallas_call x1, Pallas kernels: 9.16 us -> 3.8 us  [visits(): pl.pallas_call(functools.partial(visit_kernel, heads, span), grid_spec=pl...]
    all_to_all x8 -> x7, blocking collectives: 137 us -> 138 us  [spread(): lax.all_to_all(blocks, axis, 0, 0, tiled=True, axis_index_groups=groups)]
  transfers between devices with their start and end apart: 1 -> 1, of which waited for: 0 -> 0; matrix products, arithmetic and copies ran while one was open for 0% -> 1% of each run, Pallas kernels for 35% -> 5%
where the time goes in v4:
time: 171 us; the launch traced here: 168 us
  blocking collectives  138 us (81%)
  between operations  14.1 us (8%)
  Pallas kernels  12.5 us (7%)
    all_to_all x7, blocking collectives, spread(): lax.all_to_all(blocks, axis, 0, 0, tiled=True, axis_index_groups=groups)  138 us
    pallas_call x1, Pallas kernels, hidden_parts(): pl.pallas_call(hidden_kernel, grid=(steps,), in_specs=[pl.BlockSpec((rows...  4.62 us
    pallas_call x1, Pallas kernels, visits(): pl.pallas_call(functools.partial(visit_kernel, heads, span), grid_spec=pl...  3.8 us
  transfers between devices with their start and end apart: 1, of which 0 were waited for; matrix products, arithmetic and copies ran while one was open for 1% of the time, Pallas kernels for 5%

profile of v4, /device:TPU:6, one launch (start us, length us, event | category | flops | bytes accessed | tf_op | source)
XLA Modules:
  0.0 168.2 jit_solution(17917679101175978681)
XLA Ops:
  7.2 0.0 all-gather.2.cloned.1.call-start
  7.2 0.7 all-gather.2.cloned.1.call-update
  7.9 2.5 %shard_map.120 = bf16[8,32,1152]{2,1,0:T(8,128)(2,1)} custom-call(s32[8]{0:T(128)} %qlen_ref.1, bf16[32,512]{1,0:T(8,128)(2,1)} %query_in.1, bf16[32,512]{1,0:T(8,128)(2,1)} %grad_in.1, bf16[32,512]{1,0:T(8,128)(2,1)} %output_in.1, f32[4,32]{1,0:T(4,128)} %lse_in.1), custom_call_target="tpu_custom_call" | custom-call | tf_op jit(solution)/shard_map/pallas_call | solution.py:80
  10.4 29.6 %all_to_all.35 = bf16[8,32,1152]{2,1,0:T(8,128)(2,1)S(1)} all-to-all(bf16[8,32,1152]{2,1,0:T(8,128)(2,1)} %shard_map.120), channel_id=1, replica_groups={{0,16,32,48,64,80,96,112},{8,24,40,56,72,88,104,120},{128,144,160,176,1..., dimensions={0} | all-to-all | bytes 1179648 | tf_op jit(solution)/shard_map/all_to_all | solution.py:31
  40.0 0.2 broadcast_in_dim.4
  40.2 0.0 copy-start.2
  40.2 29.7 %all_to_all.36 = bf16[4,8,32,1152]{3,2,1,0:T(8,128)(2,1)S(1)} all-to-all(bf16[4,8,32,1152]{3,2,1,0:T(8,128)(2,1)S(1)} %broadcast_in_dim.4), channel_id=1, replica_groups={{0,128,256,384},{8,136,264,392},{16,144,272,400},{24,152,280,408},{32,1..., dimensions={0} | all-to-all | bytes 4718592 | tf_op jit(solution)/shard_map/all_to_all | solution.py:31
  69.9 0.0 copy-done.2
  69.9 1.6 shard_map.121
  71.5 0.0 copy-start
  71.5 0.0 copy-start.1
  71.5 6.3 %all_to_all.37.rows_ref = bf16[2,4,4,32,1152]{4,3,2,1,0:T(8,128)(2,1)S(1)} all-to-all(bf16[2,4,4,32,1152]{4,3,2,1,0:T(8,128)(2,1)S(1)} %get-tuple-element.10), channel_id=1, replica_groups={{0,8},{16,24},{32,40},{48,56},{64,72},{80,88},{96,104},{112,120},{128,1..., dimensions={0} | all-to-all | bytes 4718592 | tf_op jit(solution)/shard_map/all_to_all | solution.py:31
  77.9 0.0 copy-done
  77.9 0.0 copy-done.1
  77.9 3.8 %shard_map.122 = (bf16[2,8,4,32,512]{4,3,2,1,0:T(8,128)(2,1)S(1)}, f32[512,128]{1,0:T(8,128)}, f32[512,128]{1,0:T(8,128)}) custom-call(s32[2,8]{1,0:T(2,128)S(1)} %get-tuple-element.9.plan, bf16[2,4,4,32,1152]{4,3,2,1,0:T(8,128)(2,1)S(1)} %all_to_all.37.rows_ref, bf16[512,128]{1,0:T(8,128)(2,1)S(1)} %copy-done, bf16[512,128]{1,0:T(8,128)(2,1)S(1)} %copy-done.1), custom_call_target="tpu_custom_call" | custom-call | tf_op jit(solution)/shard_map/pallas_call | solution.py:198
  81.7 10.5 %all_to_all.38 = bf16[2,8,4,32,512]{4,3,2,1,0:T(8,128)(2,1)S(1)} all-to-all(bf16[2,8,4,32,512]{4,3,2,1,0:T(8,128)(2,1)S(1)} %get-tuple-element.11), channel_id=1, replica_groups={{0,8},{16,24},{32,40},{48,56},{64,72},{80,88},{96,104},{112,120},{128,1..., dimensions={0} | all-to-all | bytes 4194304 | tf_op jit(solution)/shard_map/all_to_all | solution.py:31
  92.2 0.6 reduce_sum.33
  92.8 31.6 %all_to_all.39 = bf16[32,32,512]{2,1,0:T(8,128)(2,1)S(1)} all-to-all(bf16[32,32,512]{2,1,0:T(8,128)(2,1)S(1)} %bitcast.7), channel_id=1, replica_groups={{0,16,32,48,64,80,96,112,128,144,160,176,192,208,224,240,256,272,288,30..., dimensions={0} | all-to-all | bytes 2097152 | tf_op jit(solution)/shard_map/all_to_all | solution.py:31
  124.4 0.2 convert_reduce_fusion
  124.6 0.0 copy-start.3
  124.6 0.6 convert_element_type.5.query_ref
  125.2 0.0 all-gather.2.cloned.1.call-done.weight_ref
  125.2 4.6 %shard_map.123 = bf16[8,32,512]{2,1,0:T(8,128)(2,1)} custom-call(bf16[32,512]{1,0:T(8,128)(2,1)} %convert_element_type.5.query_ref, bf16[4096,512]{1,0:T(8,128)(2,1)} %all-gather.2.cloned.1.call-done.weight_ref), custom_call_target="tpu_custom_call" | custom-call | tf_op jit(solution)/shard_map/pallas_call | solution.py:239
  129.8 17.7 %all_to_all.40 = bf16[8,32,512]{2,1,0:T(8,128)(2,1)S(1)} all-to-all(bf16[8,32,512]{2,1,0:T(8,128)(2,1)} %shard_map.123), channel_id=1, replica_groups=mesh['psg'=64,'qry'=8] {'qry'}, dimensions={0} | all-to-all | bytes 524288 | tf_op jit(solution)/shard_map/all_to_all | solution.py:31
  147.6 0.0 copy-done.3
  147.6 12.9 %all_to_all.41 = bf16[8,32,512]{2,1,0:T(8,128)(2,1)S(1)} all-to-all(bf16[8,32,512]{2,1,0:T(8,128)(2,1)S(1)} %broadcast_in_dim.5), channel_id=1, replica_groups=mesh['psg'=64,'qry'=8] {'qry'}, dimensions={0} | all-to-all | bytes 524288 | tf_op jit(solution)/shard_map/all_to_all | solution.py:31
  160.6 0.8 copy.15
  (3 shorter events, 0.1 us)
Async XLA Ops:
  7.2 118.1 %all-gather.2.cloned.1.call-start = ((), (), s32[]{:S(2)}) async-start(), calls=%async_computation.7 | async-start | bytes 4259840 | tf_op jit(solution)/shard_map/all_gather | solution.py:255
  40.2 29.8 %copy-start.2 = (s32[8,16]{1,0:T(8,128)S(1)}, s32[8,16]{1,0:T(8,128)}, u32[]{:S(2)}) copy-start(s32[8,16]{1,0:T(8,128)} %attend_ref.1) | copy-start | bytes 1540
  71.5 6.3 %copy-start = (bf16[512,128]{1,0:T(8,128)(2,1)S(1)}, bf16[512,128]{1,0:T(8,128)(2,1)}, u32[]{:S(2)}) copy-start(bf16[512,128]{1,0:T(8,128)(2,1)} %key_ref.1) | copy-start | bytes 393220
  71.5 6.3 %copy-start.1 = (bf16[512,128]{1,0:T(8,128)(2,1)S(1)}, bf16[512,128]{1,0:T(8,128)(2,1)}, u32[]{:S(2)}) copy-start(bf16[512,128]{1,0:T(8,128)(2,1)} %value_ref.1) | copy-start | bytes 393220
  124.6 23.0 %copy-start.3 = (f32[32,512]{1,0:T(8,128)}, f32[32,512]{1,0:T(8,128)S(1)}, u32[]{:S(2)}) copy-start(f32[32,512]{1,0:T(8,128)S(1)} %convert_reduce_fusion) | copy-start | bytes 196612
Sparse Core Ops, SparseCore 0:
  11.4 88.6 all-gather.1

commit v5 on v3

v5 whole, which is shorter than its diff:
```python
import functools

import jax
import jax.numpy as jnp
from jax import lax
from jax.experimental import pallas as pl
from jax.experimental.pallas import tpu as pltpu
from jax.sharding import PartitionSpec as P

WIDTH = 128
GROUP = 4
ASK_LEN = 256
XS, ZS, CS = 4, 8, 2
LOG2E = 1.4426950408889634
FAR = 1.0e6
WIDE = 63 * 2**20


def index_of(x, z, c):
    return (x * ZS + z) * CS + c


Z_GROUPS = [[index_of(x, z, c) for z in range(ZS)] for x in range(XS) for c in range(CS)]
X_GROUPS = [[index_of(x, z, c) for x in range(XS)] for z in range(ZS) for c in range(CS)]
C_GROUPS = [[index_of(x, z, c) for c in range(CS)] for x in range(XS) for z in range(ZS)]

PLANE_GROUPS = [[index_of(x, z, c) for x in range(XS) for z in range(ZS)] for c in range(CS)]

CORE_SWAP = [(i, i ^ 1) for i in range(XS * ZS * CS)]
X_STEPS = [
    [(index_of(x, z, c), index_of((x + k) % XS, z, c)) for x in range(XS) for z in range(ZS) for c in range(CS)]
    for k in range(1, XS)
]


def z_step(k):
    return [
        (index_of(x, z, c), index_of(x, (z + k) % ZS, c)) for x in range(XS) for z in range(ZS) for c in range(CS)
    ]


def spread(blocks, axis, groups):
    return lax.all_to_all(blocks, axis, 0, 0, tiled=True, axis_index_groups=groups)


def pack_kernel(heads, qlen_ref, query_in, grad_in, output_in, lse_in, out_ref, query_ref, grad_ref, output_ref, lse_ref, sems):
    copies = [
        pltpu.make_async_copy(source, target, sems.at[k])
        for k, (source, target) in enumerate(
            ((grad_in, grad_ref), (output_in, output_ref), (lse_in, lse_ref), (query_in, query_ref))
        )
    ]
    for copy in copies:
        copy.start()
    rows, columns = query_ref.shape
    shape = (rows, WIDTH)
    owner = lax.axis_index("psg")
    per_question = ASK_LEN // rows
    question = lax.div(owner, per_question)
    first = (owner - question * per_question) * rows
    column = lax.broadcasted_iota(jnp.int32, shape, 1)
    row = lax.broadcasted_iota(jnp.int32, shape, 0)
    live = first + row < qlen_ref[question]
    square = lax.broadcasted_iota(jnp.int32, (rows, rows), 0) == lax.broadcasted_iota(jnp.int32, (rows, rows), 1)
    value = jnp.zeros(shape, jnp.float32)
    for copy in copies:
        copy.wait()
    for head in range(heads):
        part = slice(head * WIDTH, (head + 1) * WIDTH)
        products = grad_ref[:, part].astype(jnp.float32) * output_ref[:, part].astype(jnp.float32)
        delta = jnp.sum(products, axis=1, keepdims=True)
        spread_lse = jnp.broadcast_to(lse_ref[head : head + 1, :], (rows, rows))
        shift = jnp.sum(jnp.where(square, spread_lse, 0.0), axis=1, keepdims=True) * (WIDTH**0.5)
        shift = jnp.where(live, shift, FAR)
        value = jnp.where(column % heads == head, jnp.where(column < 3 * heads, shift, delta), value)
    high = value.astype(jnp.bfloat16).astype(jnp.float32)
    middle = (value - high).astype(jnp.bfloat16).astype(jnp.float32)
    low = value - high - middle
    piece = (column // heads) % 3
    side = jnp.where(piece == 0, high, jnp.where(piece == 1, middle, low))
    side = jnp.where(column < 6 * heads, side, 0.0).astype(jnp.bfloat16)
    for copy in range(out_ref.shape[0]):
        out_ref[copy, :, :columns] = query_ref[...]
        out_ref[copy, :, columns : 2 * columns] = grad_ref[...]
        out_ref[copy, :, 2 * columns :] = side


def pack_rows(queries, grad_out, attn_out, log_sum, qlen, copies):
    rows, columns = queries.shape
    heads = log_sum.shape[0]
    anywhere = pl.BlockSpec(memory_space=pl.ANY)
    return pl.pallas_call(
        functools.partial(pack_kernel, heads),
        in_specs=[pl.BlockSpec(memory_space=pltpu.SMEM)] + [anywhere] * 4,
        out_specs=pl.BlockSpec(memory_space=pltpu.VMEM),
        out_shape=jax.ShapeDtypeStruct((copies, rows, 2 * columns + WIDTH), jnp.bfloat16),
        scratch_shapes=[
            pltpu.VMEM((rows, columns), jnp.bfloat16),
            pltpu.VMEM((rows, columns), jnp.bfloat16),
            pltpu.VMEM((rows, columns), jnp.bfloat16),
            pltpu.VMEM((heads, rows), jnp.float32),
            pltpu.SemaphoreType.DMA((4,)),
        ],
        compiler_params=pltpu.CompilerParams(vmem_limit_bytes=WIDE),
    )(qlen, queries, grad_out, attn_out, log_sum)


def select_kernel(attend_ref, rows_ref, out_ref, plan_ref):
    questions, top = attend_ref.shape
    slots = out_ref.shape[1]
    owner = lax.axis_index("psg")
    core = lax.rem(owner, CS)
    for target in range(CS):
        block = owner - core + target
        count = jnp.int32(0)
        chosen = [jnp.int32(0)] * slots
        for question in range(questions):
            hit = jnp.int32(0)
            for place in range(top):
                hit = hit | (attend_ref[question, place] == block).astype(jnp.int32)
            chosen = [jnp.where((hit == 1) & (count == k), question, chosen[k]) for k in range(slots)]
            count = count + hit

            @pl.when(core == target)
            def _():
                plan_ref[0, question] = hit
                plan_ref[1, question] = jnp.clip(count - 1, 0, slots - 1)

        for slot in range(slots):
            out_ref[target, slot] = rows_ref[chosen[slot]]


def select(attend, rows, slots):
    return pl.pallas_call(
        select_kernel,
        in_specs=[pl.BlockSpec(memory_space=pltpu.SMEM), pl.BlockSpec(memory_space=pltpu.VMEM)],
        out_specs=[pl.BlockSpec(memory_space=pltpu.VMEM), pl.BlockSpec(memory_space=pltpu.SMEM)],
        out_shape=[
            jax.ShapeDtypeStruct((CS, slots, *rows.shape[1:]), rows.dtype),
            jax.ShapeDtypeStruct((2, attend.shape[0]), jnp.int32),
        ],
        compiler_params=pltpu.CompilerParams(vmem_limit_bytes=16 * 2**20),
    )(attend, rows)


def visit_kernel(heads, plan, rows_ref, key_ref, value_ref, out_q, out_k, out_v):
    scale = WIDTH**-0.5
    span = key_ref.shape[0]
    cores, questions, chunks, chunk, _ = out_q.shape
    out_k[...] = jnp.zeros_like(out_k)
    out_v[...] = jnp.zeros_like(out_v)
    key_t = key_ref[...].astype(jnp.float32).T.astype(jnp.bfloat16)
    columns = lax.broadcasted_iota(jnp.int32, (span, WIDTH), 1)

    @pl.loop(0, questions)
    def _(question):
        slot = plan[1, question]

        def take(start):
            return rows_ref[:, slot, :, :, start : start + WIDTH].reshape(ASK_LEN, WIDTH)

        @pl.when(plan[0, question] == 0)
        def _():
            out_q[:, question] = jnp.zeros((cores, chunks, chunk, heads * WIDTH), out_q.dtype)

        @pl.when(plan[0, question] != 0)
        def _():
            key = key_ref[...]
            value = value_ref[...]
            grad_k = jnp.zeros((span, WIDTH), jnp.float32)
            grad_v = jnp.zeros((span, WIDTH), jnp.float32)
            side = take(2 * heads * WIDTH)
            for head in range(heads):
                query = take(head * WIDTH)
                cotangent = take((heads + head) * WIDTH)
                for_shift = (columns < 3 * heads) & (columns % heads == head)
                for_delta = (columns >= 3 * heads) & (columns < 6 * heads) & (columns % heads == head)
                minus_s = jnp.where(for_shift, -1.0, 0.0).astype(jnp.bfloat16)
                minus_d = jnp.where(for_delta, -1.0, 0.0).astype(jnp.bfloat16)
                energy = lax.dot_general(
                    jnp.concatenate([key, minus_s], axis=1),
                    jnp.concatenate([query, side], axis=1),
                    (((1,), (1,)), ((), ())),
                    preferred_element_type=jnp.float32,
                )
                prob = jnp.exp2(energy * (scale * LOG2E))
                change = lax.dot_general(
                    jnp.concatenate([value, minus_d], axis=1),
                    jnp.concatenate([cotangent, side], axis=1),
                    (((1,), (1,)), ((), ())),
                    preferred_element_type=jnp.float32,
                )
                low_score = (prob * change).astype(jnp.bfloat16)
                low_prob = prob.astype(jnp.bfloat16)
                grad_k = grad_k + jnp.dot(low_score, query, preferred_element_type=jnp.float32)
                grad_v = grad_v + jnp.dot(low_prob, cotangent, preferred_element_type=jnp.float32)
                term = jnp.dot(key_t, low_score, preferred_element_type=jnp.float32).T * scale
                term = term.astype(jnp.bfloat16).reshape(cores, chunks, chunk, WIDTH)
                out_q[:, question, :, :, head * WIDTH : (head + 1) * WIDTH] = term
            out_k[...] += grad_k * scale
            out_v[...] += grad_v


def visits(plan, rows, keys, values, heads):
    cores, _, chunks, chunk, _ = rows.shape
    vmem = pl.BlockSpec(memory_space=pltpu.VMEM)
    return pl.pallas_call(
        functools.partial(visit_kernel, heads),
        in_specs=[pl.BlockSpec(memory_space=pltpu.SMEM), vmem, vmem, vmem],
        out_specs=[vmem, vmem, vmem],
        out_shape=[
            jax.ShapeDtypeStruct((cores, plan.shape[1], chunks, chunk, heads * WIDTH), jnp.bfloat16),
            jax.ShapeDtypeStruct(keys.shape, jnp.float32),
            jax.ShapeDtypeStruct(values.shape, jnp.float32),
        ],
        compiler_params=pltpu.CompilerParams(vmem_limit_bytes=32 * 2**20),
    )(plan, rows, keys, values)


def hidden_kernel(query_ref, own_ref, other_ref, out_ref):
    place = lax.axis_index("psg")
    core = lax.rem(place, CS)
    z = lax.rem(lax.div(place, CS), ZS)
    x = lax.div(place, CS * ZS)
    parts, _, wide = out_ref.shape
    depth = query_ref.shape[1]
    per_part = XS * ZS // parts

    def product(first_ref, second_ref):
        query = query_ref[...].astype(jnp.bfloat16)
        for part in range(parts):
            blocks = []
            for chip in range(part * per_part, (part + 1) * per_part):
                far_x = lax.rem(x - chip // ZS + XS, XS)
                off_z = lax.rem(chip % ZS - z + ZS, ZS)
                base = jnp.where(off_z < 2, XS - XS * off_z, (ZS + 1 - off_z) * XS)
                blocks += [first_ref[base + far_x], second_ref[base + far_x]]
            out_ref[part] = lax.dot_general(
                query,
                jnp.concatenate(blocks, axis=0).reshape(wide, depth),
                (((1,), (1,)), ((), ())),
                preferred_element_type=jnp.float32,
            ).astype(out_ref.dtype)

    @pl.when(core == 0)
    def _():
        product(own_ref, other_ref)

    @pl.when(core != 0)
    def _():
        product(other_ref, own_ref)


def hidden_parts(grad_query, own, other, parts):
    rows = grad_query.shape[0]
    wide = CS * own.shape[0] * own.shape[1] // parts
    vmem = pl.BlockSpec(memory_space=pltpu.VMEM)
    return pl.pallas_call(
        hidden_kernel,
        in_specs=[vmem, vmem, vmem],
        out_specs=vmem,
        out_shape=jax.ShapeDtypeStruct((parts, rows, wide), jnp.bfloat16),
        compiler_params=pltpu.CompilerParams(vmem_limit_bytes=16 * 2**20),
    )(grad_query, own, other)


def on_device(queries, grad_out, attn_out, log_sum, keys, values, proj_weight, attend, qlen):
    heads = log_sum.shape[0]
    rows, columns = queries.shape
    packed = pack_rows(queries, grad_out, attn_out, log_sum, qlen, ZS)
    packed, proj_weight = lax.optimization_barrier((packed, proj_weight))
    line = spread(packed, "psg", Z_GROUPS)
    near = jnp.stack([proj_weight] + [lax.ppermute(proj_weight, "psg", steps) for steps in X_STEPS])
    line, near = lax.optimization_barrier((line, near))
    gathered = spread(jnp.broadcast_to(line[None], (XS, *line.shape)), "psg", X_GROUPS)
    trio = jnp.concatenate(
        [lax.ppermute(near, "psg", z_step(-1)), near, lax.ppermute(near, "psg", z_step(1))], axis=0
    )
    share = 5 * XS // 2
    below = lax.ppermute(trio[:share], "psg", z_step(3))
    above = lax.ppermute(trio[-share:], "psg", z_step(-3))
    question_total, top = attend.shape
    gathered = gathered.reshape(question_total, -1, rows, packed.shape[2])
    slots = min(question_total, 2 * question_total * top // (XS * ZS * CS))
    chosen, plan = select(attend, gathered, slots)
    chosen = spread(chosen, "psg", C_GROUPS)

    terms, grad_keys, grad_values = visits(plan, chosen, keys, values, heads)

    terms = spread(terms, "psg", C_GROUPS)
    pair = jnp.sum(terms.astype(jnp.float32), axis=0).astype(jnp.bfloat16)
    _, trio, below, above = lax.optimization_barrier((pair, trio, below, above))
    plane = spread(pair.reshape(XS * ZS, rows, columns), "psg", PLANE_GROUPS)
    own_weight = jnp.concatenate([trio, below, above], axis=0)
    other_weight = lax.ppermute(own_weight, "psg", CORE_SWAP)
    grad_query = jnp.sum(plane.astype(jnp.float32), axis=0)

    parts = lax.axis_size("qry")
    terms = hidden_parts(grad_query, own_weight, other_weight, parts)
    terms = spread(terms, "qry", None)
    hidden = jnp.sum(terms.astype(jnp.float32), axis=0).astype(jnp.bfloat16)
    hidden = spread(jnp.broadcast_to(hidden[None], (parts, *hidden.shape)), "qry", None)
    grad_hidden = jnp.swapaxes(hidden.astype(jnp.float32), 0, 1).reshape(rows, -1)
    return (grad_query, grad_keys, grad_values, grad_hidden)


def solution(mesh):
    in_specs = (
        P("psg", "qry"),
        P("psg", "qry"),
        P("psg", "qry"),
        P("qry", "psg"),
        P("psg", "qry"),
        P("psg", "qry"),
        P("psg", "qry"),
        P(),
        P(),
    )
    out_specs = (P("psg", "qry"), P("psg", "qry"), P("psg", "qry"), P("psg", None))
    return jax.shard_map(
        on_device, mesh=mesh, in_specs=in_specs, out_specs=out_specs, check_vma=False
    )
```

time: 219 us -> 163 us (0.74)
  blocking collectives: 146 us -> 42.7 us
  starting transfers between devices: 1.95 us -> 48.7 us
  between operations: 14.1 us -> 0.84 us
  waiting for transfers between devices: 39.9 us -> 46.8 us
  local copies, waits for them, and re-layouts: 1.11 us -> 6.12 us
  other arithmetic: 1.51 us -> 4.08 us
  Pallas kernels: 14.3 us -> 12.1 us
    all_to_all x8 -> x4, blocking collectives: 146 us -> 42.7 us  [spread(): lax.all_to_all(blocks, axis, 0, 0, tiled=True, axis_index_groups=groups)]
    all_gather x1 -> x0, waiting for transfers between devices: 39.9 us -> none  [on_device(): lax.all_gather(proj_weight, 'psg', axis=0, axis_index_groups=CORE_GROUPS)]
    all_to_all x0 -> x3, waiting for transfers between devices: none -> 25.3 us  [spread(): lax.all_to_all(blocks, axis, 0, 0, tiled=True, axis_index_groups=groups)]
    ppermute x0 -> x7, starting transfers between devices: none -> 24.6 us  [the longest x3 9.76 us: on_device(): lax.ppermute(proj_weight, 'psg', steps)]
    all_to_all x0 -> x3, starting transfers between devices: none -> 22.2 us  [spread(): lax.all_to_all(blocks, axis, 0, 0, tiled=True, axis_index_groups=groups)]
    ppermute x0 -> x7, waiting for transfers between devices: none -> 21.5 us  [the longest x1 10 us: on_device(): below = lax.ppermute(trio[:share], 'psg', z_step(3))]
  transfers between devices with their start and end apart: 2 -> 11, of which waited for: 1 -> 9; matrix products, arithmetic and copies ran while one was open for 1% -> 5% of each run, Pallas kernels for 3% -> 4%
where the time goes in v5:
time: 163 us; the launch traced here: 161 us
  starting transfers between devices  48.7 us (30%)
  waiting for transfers between devices  46.8 us (29%)
  blocking collectives  42.7 us (26%)
  Pallas kernels  12.1 us (7%)
  local copies, waits for them, and re-layouts  6.12 us (4%)
  other arithmetic  4.08 us (3%)
    all_to_all x4, blocking collectives, spread(): lax.all_to_all(blocks, axis, 0, 0, tiled=True, axis_index_groups=groups)  42.7 us
    all_to_all x3, waiting for transfers between devices, spread(): lax.all_to_all(blocks, axis, 0, 0, tiled=True, axis_index_groups=groups)  25.3 us
    all_to_all x3, starting transfers between devices, spread(): lax.all_to_all(blocks, axis, 0, 0, tiled=True, axis_index_groups=groups)  22.2 us
    ppermute x1, waiting for transfers between devices, on_device(): below = lax.ppermute(trio[:share], 'psg', z_step(3))  10 us
    ppermute x3, starting transfers between devices, on_device(): lax.ppermute(proj_weight, 'psg', steps)  9.76 us
    ppermute x1, starting transfers between devices, on_device(): above = lax.ppermute(trio[-share:], 'psg', z_step(-3))  6.93 us
    pallas_call x1, Pallas kernels, visits(): pl.pallas_call(functools.partial(visit_kernel, heads), in_specs=[pl.Block...  5.2 us
    ppermute x1, starting transfers between devices, on_device(): lax.ppermute(near, 'psg', z_step(1))  3.92 us
  transfers between devices with their start and end apart: 11, of which 9 were waited for; matrix products, arithmetic and copies ran while one was open for 5% of the time, Pallas kernels for 4%

profile of v5, /device:TPU:6, one launch (start us, length us, event | category | flops | bytes accessed | tf_op | source)
XLA Modules:
  0.0 161.5 jit_solution(15760376439046723748)
XLA Ops:
  0.6 2.4 %shard_map.120 = bf16[8,32,1152]{2,1,0:T(8,128)(2,1)} custom-call(s32[8]{0:T(128)} %qlen_ref.1, bf16[32,512]{1,0:T(8,128)(2,1)} %query_in.1, bf16[32,512]{1,0:T(8,128)(2,1)} %grad_in.1, bf16[32,512]{1,0:T(8,128)(2,1)} %output_in.1, f32[4,32]{1,0:T(4,128)} %lse_in.1), custom_call_target="tpu_custom_call" | custom-call | tf_op jit(solution)/shard_map/pallas_call | solution.py:92
  3.1 10.3 %all-to-all-start = ((bf16[8,32,1152]{2,1,0:T(8,128)(2,1)}), bf16[8,32,1152]{2,1,0:T(8,128)(2,1)S(1)}, u32[]{:S(2)}, u32[]{:S(2)}) async-start(bf16[8,32,1152]{2,1,0:T(8,128)(2,1)} %shard_map.120), calls=%async_computation | async-start | bytes 1179648 | tf_op jit(solution)/shard_map/all_to_all | solution.py:43
  13.4 2.7 %collective-permute-start.2 = (bf16[64,512]{1,0:T(8,128)(2,1)}, bf16[64,512]{1,0:T(8,128)(2,1)S(1)}, u32[]{:S(2)}, u32[]{:S(2)}) collective-permute-start(bf16[64,512]{1,0:T(8,128)(2,1)} %param.15), channel_id=1, source_target_pairs={{0,384},{8,392},{16,400},{24,408},{32,416},{40,424},{48,432},{56,4... | collective-permute-start | bytes 196616 | tf_op jit(solution)/shard_map/ppermute | solution.py:273
  16.2 3.0 %collective-permute-start.1 = (bf16[64,512]{1,0:T(8,128)(2,1)}, bf16[64,512]{1,0:T(8,128)(2,1)S(1)}, u32[]{:S(2)}, u32[]{:S(2)}) collective-permute-start(bf16[64,512]{1,0:T(8,128)(2,1)} %param.15), channel_id=1, source_target_pairs={{0,256},{8,264},{16,272},{24,280},{32,288},{40,296},{48,304},{56,3... | collective-permute-start | bytes 196616 | tf_op jit(solution)/shard_map/ppermute | solution.py:273
  19.2 4.0 %collective-permute-start = (bf16[64,512]{1,0:T(8,128)(2,1)}, bf16[64,512]{1,0:T(8,128)(2,1)S(1)}, u32[]{:S(2)}, u32[]{:S(2)}) collective-permute-start(bf16[64,512]{1,0:T(8,128)(2,1)} %param.15), channel_id=1, source_target_pairs={{0,128},{8,136},{16,144},{24,152},{32,160},{40,168},{48,176},{56,1... | collective-permute-start | bytes 196616 | tf_op jit(solution)/shard_map/ppermute | solution.py:273
  23.2 0.0 collective-permute-done.2
  23.2 0.8 collective-permute-done.1
  24.0 1.7 %collective-permute-done = bf16[64,512]{1,0:T(8,128)(2,1)S(1)} collective-permute-done((bf16[64,512]{1,0:T(8,128)(2,1)}, bf16[64,512]{1,0:T(8,128)(2,1)S(1)}, u32[]{:S(2)}, u32[]{:S(2)}) %collective-permute-start) | collective-permute-done | bytes 65568 | tf_op jit(solution)/shard_map/ppermute | solution.py:273
  25.7 0.9 pad_maximum_fusion
  26.6 5.7 %all-to-all-done = bf16[8,32,1152]{2,1,0:T(8,128)(2,1)S(1)} async-done(((bf16[8,32,1152]{2,1,0:T(8,128)(2,1)}), bf16[8,32,1152]{2,1,0:T(8,128)(2,1)S(1)}, u32[]{:S(2)}, u32[]{:S(2)}) %all-to-all-start) | async-done | bytes 589856 | tf_op jit(solution)/shard_map/all_to_all | solution.py:43
  32.3 1.6 %broadcast_in_dim.4 = bf16[4,8,32,1152]{3,2,1,0:T(8,128)(2,1)} broadcast(bf16[8,32,1152]{2,1,0:T(8,128)(2,1)S(1)} %all-to-all-done), dimensions={1,2,3} | broadcast | bytes 2949120 | tf_op jit(solution)/shard_map/broadcast_in_dim | solution.py:275
  33.9 4.8 %all-to-all-start.1 = ((bf16[4,8,32,1152]{3,2,1,0:T(8,128)(2,1)}), bf16[4,8,32,1152]{3,2,1,0:T(8,128)(2,1)S(1)}, u32[]{:S(2)}, u32[]{:S(2)}) async-start(bf16[4,8,32,1152]{3,2,1,0:T(8,128)(2,1)} %broadcast_in_dim.4), calls=%async_computation.1 | async-start | bytes 4718592 | tf_op jit(solution)/shard_map/all_to_all | solution.py:43
  38.7 0.0 copy-start.3
  38.7 2.0 %collective-permute-start.3 = (bf16[4,64,512]{2,1,0:T(8,128)(2,1)S(1)}, bf16[4,64,512]{2,1,0:T(8,128)(2,1)S(1)}, u32[]{:S(2)}, u32[]{:S(2)}) collective-permute-start(bf16[4,64,512]{2,1,0:T(8,128)(2,1)S(1)} %pad_maximum_fusion), channel_id=1, source_target_pairs={{0,112},{8,120},{16,0},{24,8},{32,16},{40,24},{48,32},{56,40},{64,... | collective-permute-start | bytes 786440 | tf_op jit(solution)/shard_map/ppermute | solution.py:277
  40.8 3.9 %collective-permute-start.4 = (bf16[4,64,512]{2,1,0:T(8,128)(2,1)S(1)}, bf16[4,64,512]{2,1,0:T(8,128)(2,1)S(1)}, u32[]{:S(2)}, u32[]{:S(2)}) collective-permute-start(bf16[4,64,512]{2,1,0:T(8,128)(2,1)S(1)} %pad_maximum_fusion), channel_id=1, source_target_pairs={{0,16},{8,24},{16,32},{24,40},{32,48},{40,56},{48,64},{56,72},{64,... | collective-permute-start | bytes 786440 | tf_op jit(solution)/shard_map/ppermute | solution.py:277
  44.7 3.7 %collective-permute-done.3 = bf16[4,64,512]{2,1,0:T(8,128)(2,1)S(1)} collective-permute-done((bf16[4,64,512]{2,1,0:T(8,128)(2,1)S(1)}, bf16[4,64,512]{2,1,0:T(8,128)(2,1)S(1)}, u32[]{:S(2)}, u32[]{:S(2)}) %collective-permute-start.3) | collective-permute-done | bytes 262176 | tf_op jit(solution)/shard_map/ppermute | solution.py:277
  48.4 3.1 %collective-permute-done.4 = bf16[4,64,512]{2,1,0:T(8,128)(2,1)S(1)} collective-permute-done((bf16[4,64,512]{2,1,0:T(8,128)(2,1)S(1)}, bf16[4,64,512]{2,1,0:T(8,128)(2,1)S(1)}, u32[]{:S(2)}, u32[]{:S(2)}) %collective-permute-start.4) | collective-permute-done | bytes 262176 | tf_op jit(solution)/shard_map/ppermute | solution.py:277
  51.6 1.2 fusion
  52.8 1.9 %collective-permute-start.5 = (bf16[10,64,512]{2,1,0:T(8,128)(2,1)}, bf16[10,64,512]{2,1,0:T(8,128)(2,1)}, u32[]{:S(2)}, u32[]{:S(2)}) collective-permute-start(bf16[10,64,512]{2,1,0:T(8,128)(2,1)} %get-tuple-element.29), channel_id=1, source_target_pairs={{0,48},{8,56},{16,64},{24,72},{32,80},{40,88},{48,96},{56,104},{64... | collective-permute-start | bytes 1966088 | tf_op jit(solution)/shard_map/ppermute | solution.py:280
  54.7 6.9 %collective-permute-start.6 = (bf16[10,64,512]{2,1,0:T(8,128)(2,1)}, bf16[10,64,512]{2,1,0:T(8,128)(2,1)}, u32[]{:S(2)}, u32[]{:S(2)}) collective-permute-start(bf16[10,64,512]{2,1,0:T(8,128)(2,1)} %get-tuple-element.28), channel_id=1, source_target_pairs={{0,80},{8,88},{16,96},{24,104},{32,112},{40,120},{48,0},{56,8},{64... | collective-permute-start | bytes 1966088 | tf_op jit(solution)/shard_map/ppermute | solution.py:281
  61.6 4.3 %all-to-all-done.1 = bf16[4,8,32,1152]{3,2,1,0:T(8,128)(2,1)S(1)} async-done(((bf16[4,8,32,1152]{3,2,1,0:T(8,128)(2,1)}), bf16[4,8,32,1152]{3,2,1,0:T(8,128)(2,1)S(1)}, u32[]{:S(2)}, u32[]{:S(2)}) %all-to-all-start.1) | async-done | bytes 2359328 | tf_op jit(solution)/shard_map/all_to_all | solution.py:43
  66.0 0.0 copy-done.3
  66.0 1.6 shard_map.121
  67.5 0.0 copy-start.1
  67.6 0.0 copy-start.2
  67.6 5.8 %all_to_all.35.rows_ref = bf16[2,4,4,32,1152]{4,3,2,1,0:T(8,128)(2,1)S(1)} all-to-all(bf16[2,4,4,32,1152]{4,3,2,1,0:T(8,128)(2,1)S(1)} %get-tuple-element.20), channel_id=1, replica_groups={{0,8},{16,24},{32,40},{48,56},{64,72},{80,88},{96,104},{112,120},{128,1..., dimensions={0} | all-to-all | bytes 4718592 | tf_op jit(solution)/shard_map/all_to_all | solution.py:43
  73.3 0.0 copy-done.1
  73.3 0.0 copy-done.2
  73.3 5.2 %shard_map.122 = (bf16[2,8,4,32,512]{4,3,2,1,0:T(8,128)(2,1)S(1)}, f32[512,128]{1,0:T(8,128)}, f32[512,128]{1,0:T(8,128)}) custom-call(s32[2,8]{1,0:T(2,128)S(1)} %get-tuple-element.19.plan, bf16[2,4,4,32,1152]{4,3,2,1,0:T(8,128)(2,1)S(1)} %all_to_all.35.rows_ref, bf16[512,128]{1,0:T(8,128)(2,1)S(1)} %copy-done.1, bf16[512,128]{1,0:T(8,128)(2,1)S(1)} %copy-done.2), custom_call_target="tpu_custom_call" | custom-call | tf_op jit(solution)/shard_map/pallas_call | solution.py:207
  78.5 5.4 %all_to_all.36 = bf16[2,8,4,32,512]{4,3,2,1,0:T(8,128)(2,1)S(1)} all-to-all(bf16[2,8,4,32,512]{4,3,2,1,0:T(8,128)(2,1)S(1)} %get-tuple-element.21), channel_id=1, replica_groups={{0,8},{16,24},{32,40},{48,56},{64,72},{80,88},{96,104},{112,120},{128,1..., dimensions={0} | all-to-all | bytes 4194304 | tf_op jit(solution)/shard_map/all_to_all | solution.py:43
  83.9 1.7 %reduce_sum.33 = bf16[8,4,32,512]{3,2,1,0:T(8,128)(2,1)} reduce(bf16[2,8,4,32,512]{4,3,2,1,0:T(8,128)(2,1)S(1)} %all_to_all.36, bf16[]{:T(256)} %constant.3.clone.1), dimensions={0}, to_apply=%region_0.0 | reduce | flops 524288 | bytes 3145730 | tf_op jit(solution)/shard_map/reduce_sum | solution.py:291
  85.7 7.1 %all-to-all-start.4 = ((bf16[32,32,512]{2,1,0:T(8,128)(2,1)}), bf16[32,32,512]{2,1,0:T(8,128)(2,1)}, u32[]{:S(2)}, u32[]{:S(2)}) async-start(bf16[32,32,512]{2,1,0:T(8,128)(2,1)} %bitcast.11), calls=%async_computation.4 | async-start | bytes 2097152 | tf_op jit(solution)/shard_map/all_to_all | solution.py:43
  92.8 10.0 %collective-permute-done.5 = bf16[10,64,512]{2,1,0:T(8,128)(2,1)} collective-permute-done((bf16[10,64,512]{2,1,0:T(8,128)(2,1)}, bf16[10,64,512]{2,1,0:T(8,128)(2,1)}, u32[]{:S(2)}, u32[]{:S(2)}) %collective-permute-start.5) | collective-permute-done | bytes 655392 | tf_op jit(solution)/shard_map/ppermute | solution.py:280
  102.8 2.2 %collective-permute-done.6 = bf16[10,64,512]{2,1,0:T(8,128)(2,1)} collective-permute-done((bf16[10,64,512]{2,1,0:T(8,128)(2,1)}, bf16[10,64,512]{2,1,0:T(8,128)(2,1)}, u32[]{:S(2)}, u32[]{:S(2)}) %collective-permute-start.6) | collective-permute-done | bytes 655392 | tf_op jit(solution)/shard_map/ppermute | solution.py:281
  105.0 0.1 constant_dynamic-update-slice_fusion.5
  105.1 1.1 constant_dynamic-update-slice_fusion.4
  106.2 1.1 constant_dynamic-update-slice_fusion.3.own_ref
  107.4 1.9 %collective-permute-start.7 = (bf16[32,64,512]{2,1,0:T(8,128)(2,1)S(1)}, bf16[32,64,512]{2,1,0:T(8,128)(2,1)}, u32[]{:S(2)}, u32[]{:S(2)}) collective-permute-start(bf16[32,64,512]{2,1,0:T(8,128)(2,1)S(1)} %constant_dynamic-update-slice_fusion.3.own_ref), channel_id=1, source_target_pairs={{0,8},{8,0},{16,24},{24,16},{32,40},{40,32},{48,56},{56,48},{64,72... | collective-permute-start | bytes 6291464 | tf_op jit(solution)/shard_map/ppermute | solution.py:295
  109.3 15.3 %all-to-all-done.4 = bf16[32,32,512]{2,1,0:T(8,128)(2,1)} async-done(((bf16[32,32,512]{2,1,0:T(8,128)(2,1)}), bf16[32,32,512]{2,1,0:T(8,128)(2,1)}, u32[]{:S(2)}, u32[]{:S(2)}) %all-to-all-start.4) | async-done | bytes 1048608 | tf_op jit(solution)/shard_map/all_to_all | solution.py:43
  124.6 1.4 convert_reduce_fusion.query_ref
  126.0 0.0 copy-start
  126.0 0.0 collective-permute-done.7.other_ref
  126.0 2.9 %shard_map.123 = bf16[8,32,512]{2,1,0:T(8,128)(2,1)S(1)} custom-call(f32[32,512]{1,0:T(8,128)S(1)} %convert_reduce_fusion.query_ref, bf16[32,64,512]{2,1,0:T(8,128)(2,1)S(1)} %constant_dynamic-update-slice_fusion.3.own_ref, bf16[32,64,512]{2,1,0:T(8,128)(2,1)} %collective-permute-done.7.other_ref), custom_call_target="tpu_custom_call" | custom-call | tf_op jit(solution)/shard_map/pallas_call | solution.py:258
  128.9 0.0 copy-done
  128.9 18.7 %all_to_all.37 = bf16[8,32,512]{2,1,0:T(8,128)(2,1)S(1)} all-to-all(bf16[8,32,512]{2,1,0:T(8,128)(2,1)S(1)} %shard_map.123), channel_id=1, replica_groups=mesh['psg'=64,'qry'=8] {'qry'}, dimensions={0} | all-to-all | bytes 524288 | tf_op jit(solution)/shard_map/all_to_all | solution.py:43
  147.7 12.9 %all_to_all.38 = bf16[8,32,512]{2,1,0:T(8,128)(2,1)S(1)} all-to-all(bf16[8,32,512]{2,1,0:T(8,128)(2,1)S(1)} %broadcast_in_dim.5), channel_id=1, replica_groups=mesh['psg'=64,'qry'=8] {'qry'}, dimensions={0} | all-to-all | bytes 524288 | tf_op jit(solution)/shard_map/all_to_all | solution.py:43
  160.6 0.8 copy.15
  (6 shorter events, 0.2 us)
Async XLA Ops:
  3.1 29.2 %all-to-all-start = ((bf16[8,32,1152]{2,1,0:T(8,128)(2,1)}), bf16[8,32,1152]{2,1,0:T(8,128)(2,1)S(1)}, u32[]{:S(2)}, u32[]{:S(2)}) async-start(bf16[8,32,1152]{2,1,0:T(8,128)(2,1)} %shard_map.120), calls=%async_computation | async-start | bytes 1179648 | tf_op jit(solution)/shard_map/all_to_all | solution.py:43
  13.4 9.8 %collective-permute-start.2 = (bf16[64,512]{1,0:T(8,128)(2,1)}, bf16[64,512]{1,0:T(8,128)(2,1)S(1)}, u32[]{:S(2)}, u32[]{:S(2)}) collective-permute-start(bf16[64,512]{1,0:T(8,128)(2,1)} %param.15), channel_id=1, source_target_pairs={{0,384},{8,392},{16,400},{24,408},{32,416},{40,424},{48,432},{56,4... | collective-permute-start | bytes 196616 | tf_op jit(solution)/shard_map/ppermute | solution.py:273
  16.2 7.9 %collective-permute-start.1 = (bf16[64,512]{1,0:T(8,128)(2,1)}, bf16[64,512]{1,0:T(8,128)(2,1)S(1)}, u32[]{:S(2)}, u32[]{:S(2)}) collective-permute-start(bf16[64,512]{1,0:T(8,128)(2,1)} %param.15), channel_id=1, source_target_pairs={{0,256},{8,264},{16,272},{24,280},{32,288},{40,296},{48,304},{56,3... | collective-permute-start | bytes 196616 | tf_op jit(solution)/shard_map/ppermute | solution.py:273
  19.2 6.5 %collective-permute-start = (bf16[64,512]{1,0:T(8,128)(2,1)}, bf16[64,512]{1,0:T(8,128)(2,1)S(1)}, u32[]{:S(2)}, u32[]{:S(2)}) collective-permute-start(bf16[64,512]{1,0:T(8,128)(2,1)} %param.15), channel_id=1, source_target_pairs={{0,128},{8,136},{16,144},{24,152},{32,160},{40,168},{48,176},{56,1... | collective-permute-start | bytes 196616 | tf_op jit(solution)/shard_map/ppermute | solution.py:273
  33.9 32.0 %all-to-all-start.1 = ((bf16[4,8,32,1152]{3,2,1,0:T(8,128)(2,1)}), bf16[4,8,32,1152]{3,2,1,0:T(8,128)(2,1)S(1)}, u32[]{:S(2)}, u32[]{:S(2)}) async-start(bf16[4,8,32,1152]{3,2,1,0:T(8,128)(2,1)} %broadcast_in_dim.4), calls=%async_computation.1 | async-start | bytes 4718592 | tf_op jit(solution)/shard_map/all_to_all | solution.py:43
  38.7 27.3 %copy-start.3 = (s32[8,16]{1,0:T(8,128)S(1)}, s32[8,16]{1,0:T(8,128)}, u32[]{:S(2)}) copy-start(s32[8,16]{1,0:T(8,128)} %attend_ref.1) | copy-start | bytes 1540
  38.7 9.7 %collective-permute-start.3 = (bf16[4,64,512]{2,1,0:T(8,128)(2,1)S(1)}, bf16[4,64,512]{2,1,0:T(8,128)(2,1)S(1)}, u32[]{:S(2)}, u32[]{:S(2)}) collective-permute-start(bf16[4,64,512]{2,1,0:T(8,128)(2,1)S(1)} %pad_maximum_fusion), channel_id=1, source_target_pairs={{0,112},{8,120},{16,0},{24,8},{32,16},{40,24},{48,32},{56,40},{64,... | collective-permute-start | bytes 786440 | tf_op jit(solution)/shard_map/ppermute | solution.py:277
  40.8 10.8 %collective-permute-start.4 = (bf16[4,64,512]{2,1,0:T(8,128)(2,1)S(1)}, bf16[4,64,512]{2,1,0:T(8,128)(2,1)S(1)}, u32[]{:S(2)}, u32[]{:S(2)}) collective-permute-start(bf16[4,64,512]{2,1,0:T(8,128)(2,1)S(1)} %pad_maximum_fusion), channel_id=1, source_target_pairs={{0,16},{8,24},{16,32},{24,40},{32,48},{40,56},{48,64},{56,72},{64,... | collective-permute-start | bytes 786440 | tf_op jit(solution)/shard_map/ppermute | solution.py:277
  52.8 50.0 %collective-permute-start.5 = (bf16[10,64,512]{2,1,0:T(8,128)(2,1)}, bf16[10,64,512]{2,1,0:T(8,128)(2,1)}, u32[]{:S(2)}, u32[]{:S(2)}) collective-permute-start(bf16[10,64,512]{2,1,0:T(8,128)(2,1)} %get-tuple-element.29), channel_id=1, source_target_pairs={{0,48},{8,56},{16,64},{24,72},{32,80},{40,88},{48,96},{56,104},{64... | collective-permute-start | bytes 1966088 | tf_op jit(solution)/shard_map/ppermute | solution.py:280
  54.7 50.3 %collective-permute-start.6 = (bf16[10,64,512]{2,1,0:T(8,128)(2,1)}, bf16[10,64,512]{2,1,0:T(8,128)(2,1)}, u32[]{:S(2)}, u32[]{:S(2)}) collective-permute-start(bf16[10,64,512]{2,1,0:T(8,128)(2,1)} %get-tuple-element.28), channel_id=1, source_target_pairs={{0,80},{8,88},{16,96},{24,104},{32,112},{40,120},{48,0},{56,8},{64... | collective-permute-start | bytes 1966088 | tf_op jit(solution)/shard_map/ppermute | solution.py:281
  67.5 5.8 %copy-start.1 = (bf16[512,128]{1,0:T(8,128)(2,1)S(1)}, bf16[512,128]{1,0:T(8,128)(2,1)}, u32[]{:S(2)}) copy-start(bf16[512,128]{1,0:T(8,128)(2,1)} %key_ref.1) | copy-start | bytes 393220
  67.6 5.8 %copy-start.2 = (bf16[512,128]{1,0:T(8,128)(2,1)S(1)}, bf16[512,128]{1,0:T(8,128)(2,1)}, u32[]{:S(2)}) copy-start(bf16[512,128]{1,0:T(8,128)(2,1)} %value_ref.1) | copy-start | bytes 393220
  85.7 38.9 %all-to-all-start.4 = ((bf16[32,32,512]{2,1,0:T(8,128)(2,1)}), bf16[32,32,512]{2,1,0:T(8,128)(2,1)}, u32[]{:S(2)}, u32[]{:S(2)}) async-start(bf16[32,32,512]{2,1,0:T(8,128)(2,1)} %bitcast.11), calls=%async_computation.4 | async-start | bytes 2097152 | tf_op jit(solution)/shard_map/all_to_all | solution.py:43
  107.4 18.6 %collective-permute-start.7 = (bf16[32,64,512]{2,1,0:T(8,128)(2,1)S(1)}, bf16[32,64,512]{2,1,0:T(8,128)(2,1)}, u32[]{:S(2)}, u32[]{:S(2)}) collective-permute-start(bf16[32,64,512]{2,1,0:T(8,128)(2,1)S(1)} %constant_dynamic-update-slice_fusion.3.own_ref), channel_id=1, source_target_pairs={{0,8},{8,0},{16,24},{24,16},{32,40},{40,32},{48,56},{56,48},{64,72... | collective-permute-start | bytes 6291464 | tf_op jit(solution)/shard_map/ppermute | solution.py:295
  126.0 2.9 %copy-start = (f32[32,512]{1,0:T(8,128)}, f32[32,512]{1,0:T(8,128)S(1)}, u32[]{:S(2)}) copy-start(f32[32,512]{1,0:T(8,128)S(1)} %convert_reduce_fusion.query_ref) | copy-start | bytes 196612

commit v6 on v5

--- a/solution.py
+++ b/solution.py
@@ -233,7 +233,7 @@
             for chip in range(part * per_part, (part + 1) * per_part):
                 far_x = lax.rem(x - chip // ZS + XS, XS)
                 off_z = lax.rem(chip % ZS - z + ZS, ZS)
-                base = jnp.where(off_z < 2, XS - XS * off_z, (ZS + 1 - off_z) * XS)
+                base = (lax.div(off_z, 2) + lax.rem(off_z, 2) * (ZS // 2)) * XS
                 blocks += [first_ref[base + far_x], second_ref[base + far_x]]
             out_ref[part] = lax.dot_general(
                 query,
@@ -273,12 +273,12 @@
     near = jnp.stack([proj_weight] + [lax.ppermute(proj_weight, "psg", steps) for steps in X_STEPS])
     line, near = lax.optimization_barrier((line, near))
     gathered = spread(jnp.broadcast_to(line[None], (XS, *line.shape)), "psg", X_GROUPS)
-    trio = jnp.concatenate(
-        [lax.ppermute(near, "psg", z_step(-1)), near, lax.ppermute(near, "psg", z_step(1))], axis=0
-    )
-    share = 5 * XS // 2
-    below = lax.ppermute(trio[:share], "psg", z_step(3))
-    above = lax.ppermute(trio[-share:], "psg", z_step(-3))
+    plus = lax.ppermute(near, "psg", z_step(-2))
+    minus = lax.ppermute(near, "psg", z_step(2))
+    far = lax.ppermute(near, "psg", z_step(4))
+    above = lax.ppermute(jnp.concatenate([near, plus], axis=0), "psg", z_step(-1))
+    below = lax.ppermute(jnp.concatenate([minus, near], axis=0), "psg", z_step(1))
+    stripes = (near, plus, far, minus, above, below)
     question_total, top = attend.shape
     gathered = gathered.reshape(question_total, -1, rows, packed.shape[2])
     slots = min(question_total, 2 * question_total * top // (XS * ZS * CS))
@@ -289,9 +289,9 @@
 
     terms = spread(terms, "psg", C_GROUPS)
     pair = jnp.sum(terms.astype(jnp.float32), axis=0).astype(jnp.bfloat16)
-    _, trio, below, above = lax.optimization_barrier((pair, trio, below, above))
+    _, *stripes = lax.optimization_barrier((pair, *stripes))
     plane = spread(pair.reshape(XS * ZS, rows, columns), "psg", PLANE_GROUPS)
-    own_weight = jnp.concatenate([trio, below, above], axis=0)
+    own_weight = jnp.concatenate(stripes, axis=0)
     other_weight = lax.ppermute(own_weight, "psg", CORE_SWAP)
     grad_query = jnp.sum(plane.astype(jnp.float32), axis=0)
 

time: 163 us -> 161 us (0.988)
  waiting for transfers between devices: 46.8 us -> 38.6 us
  starting transfers between devices: 48.7 us -> 53.5 us
  local copies, waits for them, and re-layouts: 6.12 us -> 8.3 us
    ppermute x4 -> x5, waiting for transfers between devices: 19 us -> 11.5 us  [the longest x1 7.4 us: on_device(): plus = lax.ppermute(near, 'psg', z_step(-2))]
    all_to_all x3, starting transfers between devices: 22.2 us -> 25.7 us  [spread(): lax.all_to_all(blocks, axis, 0, 0, tiled=True, axis_index_groups=groups)]
    unnamed x12 -> x19, local copies, waits for them, and re-layouts: 1.25 us -> 4.71 us
    ppermute x4 -> x5, starting transfers between devices: 14.8 us -> 16.1 us  [the longest x1 4.43 us: on_device(): minus = lax.ppermute(near, 'psg', z_step(2))]
  transfers between devices with their start and end apart: 11 -> 12, of which waited for: 9 -> 6; matrix products, arithmetic and copies ran while one was open for 5% -> 5% of each run, Pallas kernels for 4% -> 4%
where the time goes in v6:
time: 161 us; the launch traced here: 159 us
  starting transfers between devices  53.5 us (33%)
  blocking collectives  41.4 us (26%)
  waiting for transfers between devices  38.6 us (24%)
  Pallas kernels  12.1 us (8%)
  local copies, waits for them, and re-layouts  8.3 us (5%)
  other arithmetic  3.71 us (2%)
    all_to_all x4, blocking collectives, spread(): lax.all_to_all(blocks, axis, 0, 0, tiled=True, axis_index_groups=groups)  41.4 us
    all_to_all x3, starting transfers between devices, spread(): lax.all_to_all(blocks, axis, 0, 0, tiled=True, axis_index_groups=groups)  25.7 us
    all_to_all x3, waiting for transfers between devices, spread(): lax.all_to_all(blocks, axis, 0, 0, tiled=True, axis_index_groups=groups)  24.6 us
    ppermute x3, starting transfers between devices, on_device(): lax.ppermute(proj_weight, 'psg', steps)  9.76 us
    ppermute x1, waiting for transfers between devices, on_device(): plus = lax.ppermute(near, 'psg', z_step(-2))  7.4 us
    pallas_call x1, Pallas kernels, visits(): pl.pallas_call(functools.partial(visit_kernel, heads), in_specs=[pl.Block...  5.22 us
    unnamed x19, local copies, waits for them, and re-layouts  4.71 us
    ppermute x1, starting transfers between devices, on_device(): minus = lax.ppermute(near, 'psg', z_step(2))  4.43 us
  transfers between devices with their start and end apart: 12, of which 6 were waited for; matrix products, arithmetic and copies ran while one was open for 5% of the time, Pallas kernels for 4%

profile of v6, /device:TPU:6, one launch (start us, length us, event | category | flops | bytes accessed | tf_op | source)
XLA Modules:
  0.0 158.6 jit_solution(13040202073347509983)
XLA Ops:
  0.6 2.4 %shard_map.120 = bf16[8,32,1152]{2,1,0:T(8,128)(2,1)} custom-call(s32[8]{0:T(128)} %qlen_ref.1, bf16[32,512]{1,0:T(8,128)(2,1)} %query_in.1, bf16[32,512]{1,0:T(8,128)(2,1)} %grad_in.1, bf16[32,512]{1,0:T(8,128)(2,1)} %output_in.1, f32[4,32]{1,0:T(4,128)} %lse_in.1), custom_call_target="tpu_custom_call" | custom-call | tf_op jit(solution)/shard_map/pallas_call | solution.py:92
  3.1 10.3 %all-to-all-start = ((bf16[8,32,1152]{2,1,0:T(8,128)(2,1)}), bf16[8,32,1152]{2,1,0:T(8,128)(2,1)S(1)}, u32[]{:S(2)}, u32[]{:S(2)}) async-start(bf16[8,32,1152]{2,1,0:T(8,128)(2,1)} %shard_map.120), calls=%async_computation | async-start | bytes 1179648 | tf_op jit(solution)/shard_map/all_to_all | solution.py:43
  13.4 2.7 %collective-permute-start.2 = (bf16[64,512]{1,0:T(8,128)(2,1)}, bf16[64,512]{1,0:T(8,128)(2,1)S(1)}, u32[]{:S(2)}, u32[]{:S(2)}) collective-permute-start(bf16[64,512]{1,0:T(8,128)(2,1)} %param.15), channel_id=1, source_target_pairs={{0,384},{8,392},{16,400},{24,408},{32,416},{40,424},{48,432},{56,4... | collective-permute-start | bytes 196616 | tf_op jit(solution)/shard_map/ppermute | solution.py:273
  16.1 3.0 %collective-permute-start.1 = (bf16[64,512]{1,0:T(8,128)(2,1)}, bf16[64,512]{1,0:T(8,128)(2,1)S(1)}, u32[]{:S(2)}, u32[]{:S(2)}) collective-permute-start(bf16[64,512]{1,0:T(8,128)(2,1)} %param.15), channel_id=1, source_target_pairs={{0,256},{8,264},{16,272},{24,280},{32,288},{40,296},{48,304},{56,3... | collective-permute-start | bytes 196616 | tf_op jit(solution)/shard_map/ppermute | solution.py:273
  19.2 4.0 %collective-permute-start = (bf16[64,512]{1,0:T(8,128)(2,1)}, bf16[64,512]{1,0:T(8,128)(2,1)S(1)}, u32[]{:S(2)}, u32[]{:S(2)}) collective-permute-start(bf16[64,512]{1,0:T(8,128)(2,1)} %param.15), channel_id=1, source_target_pairs={{0,128},{8,136},{16,144},{24,152},{32,160},{40,168},{48,176},{56,1... | collective-permute-start | bytes 196616 | tf_op jit(solution)/shard_map/ppermute | solution.py:273
  23.2 0.0 collective-permute-done.2
  23.2 0.8 collective-permute-done.1
  24.0 1.7 %collective-permute-done = bf16[64,512]{1,0:T(8,128)(2,1)S(1)} collective-permute-done((bf16[64,512]{1,0:T(8,128)(2,1)}, bf16[64,512]{1,0:T(8,128)(2,1)S(1)}, u32[]{:S(2)}, u32[]{:S(2)}) %collective-permute-start) | collective-permute-done | bytes 65568 | tf_op jit(solution)/shard_map/ppermute | solution.py:273
  25.7 0.9 pad_maximum_fusion.2
  26.6 5.7 %all-to-all-done = bf16[8,32,1152]{2,1,0:T(8,128)(2,1)S(1)} async-done(((bf16[8,32,1152]{2,1,0:T(8,128)(2,1)}), bf16[8,32,1152]{2,1,0:T(8,128)(2,1)S(1)}, u32[]{:S(2)}, u32[]{:S(2)}) %all-to-all-start) | async-done | bytes 589856 | tf_op jit(solution)/shard_map/all_to_all | solution.py:43
  32.3 1.6 %broadcast_in_dim.4 = bf16[4,8,32,1152]{3,2,1,0:T(8,128)(2,1)} broadcast(bf16[8,32,1152]{2,1,0:T(8,128)(2,1)S(1)} %all-to-all-done), dimensions={1,2,3} | broadcast | bytes 2949120 | tf_op jit(solution)/shard_map/broadcast_in_dim | solution.py:275
  34.0 0.0 copy-start.3
  34.0 4.9 %all-to-all-start.1 = ((bf16[4,8,32,1152]{3,2,1,0:T(8,128)(2,1)}), bf16[4,8,32,1152]{3,2,1,0:T(8,128)(2,1)S(1)}, u32[]{:S(2)}, u32[]{:S(2)}) async-start(bf16[4,8,32,1152]{3,2,1,0:T(8,128)(2,1)} %broadcast_in_dim.4), calls=%async_computation.1 | async-start | bytes 4718592 | tf_op jit(solution)/shard_map/all_to_all | solution.py:43
  38.9 2.3 %collective-permute-start.3 = (bf16[4,64,512]{2,1,0:T(8,128)(2,1)S(1)}, bf16[4,64,512]{2,1,0:T(8,128)(2,1)S(1)}, u32[]{:S(2)}, u32[]{:S(2)}) collective-permute-start(bf16[4,64,512]{2,1,0:T(8,128)(2,1)S(1)} %pad_maximum_fusion.2), channel_id=1, source_target_pairs={{0,96},{8,104},{16,112},{24,120},{32,0},{40,8},{48,16},{56,24},{64... | collective-permute-start | bytes 786440 | tf_op jit(solution)/shard_map/ppermute | solution.py:276
  41.2 4.4 %collective-permute-start.5 = (bf16[4,64,512]{2,1,0:T(8,128)(2,1)S(1)}, bf16[4,64,512]{2,1,0:T(8,128)(2,1)S(1)}, u32[]{:S(2)}, u32[]{:S(2)}) collective-permute-start(bf16[4,64,512]{2,1,0:T(8,128)(2,1)S(1)} %pad_maximum_fusion.2), channel_id=1, source_target_pairs={{0,32},{8,40},{16,48},{24,56},{32,64},{40,72},{48,80},{56,88},{64,... | collective-permute-start | bytes 786440 | tf_op jit(solution)/shard_map/ppermute | solution.py:277
  45.6 7.4 %collective-permute-done.3 = bf16[4,64,512]{2,1,0:T(8,128)(2,1)S(1)} collective-permute-done((bf16[4,64,512]{2,1,0:T(8,128)(2,1)S(1)}, bf16[4,64,512]{2,1,0:T(8,128)(2,1)S(1)}, u32[]{:S(2)}, u32[]{:S(2)}) %collective-permute-start.3) | collective-permute-done | bytes 262176 | tf_op jit(solution)/shard_map/ppermute | solution.py:276
  53.0 0.0 copy-start.5
  53.0 4.1 %collective-permute-done.5 = bf16[4,64,512]{2,1,0:T(8,128)(2,1)S(1)} collective-permute-done((bf16[4,64,512]{2,1,0:T(8,128)(2,1)S(1)}, bf16[4,64,512]{2,1,0:T(8,128)(2,1)S(1)}, u32[]{:S(2)}, u32[]{:S(2)}) %collective-permute-start.5) | collective-permute-done | bytes 262176 | tf_op jit(solution)/shard_map/ppermute | solution.py:277
  57.1 0.0 copy-start.4
  57.1 0.9 pad_maximum_fusion.1
  58.0 1.9 %collective-permute-start.6 = (bf16[8,64,512]{2,1,0:T(8,128)(2,1)}, bf16[8,64,512]{2,1,0:T(8,128)(2,1)}, u32[]{:S(2)}, u32[]{:S(2)}) collective-permute-start(bf16[8,64,512]{2,1,0:T(8,128)(2,1)} %get-tuple-element.35), channel_id=1, source_target_pairs={{0,112},{8,120},{16,0},{24,8},{32,16},{40,24},{48,32},{56,40},{64,... | collective-permute-start | bytes 1572872 | tf_op jit(solution)/shard_map/ppermute | solution.py:279
  59.9 3.9 %collective-permute-start.7 = (bf16[8,64,512]{2,1,0:T(8,128)(2,1)S(1)}, bf16[8,64,512]{2,1,0:T(8,128)(2,1)}, u32[]{:S(2)}, u32[]{:S(2)}) collective-permute-start(bf16[8,64,512]{2,1,0:T(8,128)(2,1)S(1)} %get-tuple-element.34), channel_id=1, source_target_pairs={{0,16},{8,24},{16,32},{24,40},{32,48},{40,56},{48,64},{56,72},{64,... | collective-permute-start | bytes 1572872 | tf_op jit(solution)/shard_map/ppermute | solution.py:280
  63.8 0.0 copy-done.5
  63.9 0.0 copy-done.4
  63.9 3.6 %collective-permute-start.4 = (bf16[4,64,512]{2,1,0:T(8,128)(2,1)S(1)}, bf16[4,64,512]{2,1,0:T(8,128)(2,1)S(1)}, u32[]{:S(2)}, u32[]{:S(2)}) collective-permute-start(bf16[4,64,512]{2,1,0:T(8,128)(2,1)S(1)} %pad_maximum_fusion.2), channel_id=1, source_target_pairs={{0,64},{8,72},{16,80},{24,88},{32,96},{40,104},{48,112},{56,120},{... | collective-permute-start | bytes 786440 | tf_op jit(solution)/shard_map/ppermute | solution.py:278
  67.4 0.0 all-to-all-done.1
  67.4 0.0 copy-done.3
  67.5 1.6 shard_map.121
  69.0 0.0 copy-start.1
  69.0 0.0 copy-start.2
  69.1 5.8 %all_to_all.35.rows_ref = bf16[2,4,4,32,1152]{4,3,2,1,0:T(8,128)(2,1)S(1)} all-to-all(bf16[2,4,4,32,1152]{4,3,2,1,0:T(8,128)(2,1)S(1)} %get-tuple-element.23), channel_id=1, replica_groups={{0,8},{16,24},{32,40},{48,56},{64,72},{80,88},{96,104},{112,120},{128,1..., dimensions={0} | all-to-all | bytes 4718592 | tf_op jit(solution)/shard_map/all_to_all | solution.py:43
  74.8 0.0 copy-done.1
  74.8 0.0 copy-done.2
  74.8 5.2 %shard_map.122 = (bf16[2,8,4,32,512]{4,3,2,1,0:T(8,128)(2,1)S(1)}, f32[512,128]{1,0:T(8,128)}, f32[512,128]{1,0:T(8,128)}) custom-call(s32[2,8]{1,0:T(2,128)S(1)} %get-tuple-element.22.plan, bf16[2,4,4,32,1152]{4,3,2,1,0:T(8,128)(2,1)S(1)} %all_to_all.35.rows_ref, bf16[512,128]{1,0:T(8,128)(2,1)S(1)} %copy-done.1, bf16[512,128]{1,0:T(8,128)(2,1)S(1)} %copy-done.2), custom_call_target="tpu_custom_call" | custom-call | tf_op jit(solution)/shard_map/pallas_call | solution.py:207
  80.0 5.4 %all_to_all.36 = bf16[2,8,4,32,512]{4,3,2,1,0:T(8,128)(2,1)S(1)} all-to-all(bf16[2,8,4,32,512]{4,3,2,1,0:T(8,128)(2,1)S(1)} %get-tuple-element.24), channel_id=1, replica_groups={{0,8},{16,24},{32,40},{48,56},{64,72},{80,88},{96,104},{112,120},{128,1..., dimensions={0} | all-to-all | bytes 4194304 | tf_op jit(solution)/shard_map/all_to_all | solution.py:43
  85.5 1.7 %reduce_sum.33 = bf16[8,4,32,512]{3,2,1,0:T(8,128)(2,1)} reduce(bf16[2,8,4,32,512]{4,3,2,1,0:T(8,128)(2,1)S(1)} %all_to_all.36, bf16[]{:T(256)} %constant.3.clone.1), dimensions={0}, to_apply=%region_0.0 | reduce | flops 524288 | bytes 3145730 | tf_op jit(solution)/shard_map/reduce_sum | solution.py:291
  87.2 10.4 %all-to-all-start.4 = ((bf16[32,32,512]{2,1,0:T(8,128)(2,1)}), bf16[32,32,512]{2,1,0:T(8,128)(2,1)S(1)}, u32[]{:S(2)}, u32[]{:S(2)}) async-start(bf16[32,32,512]{2,1,0:T(8,128)(2,1)} %bitcast.5), calls=%async_computation.4 | async-start | bytes 2097152 | tf_op jit(solution)/shard_map/all_to_all | solution.py:43
  97.6 0.0 collective-permute-done.4
  97.6 0.0 copy-start.6
  97.6 0.0 collective-permute-done.6
  97.6 0.7 copy-done.6
  98.3 0.0 collective-permute-done.7
  98.3 1.0 constant_dynamic-update-slice_fusion.4
  99.3 1.0 constant_dynamic-update-slice_fusion.3
  100.3 1.0 constant_dynamic-update-slice_fusion.2
  101.3 1.1 constant_dynamic-update-slice_fusion.1
  102.4 1.1 constant_dynamic-update-slice_fusion.own_ref
  103.4 1.9 %collective-permute-start.8 = (bf16[32,64,512]{2,1,0:T(8,128)(2,1)S(1)}, bf16[32,64,512]{2,1,0:T(8,128)(2,1)}, u32[]{:S(2)}, u32[]{:S(2)}) collective-permute-start(bf16[32,64,512]{2,1,0:T(8,128)(2,1)S(1)} %constant_dynamic-update-slice_fusion.own_ref), channel_id=1, source_target_pairs={{0,8},{8,0},{16,24},{24,16},{32,40},{40,32},{48,56},{56,48},{64,72... | collective-permute-start | bytes 6291464 | tf_op jit(solution)/shard_map/ppermute | solution.py:295
  105.4 18.9 %all-to-all-done.4 = bf16[32,32,512]{2,1,0:T(8,128)(2,1)S(1)} async-done(((bf16[32,32,512]{2,1,0:T(8,128)(2,1)}), bf16[32,32,512]{2,1,0:T(8,128)(2,1)S(1)}, u32[]{:S(2)}, u32[]{:S(2)}) %all-to-all-start.4) | async-done | bytes 1048608 | tf_op jit(solution)/shard_map/all_to_all | solution.py:43
  124.3 0.2 convert_reduce_fusion.query_ref
  124.4 0.0 copy-start
  124.4 0.0 collective-permute-done.8.other_ref
  124.4 2.9 %shard_map.123 = bf16[8,32,512]{2,1,0:T(8,128)(2,1)S(1)} custom-call(f32[32,512]{1,0:T(8,128)S(1)} %convert_reduce_fusion.query_ref, bf16[32,64,512]{2,1,0:T(8,128)(2,1)S(1)} %constant_dynamic-update-slice_fusion.own_ref, bf16[32,64,512]{2,1,0:T(8,128)(2,1)} %collective-permute-done.8.other_ref), custom_call_target="tpu_custom_call" | custom-call | tf_op jit(solution)/shard_map/pallas_call | solution.py:258
  127.4 0.0 copy-done
  127.4 17.4 %all_to_all.37 = bf16[8,32,512]{2,1,0:T(8,128)(2,1)S(1)} all-to-all(bf16[8,32,512]{2,1,0:T(8,128)(2,1)S(1)} %shard_map.123), channel_id=1, replica_groups=mesh['psg'=64,'qry'=8] {'qry'}, dimensions={0} | all-to-all | bytes 524288 | tf_op jit(solution)/shard_map/all_to_all | solution.py:43
  144.8 12.9 %all_to_all.38 = bf16[8,32,512]{2,1,0:T(8,128)(2,1)S(1)} all-to-all(bf16[8,32,512]{2,1,0:T(8,128)(2,1)S(1)} %broadcast_in_dim.5), channel_id=1, replica_groups=mesh['psg'=64,'qry'=8] {'qry'}, dimensions={0} | all-to-all | bytes 524288 | tf_op jit(solution)/shard_map/all_to_all | solution.py:43
  157.8 0.8 copy.15
  (4 shorter events, 0.1 us)
Async XLA Ops:
  3.1 29.2 %all-to-all-start = ((bf16[8,32,1152]{2,1,0:T(8,128)(2,1)}), bf16[8,32,1152]{2,1,0:T(8,128)(2,1)S(1)}, u32[]{:S(2)}, u32[]{:S(2)}) async-start(bf16[8,32,1152]{2,1,0:T(8,128)(2,1)} %shard_map.120), calls=%async_computation | async-start | bytes 1179648 | tf_op jit(solution)/shard_map/all_to_all | solution.py:43
  13.4 9.8 %collective-permute-start.2 = (bf16[64,512]{1,0:T(8,128)(2,1)}, bf16[64,512]{1,0:T(8,128)(2,1)S(1)}, u32[]{:S(2)}, u32[]{:S(2)}) collective-permute-start(bf16[64,512]{1,0:T(8,128)(2,1)} %param.15), channel_id=1, source_target_pairs={{0,384},{8,392},{16,400},{24,408},{32,416},{40,424},{48,432},{56,4... | collective-permute-start | bytes 196616 | tf_op jit(solution)/shard_map/ppermute | solution.py:273
  16.1 7.9 %collective-permute-start.1 = (bf16[64,512]{1,0:T(8,128)(2,1)}, bf16[64,512]{1,0:T(8,128)(2,1)S(1)}, u32[]{:S(2)}, u32[]{:S(2)}) collective-permute-start(bf16[64,512]{1,0:T(8,128)(2,1)} %param.15), channel_id=1, source_target_pairs={{0,256},{8,264},{16,272},{24,280},{32,288},{40,296},{48,304},{56,3... | collective-permute-start | bytes 196616 | tf_op jit(solution)/shard_map/ppermute | solution.py:273
  19.2 6.5 %collective-permute-start = (bf16[64,512]{1,0:T(8,128)(2,1)}, bf16[64,512]{1,0:T(8,128)(2,1)S(1)}, u32[]{:S(2)}, u32[]{:S(2)}) collective-permute-start(bf16[64,512]{1,0:T(8,128)(2,1)} %param.15), channel_id=1, source_target_pairs={{0,128},{8,136},{16,144},{24,152},{32,160},{40,168},{48,176},{56,1... | collective-permute-start | bytes 196616 | tf_op jit(solution)/shard_map/ppermute | solution.py:273
  34.0 33.5 %copy-start.3 = (s32[8,16]{1,0:T(8,128)S(1)}, s32[8,16]{1,0:T(8,128)}, u32[]{:S(2)}) copy-start(s32[8,16]{1,0:T(8,128)} %attend_ref.1) | copy-start | bytes 1540
  34.0 33.5 %all-to-all-start.1 = ((bf16[4,8,32,1152]{3,2,1,0:T(8,128)(2,1)}), bf16[4,8,32,1152]{3,2,1,0:T(8,128)(2,1)S(1)}, u32[]{:S(2)}, u32[]{:S(2)}) async-start(bf16[4,8,32,1152]{3,2,1,0:T(8,128)(2,1)} %broadcast_in_dim.4), calls=%async_computation.1 | async-start | bytes 4718592 | tf_op jit(solution)/shard_map/all_to_all | solution.py:43
  38.9 14.1 %collective-permute-start.3 = (bf16[4,64,512]{2,1,0:T(8,128)(2,1)S(1)}, bf16[4,64,512]{2,1,0:T(8,128)(2,1)S(1)}, u32[]{:S(2)}, u32[]{:S(2)}) collective-permute-start(bf16[4,64,512]{2,1,0:T(8,128)(2,1)S(1)} %pad_maximum_fusion.2), channel_id=1, source_target_pairs={{0,96},{8,104},{16,112},{24,120},{32,0},{40,8},{48,16},{56,24},{64... | collective-permute-start | bytes 786440 | tf_op jit(solution)/shard_map/ppermute | solution.py:276
  41.2 15.9 %collective-permute-start.5 = (bf16[4,64,512]{2,1,0:T(8,128)(2,1)S(1)}, bf16[4,64,512]{2,1,0:T(8,128)(2,1)S(1)}, u32[]{:S(2)}, u32[]{:S(2)}) collective-permute-start(bf16[4,64,512]{2,1,0:T(8,128)(2,1)S(1)} %pad_maximum_fusion.2), channel_id=1, source_target_pairs={{0,32},{8,40},{16,48},{24,56},{32,64},{40,72},{48,80},{56,88},{64,... | collective-permute-start | bytes 786440 | tf_op jit(solution)/shard_map/ppermute | solution.py:277
  53.0 10.9 %copy-start.5 = (bf16[4,64,512]{2,1,0:T(8,128)(2,1)}, bf16[4,64,512]{2,1,0:T(8,128)(2,1)S(1)}, u32[]{:S(2)}) copy-start(bf16[4,64,512]{2,1,0:T(8,128)(2,1)S(1)} %collective-permute-done.3) | copy-start | bytes 786436
  57.1 6.8 %copy-start.4 = (bf16[4,64,512]{2,1,0:T(8,128)(2,1)}, bf16[4,64,512]{2,1,0:T(8,128)(2,1)S(1)}, u32[]{:S(2)}) copy-start(bf16[4,64,512]{2,1,0:T(8,128)(2,1)S(1)} %collective-permute-done.5) | copy-start | bytes 786436
  58.0 39.6 %collective-permute-start.6 = (bf16[8,64,512]{2,1,0:T(8,128)(2,1)}, bf16[8,64,512]{2,1,0:T(8,128)(2,1)}, u32[]{:S(2)}, u32[]{:S(2)}) collective-permute-start(bf16[8,64,512]{2,1,0:T(8,128)(2,1)} %get-tuple-element.35), channel_id=1, source_target_pairs={{0,112},{8,120},{16,0},{24,8},{32,16},{40,24},{48,32},{56,40},{64,... | collective-permute-start | bytes 1572872 | tf_op jit(solution)/shard_map/ppermute | solution.py:279
  59.9 38.4 %collective-permute-start.7 = (bf16[8,64,512]{2,1,0:T(8,128)(2,1)S(1)}, bf16[8,64,512]{2,1,0:T(8,128)(2,1)}, u32[]{:S(2)}, u32[]{:S(2)}) collective-permute-start(bf16[8,64,512]{2,1,0:T(8,128)(2,1)S(1)} %get-tuple-element.34), channel_id=1, source_target_pairs={{0,16},{8,24},{16,32},{24,40},{32,48},{40,56},{48,64},{56,72},{64,... | collective-permute-start | bytes 1572872 | tf_op jit(solution)/shard_map/ppermute | solution.py:280
  63.9 33.7 %collective-permute-start.4 = (bf16[4,64,512]{2,1,0:T(8,128)(2,1)S(1)}, bf16[4,64,512]{2,1,0:T(8,128)(2,1)S(1)}, u32[]{:S(2)}, u32[]{:S(2)}) collective-permute-start(bf16[4,64,512]{2,1,0:T(8,128)(2,1)S(1)} %pad_maximum_fusion.2), channel_id=1, source_target_pairs={{0,64},{8,72},{16,80},{24,88},{32,96},{40,104},{48,112},{56,120},{... | collective-permute-start | bytes 786440 | tf_op jit(solution)/shard_map/ppermute | solution.py:278
  69.0 5.8 %copy-start.1 = (bf16[512,128]{1,0:T(8,128)(2,1)S(1)}, bf16[512,128]{1,0:T(8,128)(2,1)}, u32[]{:S(2)}) copy-start(bf16[512,128]{1,0:T(8,128)(2,1)} %key_ref.1) | copy-start | bytes 393220
  69.0 5.8 %copy-start.2 = (bf16[512,128]{1,0:T(8,128)(2,1)S(1)}, bf16[512,128]{1,0:T(8,128)(2,1)}, u32[]{:S(2)}) copy-start(bf16[512,128]{1,0:T(8,128)(2,1)} %value_ref.1) | copy-start | bytes 393220
  87.2 37.1 %all-to-all-start.4 = ((bf16[32,32,512]{2,1,0:T(8,128)(2,1)}), bf16[32,32,512]{2,1,0:T(8,128)(2,1)S(1)}, u32[]{:S(2)}, u32[]{:S(2)}) async-start(bf16[32,32,512]{2,1,0:T(8,128)(2,1)} %bitcast.5), calls=%async_computation.4 | async-start | bytes 2097152 | tf_op jit(solution)/shard_map/all_to_all | solution.py:43
  97.6 0.7 copy-start.6
  103.4 21.0 %collective-permute-start.8 = (bf16[32,64,512]{2,1,0:T(8,128)(2,1)S(1)}, bf16[32,64,512]{2,1,0:T(8,128)(2,1)}, u32[]{:S(2)}, u32[]{:S(2)}) collective-permute-start(bf16[32,64,512]{2,1,0:T(8,128)(2,1)S(1)} %constant_dynamic-update-slice_fusion.own_ref), channel_id=1, source_target_pairs={{0,8},{8,0},{16,24},{24,16},{32,40},{40,32},{48,56},{56,48},{64,72... | collective-permute-start | bytes 6291464 | tf_op jit(solution)/shard_map/ppermute | solution.py:295
  124.4 2.9 %copy-start = (f32[32,512]{1,0:T(8,128)}, f32[32,512]{1,0:T(8,128)S(1)}, u32[]{:S(2)}) copy-start(f32[32,512]{1,0:T(8,128)S(1)} %convert_reduce_fusion.query_ref) | copy-start | bytes 196612

commit v7 on v6

--- a/solution.py
+++ b/solution.py
@@ -151,6 +151,12 @@
     out_v[...] = jnp.zeros_like(out_v)
     key_t = key_ref[...].astype(jnp.float32).T.astype(jnp.bfloat16)
     columns = lax.broadcasted_iota(jnp.int32, (span, WIDTH), 1)
+    minus = []
+    for head in range(heads):
+        of_head = columns % heads == head
+        for_shift = (columns < 3 * heads) & of_head
+        for_delta = (columns >= 3 * heads) & (columns < 6 * heads) & of_head
+        minus.append([jnp.where(here, -1.0, 0.0).astype(jnp.bfloat16) for here in (for_shift, for_delta)])
 
     @pl.loop(0, questions)
     def _(question):
@@ -173,10 +179,7 @@
             for head in range(heads):
                 query = take(head * WIDTH)
                 cotangent = take((heads + head) * WIDTH)
-                for_shift = (columns < 3 * heads) & (columns % heads == head)
-                for_delta = (columns >= 3 * heads) & (columns < 6 * heads) & (columns % heads == head)
-                minus_s = jnp.where(for_shift, -1.0, 0.0).astype(jnp.bfloat16)
-                minus_d = jnp.where(for_delta, -1.0, 0.0).astype(jnp.bfloat16)
+                minus_s, minus_d = minus[head]
                 energy = lax.dot_general(
                     jnp.concatenate([key, minus_s], axis=1),
                     jnp.concatenate([query, side], axis=1),

time: 161 us -> 162 us (level)
  no operation moved by 1% of the time
where the time goes in v7:
time: 162 us; the launch traced here: 159 us
  starting transfers between devices  54.2 us (33%)
  blocking collectives  41.4 us (26%)
  waiting for transfers between devices  38.6 us (24%)
  Pallas kernels  12.1 us (7%)
  local copies, waits for them, and re-layouts  8.3 us (5%)
  other arithmetic  3.71 us (2%)
    all_to_all x4, blocking collectives, spread(): lax.all_to_all(blocks, axis, 0, 0, tiled=True, axis_index_groups=groups)  41.4 us
    all_to_all x3, starting transfers between devices, spread(): lax.all_to_all(blocks, axis, 0, 0, tiled=True, axis_index_groups=groups)  26.4 us
    all_to_all x3, waiting for transfers between devices, spread(): lax.all_to_all(blocks, axis, 0, 0, tiled=True, axis_index_groups=groups)  24.6 us
    ppermute x3, starting transfers between devices, on_device(): lax.ppermute(proj_weight, 'psg', steps)  9.76 us
    ppermute x1, waiting for transfers between devices, on_device(): plus = lax.ppermute(near, 'psg', z_step(-2))  7.4 us
    pallas_call x1, Pallas kernels, visits(): pl.pallas_call(functools.partial(visit_kernel, heads), in_specs=[pl.Block...  5.21 us
    unnamed x19, local copies, waits for them, and re-layouts  4.71 us
    ppermute x1, starting transfers between devices, on_device(): minus = lax.ppermute(near, 'psg', z_step(2))  4.43 us
  transfers between devices with their start and end apart: 12, of which 6 were waited for; matrix products, arithmetic and copies ran while one was open for 5% of the time, Pallas kernels for 4%

profile of v7, /device:TPU:6, one launch (start us, length us, event | category | flops | bytes accessed | tf_op | source)
XLA Modules:
  0.0 159.3 jit_solution(17886173139176163361)
XLA Ops:
  0.6 2.4 %shard_map.120 = bf16[8,32,1152]{2,1,0:T(8,128)(2,1)} custom-call(s32[8]{0:T(128)} %qlen_ref.1, bf16[32,512]{1,0:T(8,128)(2,1)} %query_in.1, bf16[32,512]{1,0:T(8,128)(2,1)} %grad_in.1, bf16[32,512]{1,0:T(8,128)(2,1)} %output_in.1, f32[4,32]{1,0:T(4,128)} %lse_in.1), custom_call_target="tpu_custom_call" | custom-call | tf_op jit(solution)/shard_map/pallas_call | solution.py:92
  3.1 10.3 %all-to-all-start = ((bf16[8,32,1152]{2,1,0:T(8,128)(2,1)}), bf16[8,32,1152]{2,1,0:T(8,128)(2,1)S(1)}, u32[]{:S(2)}, u32[]{:S(2)}) async-start(bf16[8,32,1152]{2,1,0:T(8,128)(2,1)} %shard_map.120), calls=%async_computation | async-start | bytes 1179648 | tf_op jit(solution)/shard_map/all_to_all | solution.py:43
  13.4 2.7 %collective-permute-start.2 = (bf16[64,512]{1,0:T(8,128)(2,1)}, bf16[64,512]{1,0:T(8,128)(2,1)S(1)}, u32[]{:S(2)}, u32[]{:S(2)}) collective-permute-start(bf16[64,512]{1,0:T(8,128)(2,1)} %param.15), channel_id=1, source_target_pairs={{0,384},{8,392},{16,400},{24,408},{32,416},{40,424},{48,432},{56,4... | collective-permute-start | bytes 196616 | tf_op jit(solution)/shard_map/ppermute | solution.py:276
  16.1 3.0 %collective-permute-start.1 = (bf16[64,512]{1,0:T(8,128)(2,1)}, bf16[64,512]{1,0:T(8,128)(2,1)S(1)}, u32[]{:S(2)}, u32[]{:S(2)}) collective-permute-start(bf16[64,512]{1,0:T(8,128)(2,1)} %param.15), channel_id=1, source_target_pairs={{0,256},{8,264},{16,272},{24,280},{32,288},{40,296},{48,304},{56,3... | collective-permute-start | bytes 196616 | tf_op jit(solution)/shard_map/ppermute | solution.py:276
  19.2 4.0 %collective-permute-start = (bf16[64,512]{1,0:T(8,128)(2,1)}, bf16[64,512]{1,0:T(8,128)(2,1)S(1)}, u32[]{:S(2)}, u32[]{:S(2)}) collective-permute-start(bf16[64,512]{1,0:T(8,128)(2,1)} %param.15), channel_id=1, source_target_pairs={{0,128},{8,136},{16,144},{24,152},{32,160},{40,168},{48,176},{56,1... | collective-permute-start | bytes 196616 | tf_op jit(solution)/shard_map/ppermute | solution.py:276
  23.2 0.0 collective-permute-done.2
  23.2 0.8 collective-permute-done.1
  24.0 1.7 %collective-permute-done = bf16[64,512]{1,0:T(8,128)(2,1)S(1)} collective-permute-done((bf16[64,512]{1,0:T(8,128)(2,1)}, bf16[64,512]{1,0:T(8,128)(2,1)S(1)}, u32[]{:S(2)}, u32[]{:S(2)}) %collective-permute-start) | collective-permute-done | bytes 65568 | tf_op jit(solution)/shard_map/ppermute | solution.py:276
  25.7 0.9 pad_maximum_fusion.2
  26.6 5.7 %all-to-all-done = bf16[8,32,1152]{2,1,0:T(8,128)(2,1)S(1)} async-done(((bf16[8,32,1152]{2,1,0:T(8,128)(2,1)}), bf16[8,32,1152]{2,1,0:T(8,128)(2,1)S(1)}, u32[]{:S(2)}, u32[]{:S(2)}) %all-to-all-start) | async-done | bytes 589856 | tf_op jit(solution)/shard_map/all_to_all | solution.py:43
  32.3 1.6 %broadcast_in_dim.4 = bf16[4,8,32,1152]{3,2,1,0:T(8,128)(2,1)} broadcast(bf16[8,32,1152]{2,1,0:T(8,128)(2,1)S(1)} %all-to-all-done), dimensions={1,2,3} | broadcast | bytes 2949120 | tf_op jit(solution)/shard_map/broadcast_in_dim | solution.py:278
  34.0 0.0 copy-start.3
  34.0 4.9 %all-to-all-start.1 = ((bf16[4,8,32,1152]{3,2,1,0:T(8,128)(2,1)}), bf16[4,8,32,1152]{3,2,1,0:T(8,128)(2,1)S(1)}, u32[]{:S(2)}, u32[]{:S(2)}) async-start(bf16[4,8,32,1152]{3,2,1,0:T(8,128)(2,1)} %broadcast_in_dim.4), calls=%async_computation.1 | async-start | bytes 4718592 | tf_op jit(solution)/shard_map/all_to_all | solution.py:43
  38.9 2.3 %collective-permute-start.3 = (bf16[4,64,512]{2,1,0:T(8,128)(2,1)S(1)}, bf16[4,64,512]{2,1,0:T(8,128)(2,1)S(1)}, u32[]{:S(2)}, u32[]{:S(2)}) collective-permute-start(bf16[4,64,512]{2,1,0:T(8,128)(2,1)S(1)} %pad_maximum_fusion.2), channel_id=1, source_target_pairs={{0,96},{8,104},{16,112},{24,120},{32,0},{40,8},{48,16},{56,24},{64... | collective-permute-start | bytes 786440 | tf_op jit(solution)/shard_map/ppermute | solution.py:279
  41.2 4.4 %collective-permute-start.5 = (bf16[4,64,512]{2,1,0:T(8,128)(2,1)S(1)}, bf16[4,64,512]{2,1,0:T(8,128)(2,1)S(1)}, u32[]{:S(2)}, u32[]{:S(2)}) collective-permute-start(bf16[4,64,512]{2,1,0:T(8,128)(2,1)S(1)} %pad_maximum_fusion.2), channel_id=1, source_target_pairs={{0,32},{8,40},{16,48},{24,56},{32,64},{40,72},{48,80},{56,88},{64,... | collective-permute-start | bytes 786440 | tf_op jit(solution)/shard_map/ppermute | solution.py:280
  45.6 7.4 %collective-permute-done.3 = bf16[4,64,512]{2,1,0:T(8,128)(2,1)S(1)} collective-permute-done((bf16[4,64,512]{2,1,0:T(8,128)(2,1)S(1)}, bf16[4,64,512]{2,1,0:T(8,128)(2,1)S(1)}, u32[]{:S(2)}, u32[]{:S(2)}) %collective-permute-start.3) | collective-permute-done | bytes 262176 | tf_op jit(solution)/shard_map/ppermute | solution.py:279
  53.0 0.0 copy-start.5
  53.0 4.1 %collective-permute-done.5 = bf16[4,64,512]{2,1,0:T(8,128)(2,1)S(1)} collective-permute-done((bf16[4,64,512]{2,1,0:T(8,128)(2,1)S(1)}, bf16[4,64,512]{2,1,0:T(8,128)(2,1)S(1)}, u32[]{:S(2)}, u32[]{:S(2)}) %collective-permute-start.5) | collective-permute-done | bytes 262176 | tf_op jit(solution)/shard_map/ppermute | solution.py:280
  57.1 0.0 copy-start.4
  57.1 0.9 pad_maximum_fusion.1
  58.0 1.9 %collective-permute-start.6 = (bf16[8,64,512]{2,1,0:T(8,128)(2,1)}, bf16[8,64,512]{2,1,0:T(8,128)(2,1)}, u32[]{:S(2)}, u32[]{:S(2)}) collective-permute-start(bf16[8,64,512]{2,1,0:T(8,128)(2,1)} %get-tuple-element.35), channel_id=1, source_target_pairs={{0,112},{8,120},{16,0},{24,8},{32,16},{40,24},{48,32},{56,40},{64,... | collective-permute-start | bytes 1572872 | tf_op jit(solution)/shard_map/ppermute | solution.py:282
  59.9 3.9 %collective-permute-start.7 = (bf16[8,64,512]{2,1,0:T(8,128)(2,1)S(1)}, bf16[8,64,512]{2,1,0:T(8,128)(2,1)}, u32[]{:S(2)}, u32[]{:S(2)}) collective-permute-start(bf16[8,64,512]{2,1,0:T(8,128)(2,1)S(1)} %get-tuple-element.34), channel_id=1, source_target_pairs={{0,16},{8,24},{16,32},{24,40},{32,48},{40,56},{48,64},{56,72},{64,... | collective-permute-start | bytes 1572872 | tf_op jit(solution)/shard_map/ppermute | solution.py:283
  63.8 0.0 copy-done.5
  63.9 0.0 copy-done.4
  63.9 3.6 %collective-permute-start.4 = (bf16[4,64,512]{2,1,0:T(8,128)(2,1)S(1)}, bf16[4,64,512]{2,1,0:T(8,128)(2,1)S(1)}, u32[]{:S(2)}, u32[]{:S(2)}) collective-permute-start(bf16[4,64,512]{2,1,0:T(8,128)(2,1)S(1)} %pad_maximum_fusion.2), channel_id=1, source_target_pairs={{0,64},{8,72},{16,80},{24,88},{32,96},{40,104},{48,112},{56,120},{... | collective-permute-start | bytes 786440 | tf_op jit(solution)/shard_map/ppermute | solution.py:281
  67.4 0.0 all-to-all-done.1
  67.4 0.0 copy-done.3
  67.5 1.6 shard_map.121
  69.0 0.0 copy-start.1
  69.0 0.0 copy-start.2
  69.1 5.8 %all_to_all.35.rows_ref = bf16[2,4,4,32,1152]{4,3,2,1,0:T(8,128)(2,1)S(1)} all-to-all(bf16[2,4,4,32,1152]{4,3,2,1,0:T(8,128)(2,1)S(1)} %get-tuple-element.23), channel_id=1, replica_groups={{0,8},{16,24},{32,40},{48,56},{64,72},{80,88},{96,104},{112,120},{128,1..., dimensions={0} | all-to-all | bytes 4718592 | tf_op jit(solution)/shard_map/all_to_all | solution.py:43
  74.8 0.0 copy-done.1
  74.8 0.0 copy-done.2
  74.8 5.2 %shard_map.122 = (bf16[2,8,4,32,512]{4,3,2,1,0:T(8,128)(2,1)S(1)}, f32[512,128]{1,0:T(8,128)}, f32[512,128]{1,0:T(8,128)}) custom-call(s32[2,8]{1,0:T(2,128)S(1)} %get-tuple-element.22.plan, bf16[2,4,4,32,1152]{4,3,2,1,0:T(8,128)(2,1)S(1)} %all_to_all.35.rows_ref, bf16[512,128]{1,0:T(8,128)(2,1)S(1)} %copy-done.1, bf16[512,128]{1,0:T(8,128)(2,1)S(1)} %copy-done.2), custom_call_target="tpu_custom_call" | custom-call | tf_op jit(solution)/shard_map/pallas_call | solution.py:210
  80.0 5.4 %all_to_all.36 = bf16[2,8,4,32,512]{4,3,2,1,0:T(8,128)(2,1)S(1)} all-to-all(bf16[2,8,4,32,512]{4,3,2,1,0:T(8,128)(2,1)S(1)} %get-tuple-element.24), channel_id=1, replica_groups={{0,8},{16,24},{32,40},{48,56},{64,72},{80,88},{96,104},{112,120},{128,1..., dimensions={0} | all-to-all | bytes 4194304 | tf_op jit(solution)/shard_map/all_to_all | solution.py:43
  85.4 1.7 %reduce_sum.33 = bf16[8,4,32,512]{3,2,1,0:T(8,128)(2,1)} reduce(bf16[2,8,4,32,512]{4,3,2,1,0:T(8,128)(2,1)S(1)} %all_to_all.36, bf16[]{:T(256)} %constant.3.clone.1), dimensions={0}, to_apply=%region_0.0 | reduce | flops 524288 | bytes 3145730 | tf_op jit(solution)/shard_map/reduce_sum | solution.py:294
  87.1 11.1 %all-to-all-start.4 = ((bf16[32,32,512]{2,1,0:T(8,128)(2,1)}), bf16[32,32,512]{2,1,0:T(8,128)(2,1)S(1)}, u32[]{:S(2)}, u32[]{:S(2)}) async-start(bf16[32,32,512]{2,1,0:T(8,128)(2,1)} %bitcast.5), calls=%async_computation.4 | async-start | bytes 2097152 | tf_op jit(solution)/shard_map/all_to_all | solution.py:43
  98.3 0.0 collective-permute-done.4
  98.3 0.0 copy-start.6
  98.3 0.0 collective-permute-done.6
  98.3 0.7 copy-done.6
  99.0 0.0 collective-permute-done.7
  99.0 1.0 constant_dynamic-update-slice_fusion.4
  100.0 1.0 constant_dynamic-update-slice_fusion.3
  101.0 1.0 constant_dynamic-update-slice_fusion.2
  101.9 1.1 constant_dynamic-update-slice_fusion.1
  103.0 1.1 constant_dynamic-update-slice_fusion.own_ref
  104.1 1.9 %collective-permute-start.8 = (bf16[32,64,512]{2,1,0:T(8,128)(2,1)S(1)}, bf16[32,64,512]{2,1,0:T(8,128)(2,1)}, u32[]{:S(2)}, u32[]{:S(2)}) collective-permute-start(bf16[32,64,512]{2,1,0:T(8,128)(2,1)S(1)} %constant_dynamic-update-slice_fusion.own_ref), channel_id=1, source_target_pairs={{0,8},{8,0},{16,24},{24,16},{32,40},{40,32},{48,56},{56,48},{64,72... | collective-permute-start | bytes 6291464 | tf_op jit(solution)/shard_map/ppermute | solution.py:298
  106.1 18.9 %all-to-all-done.4 = bf16[32,32,512]{2,1,0:T(8,128)(2,1)S(1)} async-done(((bf16[32,32,512]{2,1,0:T(8,128)(2,1)}), bf16[32,32,512]{2,1,0:T(8,128)(2,1)S(1)}, u32[]{:S(2)}, u32[]{:S(2)}) %all-to-all-start.4) | async-done | bytes 1048608 | tf_op jit(solution)/shard_map/all_to_all | solution.py:43
  125.0 0.2 convert_reduce_fusion.query_ref
  125.1 0.0 copy-start
  125.1 0.0 collective-permute-done.8.other_ref
  125.1 2.9 %shard_map.123 = bf16[8,32,512]{2,1,0:T(8,128)(2,1)S(1)} custom-call(f32[32,512]{1,0:T(8,128)S(1)} %convert_reduce_fusion.query_ref, bf16[32,64,512]{2,1,0:T(8,128)(2,1)S(1)} %constant_dynamic-update-slice_fusion.own_ref, bf16[32,64,512]{2,1,0:T(8,128)(2,1)} %collective-permute-done.8.other_ref), custom_call_target="tpu_custom_call" | custom-call | tf_op jit(solution)/shard_map/pallas_call | solution.py:261
  128.0 0.0 copy-done
  128.0 17.4 %all_to_all.37 = bf16[8,32,512]{2,1,0:T(8,128)(2,1)S(1)} all-to-all(bf16[8,32,512]{2,1,0:T(8,128)(2,1)S(1)} %shard_map.123), channel_id=1, replica_groups=mesh['psg'=64,'qry'=8] {'qry'}, dimensions={0} | all-to-all | bytes 524288 | tf_op jit(solution)/shard_map/all_to_all | solution.py:43
  145.5 12.9 %all_to_all.38 = bf16[8,32,512]{2,1,0:T(8,128)(2,1)S(1)} all-to-all(bf16[8,32,512]{2,1,0:T(8,128)(2,1)S(1)} %broadcast_in_dim.5), channel_id=1, replica_groups=mesh['psg'=64,'qry'=8] {'qry'}, dimensions={0} | all-to-all | bytes 524288 | tf_op jit(solution)/shard_map/all_to_all | solution.py:43
  158.4 0.8 copy.15
  (4 shorter events, 0.1 us)
Async XLA Ops:
  3.1 29.2 %all-to-all-start = ((bf16[8,32,1152]{2,1,0:T(8,128)(2,1)}), bf16[8,32,1152]{2,1,0:T(8,128)(2,1)S(1)}, u32[]{:S(2)}, u32[]{:S(2)}) async-start(bf16[8,32,1152]{2,1,0:T(8,128)(2,1)} %shard_map.120), calls=%async_computation | async-start | bytes 1179648 | tf_op jit(solution)/shard_map/all_to_all | solution.py:43
  13.4 9.8 %collective-permute-start.2 = (bf16[64,512]{1,0:T(8,128)(2,1)}, bf16[64,512]{1,0:T(8,128)(2,1)S(1)}, u32[]{:S(2)}, u32[]{:S(2)}) collective-permute-start(bf16[64,512]{1,0:T(8,128)(2,1)} %param.15), channel_id=1, source_target_pairs={{0,384},{8,392},{16,400},{24,408},{32,416},{40,424},{48,432},{56,4... | collective-permute-start | bytes 196616 | tf_op jit(solution)/shard_map/ppermute | solution.py:276
  16.1 7.9 %collective-permute-start.1 = (bf16[64,512]{1,0:T(8,128)(2,1)}, bf16[64,512]{1,0:T(8,128)(2,1)S(1)}, u32[]{:S(2)}, u32[]{:S(2)}) collective-permute-start(bf16[64,512]{1,0:T(8,128)(2,1)} %param.15), channel_id=1, source_target_pairs={{0,256},{8,264},{16,272},{24,280},{32,288},{40,296},{48,304},{56,3... | collective-permute-start | bytes 196616 | tf_op jit(solution)/shard_map/ppermute | solution.py:276
  19.2 6.5 %collective-permute-start = (bf16[64,512]{1,0:T(8,128)(2,1)}, bf16[64,512]{1,0:T(8,128)(2,1)S(1)}, u32[]{:S(2)}, u32[]{:S(2)}) collective-permute-start(bf16[64,512]{1,0:T(8,128)(2,1)} %param.15), channel_id=1, source_target_pairs={{0,128},{8,136},{16,144},{24,152},{32,160},{40,168},{48,176},{56,1... | collective-permute-start | bytes 196616 | tf_op jit(solution)/shard_map/ppermute | solution.py:276
  34.0 33.5 %copy-start.3 = (s32[8,16]{1,0:T(8,128)S(1)}, s32[8,16]{1,0:T(8,128)}, u32[]{:S(2)}) copy-start(s32[8,16]{1,0:T(8,128)} %attend_ref.1) | copy-start | bytes 1540
  34.0 33.5 %all-to-all-start.1 = ((bf16[4,8,32,1152]{3,2,1,0:T(8,128)(2,1)}), bf16[4,8,32,1152]{3,2,1,0:T(8,128)(2,1)S(1)}, u32[]{:S(2)}, u32[]{:S(2)}) async-start(bf16[4,8,32,1152]{3,2,1,0:T(8,128)(2,1)} %broadcast_in_dim.4), calls=%async_computation.1 | async-start | bytes 4718592 | tf_op jit(solution)/shard_map/all_to_all | solution.py:43
  38.9 14.1 %collective-permute-start.3 = (bf16[4,64,512]{2,1,0:T(8,128)(2,1)S(1)}, bf16[4,64,512]{2,1,0:T(8,128)(2,1)S(1)}, u32[]{:S(2)}, u32[]{:S(2)}) collective-permute-start(bf16[4,64,512]{2,1,0:T(8,128)(2,1)S(1)} %pad_maximum_fusion.2), channel_id=1, source_target_pairs={{0,96},{8,104},{16,112},{24,120},{32,0},{40,8},{48,16},{56,24},{64... | collective-permute-start | bytes 786440 | tf_op jit(solution)/shard_map/ppermute | solution.py:279
  41.2 15.9 %collective-permute-start.5 = (bf16[4,64,512]{2,1,0:T(8,128)(2,1)S(1)}, bf16[4,64,512]{2,1,0:T(8,128)(2,1)S(1)}, u32[]{:S(2)}, u32[]{:S(2)}) collective-permute-start(bf16[4,64,512]{2,1,0:T(8,128)(2,1)S(1)} %pad_maximum_fusion.2), channel_id=1, source_target_pairs={{0,32},{8,40},{16,48},{24,56},{32,64},{40,72},{48,80},{56,88},{64,... | collective-permute-start | bytes 786440 | tf_op jit(solution)/shard_map/ppermute | solution.py:280
  53.0 10.9 %copy-start.5 = (bf16[4,64,512]{2,1,0:T(8,128)(2,1)}, bf16[4,64,512]{2,1,0:T(8,128)(2,1)S(1)}, u32[]{:S(2)}) copy-start(bf16[4,64,512]{2,1,0:T(8,128)(2,1)S(1)} %collective-permute-done.3) | copy-start | bytes 786436
  57.1 6.8 %copy-start.4 = (bf16[4,64,512]{2,1,0:T(8,128)(2,1)}, bf16[4,64,512]{2,1,0:T(8,128)(2,1)S(1)}, u32[]{:S(2)}) copy-start(bf16[4,64,512]{2,1,0:T(8,128)(2,1)S(1)} %collective-permute-done.5) | copy-start | bytes 786436
  58.0 40.3 %collective-permute-start.6 = (bf16[8,64,512]{2,1,0:T(8,128)(2,1)}, bf16[8,64,512]{2,1,0:T(8,128)(2,1)}, u32[]{:S(2)}, u32[]{:S(2)}) collective-permute-start(bf16[8,64,512]{2,1,0:T(8,128)(2,1)} %get-tuple-element.35), channel_id=1, source_target_pairs={{0,112},{8,120},{16,0},{24,8},{32,16},{40,24},{48,32},{56,40},{64,... | collective-permute-start | bytes 1572872 | tf_op jit(solution)/shard_map/ppermute | solution.py:282
  59.9 39.1 %collective-permute-start.7 = (bf16[8,64,512]{2,1,0:T(8,128)(2,1)S(1)}, bf16[8,64,512]{2,1,0:T(8,128)(2,1)}, u32[]{:S(2)}, u32[]{:S(2)}) collective-permute-start(bf16[8,64,512]{2,1,0:T(8,128)(2,1)S(1)} %get-tuple-element.34), channel_id=1, source_target_pairs={{0,16},{8,24},{16,32},{24,40},{32,48},{40,56},{48,64},{56,72},{64,... | collective-permute-start | bytes 1572872 | tf_op jit(solution)/shard_map/ppermute | solution.py:283
  63.9 34.4 %collective-permute-start.4 = (bf16[4,64,512]{2,1,0:T(8,128)(2,1)S(1)}, bf16[4,64,512]{2,1,0:T(8,128)(2,1)S(1)}, u32[]{:S(2)}, u32[]{:S(2)}) collective-permute-start(bf16[4,64,512]{2,1,0:T(8,128)(2,1)S(1)} %pad_maximum_fusion.2), channel_id=1, source_target_pairs={{0,64},{8,72},{16,80},{24,88},{32,96},{40,104},{48,112},{56,120},{... | collective-permute-start | bytes 786440 | tf_op jit(solution)/shard_map/ppermute | solution.py:281
  69.0 5.8 %copy-start.1 = (bf16[512,128]{1,0:T(8,128)(2,1)S(1)}, bf16[512,128]{1,0:T(8,128)(2,1)}, u32[]{:S(2)}) copy-start(bf16[512,128]{1,0:T(8,128)(2,1)} %key_ref.1) | copy-start | bytes 393220
  69.0 5.8 %copy-start.2 = (bf16[512,128]{1,0:T(8,128)(2,1)S(1)}, bf16[512,128]{1,0:T(8,128)(2,1)}, u32[]{:S(2)}) copy-start(bf16[512,128]{1,0:T(8,128)(2,1)} %value_ref.1) | copy-start | bytes 393220
  87.1 37.8 %all-to-all-start.4 = ((bf16[32,32,512]{2,1,0:T(8,128)(2,1)}), bf16[32,32,512]{2,1,0:T(8,128)(2,1)S(1)}, u32[]{:S(2)}, u32[]{:S(2)}) async-start(bf16[32,32,512]{2,1,0:T(8,128)(2,1)} %bitcast.5), calls=%async_computation.4 | async-start | bytes 2097152 | tf_op jit(solution)/shard_map/all_to_all | solution.py:43
  98.3 0.7 copy-start.6
  104.1 21.0 %collective-permute-start.8 = (bf16[32,64,512]{2,1,0:T(8,128)(2,1)S(1)}, bf16[32,64,512]{2,1,0:T(8,128)(2,1)}, u32[]{:S(2)}, u32[]{:S(2)}) collective-permute-start(bf16[32,64,512]{2,1,0:T(8,128)(2,1)S(1)} %constant_dynamic-update-slice_fusion.own_ref), channel_id=1, source_target_pairs={{0,8},{8,0},{16,24},{24,16},{32,40},{40,32},{48,56},{56,48},{64,72... | collective-permute-start | bytes 6291464 | tf_op jit(solution)/shard_map/ppermute | solution.py:298
  125.1 2.9 %copy-start = (f32[32,512]{1,0:T(8,128)}, f32[32,512]{1,0:T(8,128)S(1)}, u32[]{:S(2)}) copy-start(f32[32,512]{1,0:T(8,128)S(1)} %convert_reduce_fusion.query_ref) | copy-start | bytes 196612
